TPU v7x, 32 devices: a whole 2x2x4 slice. The times are simulated.
32 devices in a mesh: groups: 2 (over y), tensor: 16 (over z, x, core).
Axes of the slice: x: 2, y: 2, z: 4, core: 2. Of those that a mesh axis runs over, the one named last changes fastest.
Arguments:
- normed_input: bfloat16 [16, 2, 8192], P('groups', None, 'tensor'), parts along dimension 0, may hold values from -6 to 6
- query_weight: bfloat16 [8192, 8192], P('tensor'), may hold values from -0.0625 to 0.0625
- query_gain: float32 [128], replicated, may hold values from 0.5 to 50
- image_cache: bfloat16 [32, 1601, 2048], P(('groups', 'tensor')), parts along dimension 0, may hold values from -18 to 18
- tile_count: int32 [16], P('groups'), parts along dimension 0, may hold values from 1 to 4, as said below
- image_first_slot: int32 [16], P('groups'), parts along dimension 0, may hold values from 0 to 15, as said below
- cross_tile_mask: int32 [16, 2, 4], P('groups'), parts along dimension 0, may hold values 0 or 1
- output_weight: bfloat16 [8192, 8192], P(None, 'tensor'), may hold values from -0.0625 to 0.0625
- output_gate: float32 [1], replicated, may hold values from 0.3 to 1.5
Outputs:
- cross_output: bfloat16 [16, 2, 8192], P('groups', None, 'tensor'), parts along dimension 0
There are 2 independent parts, one for each index of `groups`. A program takes and returns all parts, laid end to end along the dimension named above; an argument that names none is the same for every part. Nothing has to cross between parts.
Inputs may be any that keep to these rules, and one draw needn't show every extreme that they name: tile_count sums to 16; some row has 4 tiles. Row r's tiles are pool slots image_first_slot[r] to image_first_slot[r] + tile_count[r] - 1; the images fill all 16 slots, each slot belonging to exactly one row.
All inputs are finite; a program needn't handle non-finite values.
Results may differ from a plain program's by a relative error of at most 0.0077.
Values may be sent and summed in bfloat16 or wider, within the bound.
No kernel may reach another device: no remote copies, remote signals or barrier semaphores. Data moves between devices by JAX's collectives and lax.ppermute only.
A program may use at most 64 MiB of HBM per device.

v0:
```python
import math

import jax
import jax.numpy as jnp
from jax import lax
from jax.sharding import PartitionSpec as P

EPSILON = 1e-05
NEGATIVE_FLOOR = -1e30


def membership(image_first_slot, tile_count, pool_slots):
    ends = image_first_slot + tile_count
    return (pool_slots[:, None] >= image_first_slot[None, :]) & (
        pool_slots[:, None] < ends[None, :]
    )


def active_status(member_flag, image_first_slot, cross_tile_mask, pool_slots):
    member_int = member_flag.astype(jnp.int32)
    tile_index = jnp.sum(member_int * (pool_slots[:, None] - image_first_slot[None, :]), axis=1)
    row_masks = jnp.sum(member_int[:, :, None, None] * cross_tile_mask[None], axis=1)
    positions = jnp.arange(cross_tile_mask.shape[2], dtype=jnp.int32)
    chosen = jnp.sum(
        jnp.where(positions[None, None, :] == tile_index[:, None, None], row_masks, 0), axis=2
    )
    return (tile_index[:, None] == 0) | (chosen == 1)


def tile_partial(query_rows, cache_tile, head_size):
    steps = query_rows.shape[0]
    kv_width = cache_tile.shape[1] // 2
    kv_heads = kv_width // head_size
    group = query_rows.shape[1] // kv_width
    grouped = query_rows.reshape(steps, kv_heads, group, head_size)
    keys = cache_tile[:, :kv_width].reshape(-1, kv_heads, head_size)
    values = cache_tile[:, kv_width:].reshape(-1, kv_heads, head_size)
    scores = jnp.einsum("skgd,tkd->skgt", grouped, keys, preferred_element_type=jnp.float32) * (
        1.0 / math.sqrt(head_size)
    )
    tops = jnp.max(scores, axis=3)
    weights = jnp.exp(scores - tops[..., None]).astype(jnp.bfloat16)
    totals = jnp.sum(weights.astype(jnp.float32), axis=3)
    mixed = jnp.einsum("skgt,tkd->skgd", weights, values, preferred_element_type=jnp.float32)
    return (tops.reshape(steps, -1), totals.reshape(steps, -1), mixed.reshape(steps, -1))


def finish(numer_pairs, denom_pairs, head_size):
    pairs = numer_pairs.shape[0]
    heads = denom_pairs.shape[1]
    shaped = numer_pairs.reshape(pairs, heads, head_size) / denom_pairs[..., None]
    return shaped.astype(jnp.bfloat16).reshape(pairs, heads * head_size)


def body(
    normed_input,
    query_weight,
    query_gain,
    image_cache,
    tile_count,
    image_first_slot,
    cross_tile_mask,
    output_weight,
    output_gate,
):
    rows, steps, local_width = normed_input.shape
    head_size = query_gain.shape[0]
    heads = query_weight.shape[1] // head_size
    slot_count = image_cache.shape[0]
    flattened = normed_input.reshape(rows * steps, local_width)
    query = lax.psum_scatter(
        jnp.dot(flattened, query_weight, preferred_element_type=jnp.float32),
        "tensor",
        scatter_dimension=0,
        tiled=True,
    )
    shaped = query.reshape(slot_count, heads, head_size)
    normed = (
        shaped * lax.rsqrt(jnp.mean(shaped * shaped, axis=2, keepdims=True) + EPSILON) * query_gain
    )
    normed = normed.astype(jnp.bfloat16).reshape(slot_count, heads * head_size)
    all_queries = lax.all_gather(normed, "tensor", axis=0, tiled=True)
    target_device = lax.axis_index("tensor")
    pool_slots = target_device * slot_count + jnp.arange(slot_count, dtype=jnp.int32)
    member_flag = membership(image_first_slot, tile_count, pool_slots)
    active_entry = active_status(member_flag, image_first_slot, cross_tile_mask, pool_slots)
    by_row = all_queries.reshape(rows, steps * heads * head_size)
    selected = jnp.dot(member_flag.astype(jnp.bfloat16), by_row, preferred_element_type=jnp.float32)
    selected = selected.astype(jnp.bfloat16).reshape(slot_count, steps, heads * head_size)

    def slot_term(operands):
        return tile_partial(operands[0], operands[1], head_size)

    tops, totals, mixed = lax.map(slot_term, (selected, image_cache))
    masked = jnp.where(active_entry[:, :, None], tops, NEGATIVE_FLOOR)
    pair_index = target_device * slot_count + jnp.arange(slot_count, dtype=jnp.int32)
    pair_row = pair_index // steps
    pair_step = pair_index % steps
    gathered_tops, gathered_totals, gathered_mixed = (
        lax.all_gather(masked, "tensor", axis=0, tiled=True),
        lax.all_gather(totals, "tensor", axis=0, tiled=True),
        lax.all_gather(mixed, "tensor", axis=0, tiled=True),
    )
    all_slots = gathered_tops.shape[0]
    every_slot = jnp.arange(all_slots, dtype=jnp.int32)
    full_member = membership(image_first_slot, tile_count, every_slot)
    slot_pick = full_member[:, pair_row]
    step_pick = jnp.arange(steps, dtype=jnp.int32)[None, :] == pair_step[:, None]
    chosen = slot_pick[:, :, None] & step_pick[None, :, :]
    spread = jnp.where(chosen[..., None], gathered_tops[:, None, :, :], NEGATIVE_FLOOR)
    pair_max = jnp.max(spread, axis=(0, 2))
    weights = jnp.where(chosen[..., None], jnp.exp(spread - pair_max[None, :, None, :]), 0.0)
    denom_pairs = jnp.sum(weights * gathered_totals[:, None, :, :], axis=(0, 2))
    mixed_heads = gathered_mixed.reshape(all_slots, steps, heads, head_size)
    numer_pairs = jnp.einsum(
        "spth,sthd->phd", weights, mixed_heads, precision=lax.Precision.HIGHEST
    )
    numer_pairs = numer_pairs.reshape(slot_count, heads * head_size)
    attended = finish(numer_pairs, denom_pairs, head_size)
    projected = jnp.dot(
        lax.all_gather(attended, "tensor", axis=0, tiled=True),
        output_weight,
        preferred_element_type=jnp.float32,
    )
    result = jnp.tanh(output_gate[0]) * projected
    return result.astype(jnp.bfloat16).reshape(rows, steps, -1)


def solution(mesh):
    return jax.shard_map(
        body,
        mesh=mesh,
        in_specs=(
            P("groups", None, "tensor"),
            P("tensor", None),
            P(),
            P(("groups", "tensor"), None, None),
            P("groups"),
            P("groups"),
            P("groups", None, None),
            P(None, "tensor"),
            P(),
        ),
        out_specs=P("groups", None, "tensor"),
        check_vma=False,
    )
```

profile of v0, /device:TPU:0, one launch (start us, length us, event | category | flops | bytes accessed | tf_op | source)
XLA Modules:
  0.0 216.5 jit_solution(3710583259249691234)
XLA Ops:
  6.5 0.7 reshape.264
  7.3 5.4 %fusion.27 = f32[16,8192]{1,0:T(8,128)} fusion(bf16[16,512]{1,0:T(8,128)(2,1)S(1)} %reshape.264, bf16[512,8192]{1,0:T(8,128)(2,1)} %param.10), kind=kOutput, calls=%fused_computation.45 | convolution fusion | flops 134217728 | bytes 8929280 | tf_op jit(solution)/shard_map/dot_general | solution.py:72
  12.7 3.7 %fusion.25 = (bf16[1601,1024]{1,0:T(8,128)(2,1)S(1)}, bf16[1601,1024]{1,0:T(8,128)(2,1)S(1)}) fusion(bf16[1601,2048]{1,0:T(8,128)(2,1)} %bitcast.51), kind=kLoop, calls=%fused_computation.43 | loop fusion | bytes 13115392 | tf_op jit(solution)/shard_map/while/body/eval_jaxpr/slice | solution.py:37
  16.4 0.9 copy.38
  17.3 0.3 slice_bitcast_fusion.1
  17.6 0.9 copy.39
  18.5 1.8 slice_bitcast_fusion
  20.3 0.6 dynamic-slice.4
  20.9 0.6 select_reduce_fusion.1
  21.5 84.1 %all-reduce.3.cloned.1.call-done = f32[16,8192]{1,0:T(8,128)} async-done(((f32[16,8192]{1,0:T(8,128)}), f32[16,8192]{1,0:T(8,128)}) %all-reduce.3.cloned.1.call-update) | async-done | bytes 524304
  105.6 1.6 dynamic-slice_multiply_fusion
  107.4 1.7 convert_bitcast_fusion
  109.1 23.7 %all-gather = bf16[16,1,8192]{2,1,0:T(2,128)(2,1)} all-gather(bf16[1,1,8192]{2,1,0:T(2,128)(2,1)S(1)} %convert_bitcast_fusion), channel_id=1, replica_groups=mesh['groups'=2,'tensor'=16] {'tensor'}, dimensions={0}, use_global_device_ids=true | all-gather | bytes 278528 | tf_op jit(solution)/shard_map/all_gather | solution.py:82
  132.8 3.2 %reduce.12 = bf16[16,8192]{1,0:T(8,128)(2,1)} reduce(bf16[16,1,8192]{2,1,0:T(2,128)(2,1)} %all-gather, bf16[]{:T(256)} %constant.103), dimensions={1}, to_apply=%all-gather.reduce_sub_computation | reduce | bytes 524290 | tf_op jit(solution)/shard_map/all_gather | solution.py:82
  136.0 1.1 reshape.265
  137.1 0.2 fusion.21
  137.3 1.1 fusion.26
  138.4 0.6 copy-done
  139.0 1.2 fusion.10
  140.2 0.7 broadcast_in_dim.87
  140.9 0.6 iota_compare_fusion.2
  142.9 0.2 multiply_reduce_fusion.1
  143.0 0.1 select_reduce_fusion
  143.2 1.4 convert_reduce_fusion
  144.8 17.4 %all_gather.18 = f32[16,2,64]{2,1,0:T(2,128)S(1)} all-gather(f32[1,2,64]{2,1,0:T(2,128)S(1)} %broadcast_in_dim.97), channel_id=1, replica_groups=mesh['groups'=2,'tensor'=16] {'tensor'}, dimensions={0}, use_global_device_ids=true | all-gather | bytes 8704 | tf_op jit(solution)/shard_map/all_gather | solution.py:101
  162.4 18.9 %all_gather.17 = f32[16,2,64]{2,1,0:T(2,128)S(1)} all-gather(f32[1,2,64]{2,1,0:T(2,128)S(1)} %broadcast_select_fusion.1), channel_id=1, replica_groups=mesh['groups'=2,'tensor'=16] {'tensor'}, dimensions={0}, use_global_device_ids=true | all-gather | bytes 8704 | tf_op jit(solution)/shard_map/all_gather | solution.py:100
  181.4 0.1 multiply_reduce_fusion
  181.6 2.1 reshape.269
  183.8 1.7 fusion.14
  185.6 18.9 %all-gather.1 = bf16[16,1,8192]{2,1,0:T(2,128)(2,1)S(1)} all-gather(bf16[1,1,8192]{2,1,0:T(2,128)(2,1)S(1)} %reshape.298), channel_id=1, replica_groups=mesh['groups'=2,'tensor'=16] {'tensor'}, dimensions={0}, use_global_device_ids=true | all-gather | bytes 278528 | tf_op jit(solution)/shard_map/all_gather | solution.py:121
  204.5 4.6 %fusion.13 = bf16[16,512]{1,0:T(8,128)(2,1)S(1)} fusion(bf16[8192,512]{1,0:T(8,128)(2,1)} %param.16, bf16[16,1,8192]{2,1,0:T(2,128)(2,1)S(1)} %all-gather.1, f32[]{:T(128)} %bitcast), kind=kOutput, calls=%fused_computation.10 | convolution fusion | flops 134234112 | bytes 8667140 | tf_op jit(solution)/shard_map/dot_general | solution.py:120
  209.1 0.6 reshape.271
  (39 shorter events, 1.0 us)
Async XLA Ops:
  6.5 99.1 %all-reduce.3.cloned.1.call-start = ((), (), s32[]{:S(2)}) async-start(), calls=%async_computation.1 | async-start | bytes 1048576
  12.7 169.0 %all-gather.4.cloned.1.call-start = ((), (), s32[]{:S(2)}) async-start(), calls=%async_computation | async-start | bytes 1114112 | tf_op jit(solution)/shard_map/all_gather | solution.py:102
  18.4 1.9 copy-start.6
  18.4 2.4 %copy-start.2 = (s32[8]{0:T(128)S(1)}, s32[8]{0:T(128)}, u32[]{:S(2)}) copy-start(s32[8]{0:T(128)} %param.14) | copy-start | bytes 100
  18.4 2.4 %copy-start.5 = (s32[8]{0:T(128)S(1)}, s32[8]{0:T(128)}, u32[]{:S(2)}) copy-start(s32[8]{0:T(128)} %param.13) | copy-start | bytes 100
  18.5 88.9 %copy-start.4 = (f32[128]{0:T(128)S(1)}, f32[128]{0:T(128)}, u32[]{:S(2)}) copy-start(f32[128]{0:T(128)} %param.11) | copy-start | bytes 1540
  137.1 1.9 copy-start
  138.4 1.8 copy-start.1
  138.4 4.4 %copy-start.3 = (s32[8,2,4]{0,2,1:T(4,128)S(1)}, s32[8,2,4]{0,2,1:T(4,128)}, u32[]{:S(2)}) copy-start(s32[8,2,4]{0,2,1:T(4,128)} %param.15) | copy-start | bytes 772
Sparse Core Ops, SparseCore 0:
  12.8 92.7 all-reduce.2
  141.0 35.2 all-gather.3
where the time goes:
time: 217 us
  waiting for transfers between devices  84.1 us (39%)
  blocking collectives  78.9 us (36%)
  between operations  14.9 us (7%)
  local copies, waits for them, and re-layouts  14.2 us (7%)
  matrix products  14.2 us (7%)
  other arithmetic  10.1 us (5%)
    unnamed x3, waiting for transfers between devices  84.1 us
    all_gather x1, blocking collectives, body(): all_queries = lax.all_gather(normed, 'tensor', axis=0, tiled=True)  23.7 us
    all_gather x1, blocking collectives, body(): lax.all_gather(masked, 'tensor', axis=0, tiled=True)  18.9 us
    all_gather x1, blocking collectives, body(): lax.all_gather(attended, 'tensor', axis=0, tiled=True)  18.9 us
    all_gather x1, blocking collectives, body(): lax.all_gather(totals, 'tensor', axis=0, tiled=True)  17.4 us
    dot_general x1, matrix products, body(): jnp.dot(flattened, query_weight, preferred_element_type=jnp.float32)  5.38 us
    dot_general x1, matrix products, body(): jnp.dot(lax.all_gather(attended, 'tensor', axis=0, tiled=True), output_we...  4.62 us
  transfers between devices with their start and end apart: 2, of which 1 were waited for; matrix products, arithmetic and copies ran while one was open for 5% of the time, Pallas kernels for 0%

commit v1 on v0

v1 whole, which is shorter than its diff:
```python
import functools
import math

import jax
import jax.numpy as jnp
from jax import lax
from jax.experimental import pallas as pl
from jax.experimental.pallas import tpu as pltpu
from jax.sharding import PartitionSpec as P

EPSILON = 1e-05
NEGATIVE_FLOOR = -1e30
AXIS = "tensor"
F32 = jnp.float32
BF16 = jnp.bfloat16
VMEM = pl.BlockSpec(memory_space=pltpu.VMEM)
SMEM = pl.BlockSpec(memory_space=pltpu.SMEM)
ANY = pl.BlockSpec(memory_space=pl.ANY)


def struct(shape, dtype):
    return jax.ShapeDtypeStruct(shape, dtype)


def params(mebibytes):
    return pltpu.CompilerParams(vmem_limit_bytes=mebibytes << 20)


def scatter_stages(bits):
    if bits < 3:
        return [[bit] for bit in range(bits)]
    return [[0], [1, 2]] + [[bit] for bit in range(3, bits)]


def offsets(group):
    result = [0]
    for bit in group:
        result = result + [other | (1 << bit) for other in result]
    return result


def positions(stages):
    result = [0]
    for group in stages:
        result = [base | step for base in result for step in offsets(group)]
    return result


def move_bits(value, moves):
    result = value & 0
    for source, target in moves:
        result = result | (((value >> source) & 1) << target)
    return result


def exchange(array, difference, count):
    return lax.ppermute(array, AXIS, [(i, i ^ difference) for i in range(count)])


def project_kernel(
    order, chunks, kv_heads, group, head_size, x_ref, weight_hbm, first_ref, count_ref, keep_ref,
    send_ref, weight, sems
):
    rows, steps, depth = x_ref.shape
    width = weight.shape[1]
    chunk = width // chunks
    copies = [
        pltpu.make_async_copy(
            weight_hbm.at[:, pl.ds(c * chunk, chunk)], weight.at[:, pl.ds(c * chunk, chunk)], sems.at[c]
        )
        for c in range(chunks)
    ]
    for copy in copies:
        copy.start()
    slots = len(order)
    half = slots // 2
    me = lax.axis_index(AXIS)
    shape = (steps * slots, rows * steps)
    out_row = lax.broadcasted_iota(jnp.int32, shape, 0)
    place = out_row % slots
    step = out_row // slots
    in_row = lax.broadcasted_iota(jnp.int32, shape, 1)
    bits = range(slots.bit_length() - 1)
    slot = move_bits(place, [(i, order[1 << i].bit_length() - 1) for i in bits]) ^ me
    start = jnp.zeros(shape, jnp.int32)
    length = jnp.zeros(shape, jnp.int32)
    for row in range(rows):
        here = in_row // steps == row
        start = jnp.where(here, first_ref[row], start)
        length = jnp.where(here, count_ref[row], length)
    chosen = (slot >= start) & (slot < start + length) & (in_row % steps == step)
    flat = x_ref[...].reshape(rows * steps, depth)
    picked = jnp.dot(
        jnp.where(chosen, 1.0, 0.0).astype(BF16), flat, preferred_element_type=F32
    ).astype(BF16)
    tile_rows = steps * kv_heads * group
    heads_per_chunk = chunk // head_size
    for c in range(chunks):
        copies[c].wait()
        result = jnp.dot(
            picked, weight[:, c * chunk : (c + 1) * chunk], preferred_element_type=F32
        )
        for local in range(heads_per_chunk):
            head = c * heads_per_chunk + local
            for s in range(steps):
                at = (head // group) * steps * group + s * group + head % group
                block = result[s * slots : (s + 1) * slots, local * head_size : (local + 1) * head_size]
                keep_ref[pl.ds(at, half, stride=tile_rows), :] = block[:half]
                send_ref[pl.ds(at, half, stride=tile_rows), :] = block[half:]


def sum_kernel(inputs, *refs):
    total = refs[0][...]
    for ref in refs[1:inputs]:
        total = total + ref[...]
    outs = refs[inputs:]
    size = outs[0].shape[0]
    for i, out in enumerate(outs):
        out[...] = total[i * size : (i + 1) * size]


def add_and_split(arrays, pieces):
    rows, lanes = arrays[0].shape
    return pl.pallas_call(
        functools.partial(sum_kernel, len(arrays)),
        out_shape=[struct((rows // pieces, lanes), F32)] * pieces,
        in_specs=[VMEM] * len(arrays),
        out_specs=[VMEM] * pieces,
        compiler_params=params(16),
    )(*arrays)


def attend_kernel(
    partials, kv_heads, group, steps, *refs
):
    parts = refs[:partials]
    gain_ref, cache_ref, first_ref, count_ref, mask_ref, out_ref = refs[partials:]
    head_size = gain_ref.shape[-1]
    kv_width = kv_heads * head_size
    query = parts[0][...]
    for part in parts[1:]:
        query = query + part[...]
    mean = jnp.mean(query * query, axis=1, keepdims=True)
    normed = (query * lax.rsqrt(mean + EPSILON) * gain_ref[...]).astype(BF16)
    me = lax.axis_index(AXIS)
    rows = first_ref.shape[0]

    def find(row, carry):
        owner, tile = carry
        offset = me - first_ref[row]
        inside = (offset >= 0) & (offset < count_ref[row])
        return jnp.where(inside, row, owner), jnp.where(inside, offset, tile)

    owner, tile = lax.fori_loop(0, rows, find, (jnp.int32(0), jnp.int32(0)), unroll=rows <= 16)
    size = steps * group
    row_in_tile = lax.broadcasted_iota(jnp.int32, (size, head_size), 0)
    lane = lax.broadcasted_iota(jnp.int32, (size, head_size), 1)
    stats = jnp.zeros((size, head_size), F32)
    scale = 1.0 / math.sqrt(head_size)
    for h in range(kv_heads):
        keys = cache_ref[0, :, h * head_size : (h + 1) * head_size]
        values = cache_ref[0, :, kv_width + h * head_size : kv_width + (h + 1) * head_size]
        scores = lax.dot_general(
            normed[h * size : (h + 1) * size],
            keys,
            (((1,), (1,)), ((), ())),
            preferred_element_type=F32,
        ) * scale
        top = jnp.max(scores, axis=1, keepdims=True)
        weights = jnp.exp(scores - top).astype(BF16)
        total = jnp.sum(weights.astype(F32), axis=1, keepdims=True)
        mixed = jnp.dot(weights, values, preferred_element_type=F32)
        out_ref[h * size : (h + 1) * size, :] = (mixed / total).astype(BF16)
        here = lane % kv_heads == h
        stats = jnp.where(here, jnp.where(lane < 3 * kv_heads, top, total), stats)
    live = jnp.zeros((size, head_size), jnp.bool_)
    for s in range(steps):
        alive = (tile == 0) | (mask_ref[owner, s, tile] == 1)
        live = live | ((row_in_tile // group == s) & alive)
    stats = jnp.where(live | (lane >= 3 * kv_heads), stats, NEGATIVE_FLOOR)
    high = stats.astype(BF16).astype(F32)
    rest = stats - high
    middle = rest.astype(BF16).astype(F32)
    low = rest - middle
    piece = (lane // kv_heads) % 3
    packed = jnp.where(piece == 0, high, jnp.where(piece == 1, middle, low))
    out_ref[kv_heads * size :, :] = packed.astype(BF16)


def finish_kernel(
    order, kv_heads, group, steps, max_tiles, gate_ref, first_ref, count_ref, tiles_ref, weight_ref, out_ref, stats, turned
):
    rows = first_ref.shape[0]
    head_size = tiles_ref.shape[-1]
    size = steps * group
    block = (kv_heads + 1) * size
    slots = tiles_ref.shape[0]
    me = lax.axis_index(AXIS)
    packed = tiles_ref[:, kv_heads * size :, :].astype(F32).reshape(slots * size, head_size)
    whole = (
        packed
        + pltpu.roll(packed, head_size - kv_heads, 1)
        + pltpu.roll(packed, head_size - 2 * kv_heads, 1)
    )
    stats[0] = whole
    stats[1] = pltpu.roll(whole, head_size - 3 * kv_heads, 1)
    pairs = rows * steps
    moves = [(order[1 << i].bit_length() - 1, i) for i in range(slots.bit_length() - 1)]

    def one_row(row, carry):
        begin = first_ref[row]
        length = count_ref[row]
        places = [
            move_bits(me ^ (begin + jnp.minimum(k, length - 1)), moves) for k in range(max_tiles)
        ]
        tops = []
        for k in range(max_tiles):
            top = stats[0, pl.ds(places[k] * size, size), :]
            tops.append(jnp.where(k < length, top, NEGATIVE_FLOOR))
        best = functools.reduce(jnp.maximum, tops)
        factors = []
        for k in range(max_tiles):
            total = stats[1, pl.ds(places[k] * size, size), :]
            factor = jnp.exp(tops[k] - best) * total
            factors.append(jnp.where(tops[k] > 0.5 * NEGATIVE_FLOOR, factor, 0.0))
        denominator = functools.reduce(jnp.add, factors)
        shares = [factor / denominator for factor in factors]
        for h in range(kv_heads):
            mixed = jnp.zeros((size, head_size), F32)
            for k in range(max_tiles):
                value = tiles_ref[places[k], h * size : (h + 1) * size, :].astype(F32)
                mixed = mixed + shares[k][:, h : h + 1] * value
            for s in range(steps):
                turned[pl.ds(h * group * pairs + row * steps + s, group, stride=pairs), :] = mixed[
                    s * group : (s + 1) * group
                ]
        return carry

    lax.fori_loop(0, rows, one_row, 0)
    total = jnp.zeros((pairs, weight_ref.shape[1]), F32)
    for h in range(kv_heads):
        left = jnp.concatenate(
            [
                turned[(h * group + g) * pairs : (h * group + g + 1) * pairs, :].astype(BF16)
                for g in range(group)
            ],
            axis=1,
        )
        span = group * head_size
        total = total + jnp.dot(
            left, weight_ref[h * span : (h + 1) * span, :], preferred_element_type=F32
        )
    gate = jnp.tanh(jnp.full((1, 1), gate_ref[0], F32))
    result = (total * gate).astype(BF16)
    out_ref[...] = result.reshape(rows, steps, result.shape[1])


def body(
    devices,
    normed_input,
    query_weight,
    query_gain,
    image_cache,
    tile_count,
    image_first_slot,
    cross_tile_mask,
    output_weight,
    output_gate,
):
    rows, steps, depth = normed_input.shape
    head_size = query_gain.shape[0]
    width = query_weight.shape[1]
    heads = width // head_size
    kv_heads = image_cache.shape[2] // (2 * head_size)
    group = heads // kv_heads
    tile_rows = steps * heads
    stages = scatter_stages(devices.bit_length() - 1)
    order = positions(stages)
    half = devices // 2
    chunks = 8
    keep, send = pl.pallas_call(
        functools.partial(project_kernel, order, chunks, kv_heads, group, head_size),
        out_shape=[struct((half * tile_rows, head_size), F32)] * 2,
        in_specs=[VMEM, ANY, SMEM, SMEM],
        out_specs=[VMEM, VMEM],
        scratch_shapes=[pltpu.VMEM((depth, width), BF16), pltpu.SemaphoreType.DMA((chunks,))],
        compiler_params=params(40),
    )(normed_input, query_weight, image_first_slot, tile_count)
    parts = [keep, exchange(send, 1, devices)]
    for group_bits in stages[1:]:
        steps_out = offsets(group_bits)
        pieces = add_and_split(parts, len(steps_out))
        parts = [pieces[0]] + [
            exchange(piece, step, devices) for piece, step in zip(pieces[1:], steps_out[1:])
        ]
    block = (kv_heads + 1) * steps * group
    tile = pl.pallas_call(
        functools.partial(attend_kernel, len(parts), kv_heads, group, steps),
        out_shape=struct((block, head_size), BF16),
        in_specs=[VMEM] * (len(parts) + 2) + [SMEM] * 3,
        out_specs=VMEM,
        compiler_params=params(16),
    )(*parts, query_gain, image_cache, image_first_slot, tile_count, cross_tile_mask)
    gathered = tile[None]
    for group_bits in reversed(stages):
        gathered = jnp.concatenate(
            [gathered] + [exchange(gathered, step, devices) for step in offsets(group_bits)[1:]], axis=0
        )
    return pl.pallas_call(
        functools.partial(finish_kernel, order, kv_heads, group, steps, cross_tile_mask.shape[2]),
        out_shape=struct((rows, steps, output_weight.shape[1]), BF16),
        in_specs=[SMEM] * 3 + [VMEM, VMEM],
        out_specs=VMEM,
        scratch_shapes=[
            pltpu.VMEM((2, devices * steps * group, head_size), F32),
            pltpu.VMEM((heads * rows * steps, head_size), F32),
        ],
        compiler_params=params(24),
    )(output_gate, image_first_slot, tile_count, gathered, output_weight)


def solution(mesh):
    return jax.shard_map(
        functools.partial(body, mesh.shape[AXIS]),
        mesh=mesh,
        in_specs=(
            P("groups", None, "tensor"),
            P("tensor", None),
            P(),
            P(("groups", "tensor"), None, None),
            P("groups"),
            P("groups"),
            P("groups", None, None),
            P(None, "tensor"),
            P(),
        ),
        out_specs=P("groups", None, "tensor"),
        check_vma=False,
    )
```

time: 217 us -> 54.7 us (0.25)
  blocking collectives: 78.9 us -> 0 us
  waiting for transfers between devices: 84.1 us -> 18.3 us
  starting transfers between devices: 0.04 us -> 14.3 us
  matrix products: 14.2 us -> 0 us
  between operations: 14.9 us -> 0.73 us
  Pallas kernels: 0 us -> 12.6 us
  other arithmetic: 10.1 us -> 0.01 us
  local copies, waits for them, and re-layouts: 14.2 us -> 8.59 us
    unnamed x3 -> x0, waiting for transfers between devices: 84.1 us -> none
    all_gather x4 -> x0, blocking collectives: 78.9 us -> none  [the longest x1 23.7 us: body(): all_queries = lax.all_gather(normed, 'tensor', axis=0, tiled=True)]
    ppermute x0 -> x10, waiting for transfers between devices: none -> 18.3 us  [exchange(): lax.ppermute(array, AXIS, [(i, i ^ difference) for i in range(count)])]
    ppermute x0 -> x10, starting transfers between devices: none -> 14.3 us  [exchange(): lax.ppermute(array, AXIS, [(i, i ^ difference) for i in range(count)])]
    dot_general x6 -> x0, matrix products: 14.2 us -> none  [the longest x1 5.38 us: body(): jnp.dot(flattened, query_weight, preferred_element_type=jnp.float32)]
    pallas_call x0 -> x5, Pallas kernels: none -> 12.6 us  [the longest x1 4.45 us: body(): pl.pallas_call(functools.partial(project_kernel, order, chunks, kv_heads,...]
    reshape x6 -> x0, local copies, waits for them, and re-layouts: 6.62 us -> none  [the longest x1 2.13 us: body(): mixed_heads = gathered_mixed.reshape(all_slots, steps, heads, head_size)]
    unnamed x18 -> x25, local copies, waits for them, and re-layouts: 2.9 us -> 8.52 us
  transfers between devices with their start and end apart: 2 -> 10, of which waited for: 1 -> 10; matrix products, arithmetic and copies ran while one was open for 5% -> 0% of each run, Pallas kernels for 0% -> 0%
where the time goes in v1:
time: 54.7 us; the launch traced here: 54.5 us
  waiting for transfers between devices  18.3 us (33%)
  starting transfers between devices  14.3 us (26%)
  Pallas kernels  12.6 us (23%)
  local copies, waits for them, and re-layouts  8.59 us (16%)
  between operations  0.73 us (1%)
    ppermute x10, waiting for transfers between devices, exchange(): lax.ppermute(array, AXIS, [(i, i ^ difference) for i in range(count)])  18.3 us
    ppermute x10, starting transfers between devices, exchange(): lax.ppermute(array, AXIS, [(i, i ^ difference) for i in range(count)])  14.3 us
    unnamed x25, local copies, waits for them, and re-layouts  8.52 us
    pallas_call x1, Pallas kernels, body(): pl.pallas_call(functools.partial(project_kernel, order, chunks, kv_heads,...  4.45 us
    pallas_call x1, Pallas kernels, body(): pl.pallas_call(functools.partial(finish_kernel, order, kv_heads, group, s...  4.1 us
    pallas_call x1, Pallas kernels, body(): pl.pallas_call(functools.partial(attend_kernel, len(parts), kv_heads, gro...  3.97 us
  transfers between devices with their start and end apart: 10, of which 10 were waited for; matrix products, arithmetic and copies ran while one was open for 0% of the time, Pallas kernels for 0%

profile of v1, /device:TPU:0, one launch (start us, length us, event | category | flops | bytes accessed | tf_op | source)
XLA Modules:
  0.0 54.5 jit_solution(10680205568844377308)
XLA Ops:
  0.0 3.4 %copy-done.1 = bf16[512,8192]{1,0:T(8,128)(2,1)S(1)} copy-done((bf16[512,8192]{1,0:T(8,128)(2,1)S(1)}, bf16[512,8192]{1,0:T(8,128)(2,1)}, u32[]{:S(2)}) %copy-start.1) | copy-done | bytes 8388632
  3.4 0.7 %copy-done.3 = bf16[8,2,512]{2,1,0:T(2,128)(2,1)S(1)} copy-done((bf16[8,2,512]{2,1,0:T(2,128)(2,1)S(1)}, bf16[8,2,512]{2,1,0:T(2,128)(2,1)}, u32[]{:S(2)}) %copy-start.3) | copy-done | bytes 16408
  4.1 0.7 %copy-done.4 = s32[8]{0:T(128)S(1)} copy-done((s32[8]{0:T(128)S(1)}, s32[8]{0:T(128)}, u32[]{:S(2)}) %copy-start.4) | copy-done | bytes 56
  4.8 0.7 %copy-done.6 = s32[8]{0:T(128)S(1)} copy-done((s32[8]{0:T(128)S(1)}, s32[8]{0:T(128)}, u32[]{:S(2)}) %copy-start.6) | copy-done | bytes 56
  5.4 4.4 %shard_map.91 = (f32[1024,128]{1,0:T(8,128)S(1)}, f32[1024,128]{1,0:T(8,128)S(1)}) custom-call(bf16[8,2,512]{2,1,0:T(2,128)(2,1)S(1)} %copy-done.3, bf16[512,8192]{1,0:T(8,128)(2,1)S(1)} %copy-done.1, s32[8]{0:T(128)S(1)} %copy-done.4, s32[8]{0:T(128)S(1)} %copy-done.6), custom_call_target="tpu_custom_call" | custom-call | tf_op jit(solution)/shard_map/pallas_call | solution.py:281
  9.9 0.5 collective-permute-start
  10.4 1.5 %collective-permute-done.refs_1_ = f32[1024,128]{1,0:T(8,128)S(1)} collective-permute-done((f32[1024,128]{1,0:T(8,128)S(1)}, f32[1024,128]{1,0:T(8,128)S(1)}, u32[]{:S(2)}, u32[]{:S(2)}) %collective-permute-start) | collective-permute-done | bytes 524320 | tf_op jit(solution)/shard_map/ppermute | solution.py:57
  11.9 0.1 shard_map.92
  12.0 2.9 %collective-permute-start.1 = (f32[256,128]{1,0:T(8,128)S(1)}, f32[256,128]{1,0:T(8,128)S(1)}, u32[]{:S(2)}, u32[]{:S(2)}) collective-permute-start(f32[256,128]{1,0:T(8,128)S(1)} %get-tuple-element.16), channel_id=1, source_target_pairs={{0,2},{1,3},{2,0},{3,1},{4,6},{5,7},{6,4},{7,5},{8,10},{9,11},{10,... | collective-permute-start | bytes 393224 | tf_op jit(solution)/shard_map/ppermute | solution.py:57
  14.9 1.6 %collective-permute-start.2 = (f32[256,128]{1,0:T(8,128)S(1)}, f32[256,128]{1,0:T(8,128)S(1)}, u32[]{:S(2)}, u32[]{:S(2)}) collective-permute-start(f32[256,128]{1,0:T(8,128)S(1)} %get-tuple-element.17), channel_id=1, source_target_pairs={{0,4},{1,5},{2,6},{3,7},{4,0},{5,1},{6,2},{7,3},{8,12},{9,13},{10,... | collective-permute-start | bytes 393224 | tf_op jit(solution)/shard_map/ppermute | solution.py:57
  16.5 0.0 collective-permute-start.3
  16.5 2.2 %collective-permute-done.1.refs_1_ = f32[256,128]{1,0:T(8,128)S(1)} collective-permute-done((f32[256,128]{1,0:T(8,128)S(1)}, f32[256,128]{1,0:T(8,128)S(1)}, u32[]{:S(2)}, u32[]{:S(2)}) %collective-permute-start.1) | collective-permute-done | bytes 131104 | tf_op jit(solution)/shard_map/ppermute | solution.py:57
  18.7 2.6 %collective-permute-done.2.refs_2_ = f32[256,128]{1,0:T(8,128)S(1)} collective-permute-done((f32[256,128]{1,0:T(8,128)S(1)}, f32[256,128]{1,0:T(8,128)S(1)}, u32[]{:S(2)}, u32[]{:S(2)}) %collective-permute-start.2) | collective-permute-done | bytes 131104 | tf_op jit(solution)/shard_map/ppermute | solution.py:57
  21.3 1.5 %collective-permute-done.3.refs_3_ = f32[256,128]{1,0:T(8,128)S(1)} collective-permute-done((f32[256,128]{1,0:T(8,128)S(1)}, f32[256,128]{1,0:T(8,128)S(1)}, u32[]{:S(2)}, u32[]{:S(2)}) %collective-permute-start.3) | collective-permute-done | bytes 131104 | tf_op jit(solution)/shard_map/ppermute | solution.py:57
  22.8 2.8 %collective-permute-start.4 = (f32[128,128]{1,0:T(8,128)S(1)}, f32[128,128]{1,0:T(8,128)S(1)}, u32[]{:S(2)}, u32[]{:S(2)}) collective-permute-start(f32[128,128]{1,0:T(8,128)S(1)} %get-tuple-element.20), channel_id=1, source_target_pairs={{0,8},{1,9},{2,10},{3,11},{4,12},{5,13},{6,14},{7,15},{8,0},{9,1},... | collective-permute-start | bytes 196616 | tf_op jit(solution)/shard_map/ppermute | solution.py:57
  25.7 0.1 copy.10.refs_6_
  25.7 2.3 %collective-permute-done.4.refs_1_ = f32[128,128]{1,0:T(8,128)S(1)} collective-permute-done((f32[128,128]{1,0:T(8,128)S(1)}, f32[128,128]{1,0:T(8,128)S(1)}, u32[]{:S(2)}, u32[]{:S(2)}) %collective-permute-start.4) | collective-permute-done | bytes 65568 | tf_op jit(solution)/shard_map/ppermute | solution.py:57
  28.1 0.0 copy-done.7
  28.1 0.0 copy-start.2
  28.1 2.9 %copy-done.2 = bf16[1,1601,2048]{2,1,0:T(8,128)(2,1)S(1)} copy-done((bf16[1,1601,2048]{2,1,0:T(8,128)(2,1)S(1)}, bf16[1,1601,2048]{2,1,0:T(8,128)(2,1)}, u32[]{:S(2)}) %copy-start.2) | copy-done | bytes 6557720
  31.0 4.0 %shard_map.94 = bf16[144,128]{1,0:T(8,128)(2,1)S(1)} custom-call(f32[128,128]{1,0:T(8,128)S(1)} %get-tuple-element.19.refs_0_, f32[128,128]{1,0:T(8,128)S(1)} %collective-permute-done.4.refs_1_, f32[128]{0:T(128)S(1)} %copy-done.8, bf16[1,1601,2048]{2,1,0:T(8,128)(2,1)S(1)} %copy-done.2, s32[8]{0:T(128)S(1)} %copy-done.5, s32[8]{0:T(128)S(1)} %copy-done.7, ...), custom_call_target="tpu_custom_call" | custom-call | tf_op jit(solution)/shard_map/pallas_call | solution.py:297
  35.0 2.8 %collective-permute-start.5 = (bf16[1,144,128]{2,1,0:T(8,128)(2,1)S(1)}, bf16[1,144,128]{2,1,0:T(8,128)(2,1)S(1)}, u32[]{:S(2)}, u32[]{:S(2)}) collective-permute-start(bf16[1,144,128]{2,1,0:T(8,128)(2,1)S(1)} %bitcast.3), channel_id=1, source_target_pairs={{0,8},{1,9},{2,10},{3,11},{4,12},{5,13},{6,14},{7,15},{8,0},{9,1},... | collective-permute-start | bytes 110600 | tf_op jit(solution)/shard_map/ppermute | solution.py:57
  37.8 2.1 %collective-permute-done.5 = bf16[1,144,128]{2,1,0:T(8,128)(2,1)S(1)} collective-permute-done((bf16[1,144,128]{2,1,0:T(8,128)(2,1)S(1)}, bf16[1,144,128]{2,1,0:T(8,128)(2,1)S(1)}, u32[]{:S(2)}, u32[]{:S(2)}) %collective-permute-start.5) | collective-permute-done | bytes 36896 | tf_op jit(solution)/shard_map/ppermute | solution.py:57
  39.9 1.7 %collective-permute-start.6 = (bf16[2,144,128]{2,1,0:T(8,128)(2,1)S(1)}, bf16[2,144,128]{2,1,0:T(8,128)(2,1)S(1)}, u32[]{:S(2)}, u32[]{:S(2)}) collective-permute-start(bf16[2,144,128]{2,1,0:T(8,128)(2,1)S(1)} %pad_maximum_fusion), channel_id=1, source_target_pairs={{0,2},{1,3},{2,0},{3,1},{4,6},{5,7},{6,4},{7,5},{8,10},{9,11},{10,... | collective-permute-start | bytes 221192 | tf_op jit(solution)/shard_map/ppermute | solution.py:57
  41.6 1.8 %collective-permute-start.7 = (bf16[2,144,128]{2,1,0:T(8,128)(2,1)S(1)}, bf16[2,144,128]{2,1,0:T(8,128)(2,1)S(1)}, u32[]{:S(2)}, u32[]{:S(2)}) collective-permute-start(bf16[2,144,128]{2,1,0:T(8,128)(2,1)S(1)} %pad_maximum_fusion), channel_id=1, source_target_pairs={{0,4},{1,5},{2,6},{3,7},{4,0},{5,1},{6,2},{7,3},{8,12},{9,13},{10,... | collective-permute-start | bytes 221192 | tf_op jit(solution)/shard_map/ppermute | solution.py:57
  43.4 0.1 collective-permute-start.8
  43.5 1.6 %collective-permute-done.6 = bf16[2,144,128]{2,1,0:T(8,128)(2,1)S(1)} collective-permute-done((bf16[2,144,128]{2,1,0:T(8,128)(2,1)S(1)}, bf16[2,144,128]{2,1,0:T(8,128)(2,1)S(1)}, u32[]{:S(2)}, u32[]{:S(2)}) %collective-permute-start.6) | collective-permute-done | bytes 73760 | tf_op jit(solution)/shard_map/ppermute | solution.py:57
  45.1 0.8 %collective-permute-done.7 = bf16[2,144,128]{2,1,0:T(8,128)(2,1)S(1)} collective-permute-done((bf16[2,144,128]{2,1,0:T(8,128)(2,1)S(1)}, bf16[2,144,128]{2,1,0:T(8,128)(2,1)S(1)}, u32[]{:S(2)}, u32[]{:S(2)}) %collective-permute-start.7) | collective-permute-done | bytes 73760 | tf_op jit(solution)/shard_map/ppermute | solution.py:57
  46.0 2.7 %collective-permute-done.8 = bf16[2,144,128]{2,1,0:T(8,128)(2,1)S(1)} collective-permute-done((bf16[2,144,128]{2,1,0:T(8,128)(2,1)S(1)}, bf16[2,144,128]{2,1,0:T(8,128)(2,1)S(1)}, u32[]{:S(2)}, u32[]{:S(2)}) %collective-permute-start.8) | collective-permute-done | bytes 73760 | tf_op jit(solution)/shard_map/ppermute | solution.py:57
  48.7 0.1 collective-permute-start.9
  49.4 0.9 %collective-permute-done.9 = bf16[8,144,128]{2,1,0:T(8,128)(2,1)S(1)} collective-permute-done((bf16[8,144,128]{2,1,0:T(8,128)(2,1)S(1)}, bf16[8,144,128]{2,1,0:T(8,128)(2,1)S(1)}, u32[]{:S(2)}, u32[]{:S(2)}) %collective-permute-start.9) | collective-permute-done | bytes 294944 | tf_op jit(solution)/shard_map/ppermute | solution.py:57
  50.4 4.1 %shard_map.95 = bf16[8,2,512]{2,1,0:T(2,128)(2,1)} custom-call(f32[1]{0:T(128)S(6)} %copy.20.gate_ref, s32[8]{0:T(128)S(1)} %copy-done.5, s32[8]{0:T(128)S(1)} %copy-done.7, bf16[16,144,128]{2,1,0:T(8,128)(2,1)S(1)} %constant_dynamic-update-slice_fusion.5.tiles_ref, bf16[8192,512]{1,0:T(8,128)(2,1)S(1)} %copy-done), custom_call_target="tpu_custom_call" | custom-call | tf_op jit(solution)/shard_map/pallas_call | solution.py:309
  (21 shorter events, 0.2 us)
Async XLA Ops:
  0.0 3.4 %copy-start.1 = (bf16[512,8192]{1,0:T(8,128)(2,1)S(1)}, bf16[512,8192]{1,0:T(8,128)(2,1)}, u32[]{:S(2)}) copy-start(bf16[512,8192]{1,0:T(8,128)(2,1)} %weight_hbm.1) | copy-start | bytes 25165828
  3.4 0.7 %copy-start.3 = (bf16[8,2,512]{2,1,0:T(2,128)(2,1)S(1)}, bf16[8,2,512]{2,1,0:T(2,128)(2,1)}, u32[]{:S(2)}) copy-start(bf16[8,2,512]{2,1,0:T(2,128)(2,1)} %x_ref.1) | copy-start | bytes 49156
  4.1 0.7 %copy-start.4 = (s32[8]{0:T(128)S(1)}, s32[8]{0:T(128)}, u32[]{:S(2)}) copy-start(s32[8]{0:T(128)} %first_ref.3) | copy-start | bytes 100
  4.8 0.7 %copy-start.6 = (s32[8]{0:T(128)S(1)}, s32[8]{0:T(128)}, u32[]{:S(2)}) copy-start(s32[8]{0:T(128)} %count_ref.3) | copy-start | bytes 100
  5.4 20.2 %copy-start.9 = (s32[8,2,4]{0,2,1:T(4,128)S(1)}, s32[8,2,4]{0,2,1:T(4,128)}, u32[]{:S(2)}) copy-start(s32[8,2,4]{0,2,1:T(4,128)} %param.15) | copy-start | bytes 772
  5.4 22.6 %copy-start.5 = (s32[8]{0:T(128)S(1)}, s32[8]{0:T(128)}, u32[]{:S(2)}) copy-start(s32[8]{0:T(128)} %first_ref.3) | copy-start | bytes 100
  5.4 22.6 %copy-start.7 = (s32[8]{0:T(128)S(1)}, s32[8]{0:T(128)}, u32[]{:S(2)}) copy-start(s32[8]{0:T(128)} %count_ref.3) | copy-start | bytes 100
  5.4 22.7 %copy-start.8 = (f32[128]{0:T(128)S(1)}, f32[128]{0:T(128)}, u32[]{:S(2)}) copy-start(f32[128]{0:T(128)} %refs_2_.1) | copy-start | bytes 1540
  9.9 2.1 %collective-permute-start = (f32[1024,128]{1,0:T(8,128)S(1)}, f32[1024,128]{1,0:T(8,128)S(1)}, u32[]{:S(2)}, u32[]{:S(2)}) collective-permute-start(f32[1024,128]{1,0:T(8,128)S(1)} %get-tuple-element.14), channel_id=1, source_target_pairs={{0,1},{1,0},{2,3},{3,2},{4,5},{5,4},{6,7},{7,6},{8,9},{9,8},{10,11... | collective-permute-start | bytes 1572872 | tf_op jit(solution)/shard_map/ppermute | solution.py:57
  12.0 6.7 %collective-permute-start.1 = (f32[256,128]{1,0:T(8,128)S(1)}, f32[256,128]{1,0:T(8,128)S(1)}, u32[]{:S(2)}, u32[]{:S(2)}) collective-permute-start(f32[256,128]{1,0:T(8,128)S(1)} %get-tuple-element.16), channel_id=1, source_target_pairs={{0,2},{1,3},{2,0},{3,1},{4,6},{5,7},{6,4},{7,5},{8,10},{9,11},{10,... | collective-permute-start | bytes 393224 | tf_op jit(solution)/shard_map/ppermute | solution.py:57
  14.9 6.4 %collective-permute-start.2 = (f32[256,128]{1,0:T(8,128)S(1)}, f32[256,128]{1,0:T(8,128)S(1)}, u32[]{:S(2)}, u32[]{:S(2)}) collective-permute-start(f32[256,128]{1,0:T(8,128)S(1)} %get-tuple-element.17), channel_id=1, source_target_pairs={{0,4},{1,5},{2,6},{3,7},{4,0},{5,1},{6,2},{7,3},{8,12},{9,13},{10,... | collective-permute-start | bytes 393224 | tf_op jit(solution)/shard_map/ppermute | solution.py:57
  16.5 6.3 %collective-permute-start.3 = (f32[256,128]{1,0:T(8,128)S(1)}, f32[256,128]{1,0:T(8,128)S(1)}, u32[]{:S(2)}, u32[]{:S(2)}) collective-permute-start(f32[256,128]{1,0:T(8,128)S(1)} %get-tuple-element.18), channel_id=1, source_target_pairs={{0,6},{1,7},{2,4},{3,5},{4,2},{5,3},{6,0},{7,1},{8,14},{9,15},{10,... | collective-permute-start | bytes 393224 | tf_op jit(solution)/shard_map/ppermute | solution.py:57
  22.8 5.2 %collective-permute-start.4 = (f32[128,128]{1,0:T(8,128)S(1)}, f32[128,128]{1,0:T(8,128)S(1)}, u32[]{:S(2)}, u32[]{:S(2)}) collective-permute-start(f32[128,128]{1,0:T(8,128)S(1)} %get-tuple-element.20), channel_id=1, source_target_pairs={{0,8},{1,9},{2,10},{3,11},{4,12},{5,13},{6,14},{7,15},{8,0},{9,1},... | collective-permute-start | bytes 196616 | tf_op jit(solution)/shard_map/ppermute | solution.py:57
  25.7 24.6 %copy-start = (bf16[8192,512]{1,0:T(8,128)(2,1)S(1)}, bf16[8192,512]{1,0:T(8,128)(2,1)}, u32[]{:S(2)}) copy-start(bf16[8192,512]{1,0:T(8,128)(2,1)} %weight_ref.1) | copy-start | bytes 25165828
  28.1 2.9 %copy-start.2 = (bf16[1,1601,2048]{2,1,0:T(8,128)(2,1)S(1)}, bf16[1,1601,2048]{2,1,0:T(8,128)(2,1)}, u32[]{:S(2)}) copy-start(bf16[1,1601,2048]{2,1,0:T(8,128)(2,1)} %refs_3_.1) | copy-start | bytes 19673092
  35.0 4.9 %collective-permute-start.5 = (bf16[1,144,128]{2,1,0:T(8,128)(2,1)S(1)}, bf16[1,144,128]{2,1,0:T(8,128)(2,1)S(1)}, u32[]{:S(2)}, u32[]{:S(2)}) collective-permute-start(bf16[1,144,128]{2,1,0:T(8,128)(2,1)S(1)} %bitcast.3), channel_id=1, source_target_pairs={{0,8},{1,9},{2,10},{3,11},{4,12},{5,13},{6,14},{7,15},{8,0},{9,1},... | collective-permute-start | bytes 110600 | tf_op jit(solution)/shard_map/ppermute | solution.py:57
  39.9 5.2 %collective-permute-start.6 = (bf16[2,144,128]{2,1,0:T(8,128)(2,1)S(1)}, bf16[2,144,128]{2,1,0:T(8,128)(2,1)S(1)}, u32[]{:S(2)}, u32[]{:S(2)}) collective-permute-start(bf16[2,144,128]{2,1,0:T(8,128)(2,1)S(1)} %pad_maximum_fusion), channel_id=1, source_target_pairs={{0,2},{1,3},{2,0},{3,1},{4,6},{5,7},{6,4},{7,5},{8,10},{9,11},{10,... | collective-permute-start | bytes 221192 | tf_op jit(solution)/shard_map/ppermute | solution.py:57
  41.6 4.4 %collective-permute-start.7 = (bf16[2,144,128]{2,1,0:T(8,128)(2,1)S(1)}, bf16[2,144,128]{2,1,0:T(8,128)(2,1)S(1)}, u32[]{:S(2)}, u32[]{:S(2)}) collective-permute-start(bf16[2,144,128]{2,1,0:T(8,128)(2,1)S(1)} %pad_maximum_fusion), channel_id=1, source_target_pairs={{0,4},{1,5},{2,6},{3,7},{4,0},{5,1},{6,2},{7,3},{8,12},{9,13},{10,... | collective-permute-start | bytes 221192 | tf_op jit(solution)/shard_map/ppermute | solution.py:57
  43.4 5.3 %collective-permute-start.8 = (bf16[2,144,128]{2,1,0:T(8,128)(2,1)S(1)}, bf16[2,144,128]{2,1,0:T(8,128)(2,1)S(1)}, u32[]{:S(2)}, u32[]{:S(2)}) collective-permute-start(bf16[2,144,128]{2,1,0:T(8,128)(2,1)S(1)} %pad_maximum_fusion), channel_id=1, source_target_pairs={{0,6},{1,7},{2,4},{3,5},{4,2},{5,3},{6,0},{7,1},{8,14},{9,15},{10,... | collective-permute-start | bytes 221192 | tf_op jit(solution)/shard_map/ppermute | solution.py:57
  48.7 1.6 %collective-permute-start.9 = (bf16[8,144,128]{2,1,0:T(8,128)(2,1)S(1)}, bf16[8,144,128]{2,1,0:T(8,128)(2,1)S(1)}, u32[]{:S(2)}, u32[]{:S(2)}) collective-permute-start(bf16[8,144,128]{2,1,0:T(8,128)(2,1)S(1)} %get-tuple-element.21), channel_id=1, source_target_pairs={{0,1},{1,0},{2,3},{3,2},{4,5},{5,4},{6,7},{7,6},{8,9},{9,8},{10,11... | collective-permute-start | bytes 884744 | tf_op jit(solution)/shard_map/ppermute | solution.py:57

commit v2 on v1

--- a/solution.py
+++ b/solution.py
@@ -16,10 +16,15 @@
 VMEM = pl.BlockSpec(memory_space=pltpu.VMEM)
 SMEM = pl.BlockSpec(memory_space=pltpu.SMEM)
 ANY = pl.BlockSpec(memory_space=pl.ANY)
+HBM = pl.BlockSpec(memory_space=pltpu.HBM)
 
 
 def struct(shape, dtype):
     return jax.ShapeDtypeStruct(shape, dtype)
+
+
+def in_hbm(array):
+    return pltpu.with_memory_space_constraint(array, pltpu.HBM)
 
 
 def params(mebibytes):
@@ -58,12 +63,20 @@
 
 
 def project_kernel(
-    order, chunks, kv_heads, group, head_size, x_ref, weight_hbm, first_ref, count_ref, keep_ref,
-    send_ref, weight, sems
+    order, chunks, kv_heads, group, head_size, x_hbm, weight_hbm, first_hbm, count_hbm, keep_ref,
+    send_ref, weight, x_ref, first_ref, count_ref, sems, small_sems
 ):
     rows, steps, depth = x_ref.shape
     width = weight.shape[1]
     chunk = width // chunks
+    small = [
+        pltpu.make_async_copy(source, target, small_sems.at[i])
+        for i, (source, target) in enumerate(
+            [(x_hbm, x_ref), (first_hbm, first_ref), (count_hbm, count_ref)]
+        )
+    ]
+    for copy in small:
+        copy.start()
     copies = [
         pltpu.make_async_copy(
             weight_hbm.at[:, pl.ds(c * chunk, chunk)], weight.at[:, pl.ds(c * chunk, chunk)], sems.at[c]
@@ -72,6 +85,8 @@
     ]
     for copy in copies:
         copy.start()
+    for copy in small:
+        copy.wait()
     slots = len(order)
     half = slots // 2
     me = lax.axis_index(AXIS)
@@ -109,37 +124,42 @@
                 send_ref[pl.ds(at, half, stride=tile_rows), :] = block[half:]
 
 
-def sum_kernel(inputs, *refs):
-    total = refs[0][...]
-    for ref in refs[1:inputs]:
-        total = total + ref[...]
-    outs = refs[inputs:]
-    size = outs[0].shape[0]
-    for i, out in enumerate(outs):
-        out[...] = total[i * size : (i + 1) * size]
-
-
-def add_and_split(arrays, pieces):
-    rows, lanes = arrays[0].shape
+def fetch_kernel(cache_hbm, after_ref, cache_ref, sems):
+    del after_ref
+    pieces = sems.shape[0]
+    span = cache_hbm.shape[2] // pieces
+    copies = [
+        pltpu.make_async_copy(
+            cache_hbm.at[:, :, pl.ds(i * span, span)], cache_ref.at[:, :, pl.ds(i * span, span)], sems.at[i]
+        )
+        for i in range(pieces)
+    ]
+    for copy in copies:
+        copy.start()
+    for copy in copies:
+        copy.wait()
+
+
+def fetch(cache, after):
     return pl.pallas_call(
-        functools.partial(sum_kernel, len(arrays)),
-        out_shape=[struct((rows // pieces, lanes), F32)] * pieces,
-        in_specs=[VMEM] * len(arrays),
-        out_specs=[VMEM] * pieces,
-        compiler_params=params(16),
-    )(*arrays)
+        fetch_kernel,
+        out_shape=struct(cache.shape, cache.dtype),
+        in_specs=[HBM, ANY],
+        out_specs=VMEM,
+        scratch_shapes=[pltpu.SemaphoreType.DMA((4,))],
+        compiler_params=params(1),
+        cost_estimate=pl.CostEstimate(flops=0, bytes_accessed=2 * cache.size, transcendentals=0),
+    )(in_hbm(cache), after)
 
 
 def attend_kernel(
-    partials, kv_heads, group, steps, *refs
+    kv_heads, group, steps, query_ref, gain_ref, cache_ref, first_ref, count_ref, mask_ref, out_ref
 ):
-    parts = refs[:partials]
-    gain_ref, cache_ref, first_ref, count_ref, mask_ref, out_ref = refs[partials:]
     head_size = gain_ref.shape[-1]
     kv_width = kv_heads * head_size
-    query = parts[0][...]
-    for part in parts[1:]:
-        query = query + part[...]
+    join = 2 if kv_heads % 2 == 0 else 1
+    span = join * head_size
+    query = query_ref[...]
     mean = jnp.mean(query * query, axis=1, keepdims=True)
     normed = (query * lax.rsqrt(mean + EPSILON) * gain_ref[...]).astype(BF16)
     me = lax.axis_index(AXIS)
@@ -157,22 +177,41 @@
     lane = lax.broadcasted_iota(jnp.int32, (size, head_size), 1)
     stats = jnp.zeros((size, head_size), F32)
     scale = 1.0 / math.sqrt(head_size)
-    for h in range(kv_heads):
-        keys = cache_ref[0, :, h * head_size : (h + 1) * head_size]
-        values = cache_ref[0, :, kv_width + h * head_size : kv_width + (h + 1) * head_size]
+    blank = jnp.zeros((size, head_size), BF16)
+    for base in range(0, kv_heads, join):
+        at = base * head_size
+        keys = cache_ref[0, :, at : at + span]
+        left = jnp.concatenate(
+            [
+                jnp.concatenate(
+                    [
+                        normed[(base + i) * size : (base + i + 1) * size] if i == j else blank
+                        for j in range(join)
+                    ],
+                    axis=1,
+                )
+                for i in range(join)
+            ],
+            axis=0,
+        )
         scores = lax.dot_general(
-            normed[h * size : (h + 1) * size],
-            keys,
-            (((1,), (1,)), ((), ())),
-            preferred_element_type=F32,
+            left, keys, (((1,), (1,)), ((), ())), preferred_element_type=F32
         ) * scale
         top = jnp.max(scores, axis=1, keepdims=True)
         weights = jnp.exp(scores - top).astype(BF16)
         total = jnp.sum(weights.astype(F32), axis=1, keepdims=True)
-        mixed = jnp.dot(weights, values, preferred_element_type=F32)
-        out_ref[h * size : (h + 1) * size, :] = (mixed / total).astype(BF16)
-        here = lane % kv_heads == h
-        stats = jnp.where(here, jnp.where(lane < 3 * kv_heads, top, total), stats)
+        values = cache_ref[0, :, kv_width + at : kv_width + at + span]
+        mixed = jnp.dot(weights, values, preferred_element_type=F32) / total
+        for i in range(join):
+            h = base + i
+            rows_here = slice(i * size, (i + 1) * size)
+            out_ref[h * size : (h + 1) * size, :] = mixed[
+                rows_here, i * head_size : (i + 1) * head_size
+            ].astype(BF16)
+            here = lane % kv_heads == h
+            stats = jnp.where(
+                here, jnp.where(lane < 3 * kv_heads, top[rows_here], total[rows_here]), stats
+            )
     live = jnp.zeros((size, head_size), jnp.bool_)
     for s in range(steps):
         alive = (tile == 0) | (mask_ref[owner, s, tile] == 1)
@@ -281,26 +320,37 @@
     keep, send = pl.pallas_call(
         functools.partial(project_kernel, order, chunks, kv_heads, group, head_size),
         out_shape=[struct((half * tile_rows, head_size), F32)] * 2,
-        in_specs=[VMEM, ANY, SMEM, SMEM],
+        in_specs=[HBM] * 4,
         out_specs=[VMEM, VMEM],
-        scratch_shapes=[pltpu.VMEM((depth, width), BF16), pltpu.SemaphoreType.DMA((chunks,))],
-        compiler_params=params(40),
-    )(normed_input, query_weight, image_first_slot, tile_count)
-    parts = [keep, exchange(send, 1, devices)]
+        scratch_shapes=[
+            pltpu.VMEM((depth, width), BF16),
+            pltpu.VMEM(normed_input.shape, BF16),
+            pltpu.SMEM(image_first_slot.shape, jnp.int32),
+            pltpu.SMEM(tile_count.shape, jnp.int32),
+            pltpu.SemaphoreType.DMA((chunks,)),
+            pltpu.SemaphoreType.DMA((3,)),
+        ],
+        compiler_params=params(12),
+    )(*[in_hbm(x) for x in (normed_input, query_weight, image_first_slot, tile_count)])
+    total = keep + exchange(send, 1, devices)
+    cache = None
     for group_bits in stages[1:]:
         steps_out = offsets(group_bits)
-        pieces = add_and_split(parts, len(steps_out))
-        parts = [pieces[0]] + [
-            exchange(piece, step, devices) for piece, step in zip(pieces[1:], steps_out[1:])
-        ]
+        size = total.shape[0] // len(steps_out)
+        pieces = [total[i * size : (i + 1) * size] for i in range(len(steps_out))]
+        sent = [piece.astype(jnp.float16) for piece in pieces[1:]]
+        got = [exchange(piece, step, devices) for piece, step in zip(sent, steps_out[1:])]
+        if cache is None:
+            cache = fetch(image_cache, pieces[0])
+        total = functools.reduce(jnp.add, [pieces[0]] + [piece.astype(F32) for piece in got])
     block = (kv_heads + 1) * steps * group
     tile = pl.pallas_call(
-        functools.partial(attend_kernel, len(parts), kv_heads, group, steps),
+        functools.partial(attend_kernel, kv_heads, group, steps),
         out_shape=struct((block, head_size), BF16),
-        in_specs=[VMEM] * (len(parts) + 2) + [SMEM] * 3,
+        in_specs=[VMEM] * 3 + [SMEM] * 3,
         out_specs=VMEM,
-        compiler_params=params(16),
-    )(*parts, query_gain, image_cache, image_first_slot, tile_count, cross_tile_mask)
+        compiler_params=params(6),
+    )(total, query_gain, cache, image_first_slot, tile_count, cross_tile_mask)
     gathered = tile[None]
     for group_bits in reversed(stages):
         gathered = jnp.concatenate(
@@ -315,7 +365,7 @@
             pltpu.VMEM((2, devices * steps * group, head_size), F32),
             pltpu.VMEM((heads * rows * steps, head_size), F32),
         ],
-        compiler_params=params(24),
+        compiler_params=params(8),
     )(output_gate, image_first_slot, tile_count, gathered, output_weight)
 
 

time: 54.7 us -> 44 us (0.80)
  local copies, waits for them, and re-layouts: 8.59 us -> 0.32 us
  waiting for transfers between devices: 18.3 us -> 14.2 us
  Pallas kernels: 12.6 us -> 15.5 us
  starting transfers between devices: 14.3 us -> 12.9 us
    unnamed x25 -> x17, local copies, waits for them, and re-layouts: 8.52 us -> 0.2 us
    ppermute x10, waiting for transfers between devices: 18.3 us -> 14.2 us  [exchange(): lax.ppermute(array, AXIS, [(i, i ^ difference) for i in range(count)])]
    pallas_call x3 -> x2, Pallas kernels: 4.07 us -> 6.26 us  [the longest x1 3.14 us: fetch(): pl.pallas_call(fetch_kernel, out_shape=struct(cache.shape, cache.dtype),...]
    ppermute x10, starting transfers between devices: 14.3 us -> 12.9 us  [exchange(): lax.ppermute(array, AXIS, [(i, i ^ difference) for i in range(count)])]
    pallas_call x1, Pallas kernels: 4.45 us -> 5.16 us  [body(): pl.pallas_call(functools.partial(project_kernel, order, chunks, kv_heads,...]
  transfers between devices with their start and end apart: 10 -> 10, of which waited for: 10 -> 9; matrix products, arithmetic and copies ran while one was open for 0% -> 0% of each run, Pallas kernels for 0% -> 7%
where the time goes in v2:
time: 44 us; the launch traced here: 43.9 us
  Pallas kernels  15.5 us (35%)
  waiting for transfers between devices  14.2 us (32%)
  starting transfers between devices  12.9 us (29%)
  between operations  0.81 us (2%)
    ppermute x10, waiting for transfers between devices, exchange(): lax.ppermute(array, AXIS, [(i, i ^ difference) for i in range(count)])  14.2 us
    ppermute x10, starting transfers between devices, exchange(): lax.ppermute(array, AXIS, [(i, i ^ difference) for i in range(count)])  12.9 us
    pallas_call x1, Pallas kernels, body(): pl.pallas_call(functools.partial(project_kernel, order, chunks, kv_heads,...  5.16 us
    pallas_call x1, Pallas kernels, body(): pl.pallas_call(functools.partial(finish_kernel, order, kv_heads, group, s...  4.1 us
    pallas_call x1, Pallas kernels, fetch(): pl.pallas_call(fetch_kernel, out_shape=struct(cache.shape, cache.dtype),...  3.14 us
    pallas_call x1, Pallas kernels, body(): pl.pallas_call(functools.partial(attend_kernel, kv_heads, group, steps),...  3.12 us
  transfers between devices with their start and end apart: 10, of which 9 were waited for; matrix products, arithmetic and copies ran while one was open for 0% of the time, Pallas kernels for 7%

profile of v2, /device:TPU:0, one launch (start us, length us, event | category | flops | bytes accessed | tf_op | source)
XLA Modules:
  0.0 43.9 jit_solution(12477564462767003890)
XLA Ops:
  0.0 5.2 %shard_map.91 = (f32[1024,128]{1,0:T(8,128)S(1)}, f32[1024,128]{1,0:T(8,128)S(1)}) custom-call(bf16[8,2,512]{2,1,0:T(2,128)(2,1)} %x_hbm.1, bf16[512,8192]{1,0:T(8,128)(2,1)} %weight_hbm.1, s32[8]{0:T(128)} %first_ref.3, s32[8]{0:T(128)} %count_ref.3), custom_call_target="tpu_custom_call" | custom-call | tf_op jit(solution)/shard_map/pallas_call | solution.py:320
  5.2 0.0 copy-start
  5.2 0.0 copy-start.1
  5.2 0.0 copy-start.2
  5.2 0.5 %collective-permute-start = (f32[1024,128]{1,0:T(8,128)S(1)}, f32[1024,128]{1,0:T(8,128)S(1)}, u32[]{:S(2)}, u32[]{:S(2)}) collective-permute-start(f32[1024,128]{1,0:T(8,128)S(1)} %get-tuple-element.8), channel_id=1, source_target_pairs={{0,1},{1,0},{2,3},{3,2},{4,5},{5,4},{6,7},{7,6},{8,9},{9,8},{10,11... | collective-permute-start | bytes 1572872 | tf_op jit(solution)/shard_map/ppermute | solution.py:62
  5.7 1.5 %collective-permute-done = f32[1024,128]{1,0:T(8,128)S(1)} collective-permute-done((f32[1024,128]{1,0:T(8,128)S(1)}, f32[1024,128]{1,0:T(8,128)S(1)}, u32[]{:S(2)}, u32[]{:S(2)}) %collective-permute-start) | collective-permute-done | bytes 524320 | tf_op jit(solution)/shard_map/ppermute | solution.py:62
  7.3 0.1 fusion
  7.4 2.9 %collective-permute-start.1 = (f16[256,128]{1,0:T(8,128)(2,1)S(1)}, f16[256,128]{1,0:T(8,128)(2,1)S(1)}, u32[]{:S(2)}, u32[]{:S(2)}) collective-permute-start(f16[256,128]{1,0:T(8,128)(2,1)S(1)} %get-tuple-element.13), channel_id=1, source_target_pairs={{0,2},{1,3},{2,0},{3,1},{4,6},{5,7},{6,4},{7,5},{8,10},{9,11},{10,... | collective-permute-start | bytes 196616 | tf_op jit(solution)/shard_map/ppermute | solution.py:62
  10.3 1.6 %collective-permute-start.2 = (f16[256,128]{1,0:T(8,128)(2,1)S(1)}, f16[256,128]{1,0:T(8,128)(2,1)S(1)}, u32[]{:S(2)}, u32[]{:S(2)}) collective-permute-start(f16[256,128]{1,0:T(8,128)(2,1)S(1)} %get-tuple-element.15), channel_id=1, source_target_pairs={{0,4},{1,5},{2,6},{3,7},{4,0},{5,1},{6,2},{7,3},{8,12},{9,13},{10,... | collective-permute-start | bytes 196616 | tf_op jit(solution)/shard_map/ppermute | solution.py:62
  11.9 0.0 collective-permute-start.3
  11.9 0.8 %collective-permute-done.1 = f16[256,128]{1,0:T(8,128)(2,1)S(1)} collective-permute-done((f16[256,128]{1,0:T(8,128)(2,1)S(1)}, f16[256,128]{1,0:T(8,128)(2,1)S(1)}, u32[]{:S(2)}, u32[]{:S(2)}) %collective-permute-start.1) | collective-permute-done | bytes 65568 | tf_op jit(solution)/shard_map/ppermute | solution.py:62
  12.7 2.4 %collective-permute-done.2 = f16[256,128]{1,0:T(8,128)(2,1)S(1)} collective-permute-done((f16[256,128]{1,0:T(8,128)(2,1)S(1)}, f16[256,128]{1,0:T(8,128)(2,1)S(1)}, u32[]{:S(2)}, u32[]{:S(2)}) %collective-permute-start.2) | collective-permute-done | bytes 65568 | tf_op jit(solution)/shard_map/ppermute | solution.py:62
  15.1 1.9 %collective-permute-done.3 = f16[256,128]{1,0:T(8,128)(2,1)S(1)} collective-permute-done((f16[256,128]{1,0:T(8,128)(2,1)S(1)}, f16[256,128]{1,0:T(8,128)(2,1)S(1)}, u32[]{:S(2)}, u32[]{:S(2)}) %collective-permute-start.3) | collective-permute-done | bytes 65568 | tf_op jit(solution)/shard_map/ppermute | solution.py:62
  17.1 2.7 %collective-permute-start.4 = (f16[128,128]{1,0:T(8,128)(2,1)S(1)}, f16[128,128]{1,0:T(8,128)(2,1)S(1)}, u32[]{:S(2)}, u32[]{:S(2)}) collective-permute-start(f16[128,128]{1,0:T(8,128)(2,1)S(1)} %slice_convert_fusion), channel_id=1, source_target_pairs={{0,8},{1,9},{2,10},{3,11},{4,12},{5,13},{6,14},{7,15},{8,0},{9,1},... | collective-permute-start | bytes 98312 | tf_op jit(solution)/shard_map/ppermute | solution.py:62
  19.8 0.0 copy-done.3
  19.8 0.1 copy.10.mask_ref
  19.9 3.1 %shard_map.92.cache_ref = bf16[1,1601,2048]{2,1,0:T(8,128)(2,1)S(1)} custom-call(bf16[1,1601,2048]{2,1,0:T(8,128)(2,1)} %cache_hbm.1, f32[256,128]{1,0:T(8,128)S(1)} %get-tuple-element.11.after_ref), custom_call_target="tpu_custom_call" | custom-call | bytes 6557696 | tf_op jit(solution)/shard_map/pallas_call | solution.py:144
  23.0 0.0 collective-permute-done.4
  23.0 0.0 copy-done
  23.1 0.0 copy-done.1
  23.1 3.1 %shard_map.93 = bf16[144,128]{1,0:T(8,128)(2,1)S(1)} custom-call(f32[128,128]{1,0:T(8,128)S(1)} %slice_add_fusion.query_ref, f32[128]{0:T(128)S(1)} %copy-done.2, bf16[1,1601,2048]{2,1,0:T(8,128)(2,1)S(1)} %shard_map.92.cache_ref, s32[8]{0:T(128)S(1)} %copy-done, s32[8]{0:T(128)S(1)} %copy-done.1, s32[8,2,4]{2,1,0:T(2,128)S(1)} %copy.10.mask_ref), custom_call_target="tpu_custom_call" | custom-call | tf_op jit(solution)/shard_map/pallas_call | solution.py:347
  26.2 1.6 %collective-permute-start.5 = (bf16[1,144,128]{2,1,0:T(8,128)(2,1)S(1)}, bf16[1,144,128]{2,1,0:T(8,128)(2,1)S(1)}, u32[]{:S(2)}, u32[]{:S(2)}) collective-permute-start(bf16[1,144,128]{2,1,0:T(8,128)(2,1)S(1)} %bitcast.5), channel_id=1, source_target_pairs={{0,8},{1,9},{2,10},{3,11},{4,12},{5,13},{6,14},{7,15},{8,0},{9,1},... | collective-permute-start | bytes 110600 | tf_op jit(solution)/shard_map/ppermute | solution.py:62
  27.8 3.6 %collective-permute-done.5 = bf16[1,144,128]{2,1,0:T(8,128)(2,1)S(1)} collective-permute-done((bf16[1,144,128]{2,1,0:T(8,128)(2,1)S(1)}, bf16[1,144,128]{2,1,0:T(8,128)(2,1)S(1)}, u32[]{:S(2)}, u32[]{:S(2)}) %collective-permute-start.5) | collective-permute-done | bytes 36896 | tf_op jit(solution)/shard_map/ppermute | solution.py:62
  31.4 0.3 collective-permute-start.6
  31.7 1.0 %collective-permute-start.7 = (bf16[2,144,128]{2,1,0:T(8,128)(2,1)S(1)}, bf16[2,144,128]{2,1,0:T(8,128)(2,1)S(1)}, u32[]{:S(2)}, u32[]{:S(2)}) collective-permute-start(bf16[2,144,128]{2,1,0:T(8,128)(2,1)S(1)} %pad_maximum_fusion), channel_id=1, source_target_pairs={{0,4},{1,5},{2,6},{3,7},{4,0},{5,1},{6,2},{7,3},{8,12},{9,13},{10,... | collective-permute-start | bytes 221192 | tf_op jit(solution)/shard_map/ppermute | solution.py:62
  32.7 2.2 %collective-permute-start.8 = (bf16[2,144,128]{2,1,0:T(8,128)(2,1)S(1)}, bf16[2,144,128]{2,1,0:T(8,128)(2,1)S(1)}, u32[]{:S(2)}, u32[]{:S(2)}) collective-permute-start(bf16[2,144,128]{2,1,0:T(8,128)(2,1)S(1)} %pad_maximum_fusion), channel_id=1, source_target_pairs={{0,6},{1,7},{2,4},{3,5},{4,2},{5,3},{6,0},{7,1},{8,14},{9,15},{10,... | collective-permute-start | bytes 221192 | tf_op jit(solution)/shard_map/ppermute | solution.py:62
  34.9 0.8 %collective-permute-done.6 = bf16[2,144,128]{2,1,0:T(8,128)(2,1)S(1)} collective-permute-done((bf16[2,144,128]{2,1,0:T(8,128)(2,1)S(1)}, bf16[2,144,128]{2,1,0:T(8,128)(2,1)S(1)}, u32[]{:S(2)}, u32[]{:S(2)}) %collective-permute-start.6) | collective-permute-done | bytes 73760 | tf_op jit(solution)/shard_map/ppermute | solution.py:62
  35.8 0.2 collective-permute-done.7
  36.1 2.0 %collective-permute-done.8 = bf16[2,144,128]{2,1,0:T(8,128)(2,1)S(1)} collective-permute-done((bf16[2,144,128]{2,1,0:T(8,128)(2,1)S(1)}, bf16[2,144,128]{2,1,0:T(8,128)(2,1)S(1)}, u32[]{:S(2)}, u32[]{:S(2)}) %collective-permute-start.8) | collective-permute-done | bytes 73760 | tf_op jit(solution)/shard_map/ppermute | solution.py:62
  38.1 0.1 collective-permute-start.9
  38.8 0.9 %collective-permute-done.9 = bf16[8,144,128]{2,1,0:T(8,128)(2,1)S(1)} collective-permute-done((bf16[8,144,128]{2,1,0:T(8,128)(2,1)S(1)}, bf16[8,144,128]{2,1,0:T(8,128)(2,1)S(1)}, u32[]{:S(2)}, u32[]{:S(2)}) %collective-permute-start.9) | collective-permute-done | bytes 294944 | tf_op jit(solution)/shard_map/ppermute | solution.py:62
  39.8 4.1 %shard_map.94 = bf16[8,2,512]{2,1,0:T(2,128)(2,1)} custom-call(f32[1]{0:T(128)S(6)} %copy.20.gate_ref, s32[8]{0:T(128)S(1)} %copy-done, s32[8]{0:T(128)S(1)} %copy-done.1, bf16[16,144,128]{2,1,0:T(8,128)(2,1)S(1)} %constant_dynamic-update-slice_fusion.5.tiles_ref, bf16[8192,512]{1,0:T(8,128)(2,1)S(1)} %bitcast.4), custom_call_target="tpu_custom_call" | custom-call | tf_op jit(solution)/shard_map/pallas_call | solution.py:359
  (18 shorter events, 0.3 us)
Async XLA Ops:
  0.0 19.8 %copy-start.3 = (s32[8,2,4]{0,2,1:T(4,128)S(1)}, s32[8,2,4]{0,2,1:T(4,128)}, u32[]{:S(2)}) copy-start(s32[8,2,4]{0,2,1:T(4,128)} %param.15) | copy-start | bytes 772
  5.2 17.9 %copy-start = (s32[8]{0:T(128)S(1)}, s32[8]{0:T(128)}, u32[]{:S(2)}) copy-start(s32[8]{0:T(128)} %first_ref.3) | copy-start | bytes 100
  5.2 17.9 %copy-start.1 = (s32[8]{0:T(128)S(1)}, s32[8]{0:T(128)}, u32[]{:S(2)}) copy-start(s32[8]{0:T(128)} %count_ref.3) | copy-start | bytes 100
  5.2 17.9 %copy-start.2 = (f32[128]{0:T(128)S(1)}, f32[128]{0:T(128)}, u32[]{:S(2)}) copy-start(f32[128]{0:T(128)} %gain_ref.1) | copy-start | bytes 1540
  5.2 2.1 %collective-permute-start = (f32[1024,128]{1,0:T(8,128)S(1)}, f32[1024,128]{1,0:T(8,128)S(1)}, u32[]{:S(2)}, u32[]{:S(2)}) collective-permute-start(f32[1024,128]{1,0:T(8,128)S(1)} %get-tuple-element.8), channel_id=1, source_target_pairs={{0,1},{1,0},{2,3},{3,2},{4,5},{5,4},{6,7},{7,6},{8,9},{9,8},{10,11... | collective-permute-start | bytes 1572872 | tf_op jit(solution)/shard_map/ppermute | solution.py:62
  7.4 5.3 %collective-permute-start.1 = (f16[256,128]{1,0:T(8,128)(2,1)S(1)}, f16[256,128]{1,0:T(8,128)(2,1)S(1)}, u32[]{:S(2)}, u32[]{:S(2)}) collective-permute-start(f16[256,128]{1,0:T(8,128)(2,1)S(1)} %get-tuple-element.13), channel_id=1, source_target_pairs={{0,2},{1,3},{2,0},{3,1},{4,6},{5,7},{6,4},{7,5},{8,10},{9,11},{10,... | collective-permute-start | bytes 196616 | tf_op jit(solution)/shard_map/ppermute | solution.py:62
  10.3 4.8 %collective-permute-start.2 = (f16[256,128]{1,0:T(8,128)(2,1)S(1)}, f16[256,128]{1,0:T(8,128)(2,1)S(1)}, u32[]{:S(2)}, u32[]{:S(2)}) collective-permute-start(f16[256,128]{1,0:T(8,128)(2,1)S(1)} %get-tuple-element.15), channel_id=1, source_target_pairs={{0,4},{1,5},{2,6},{3,7},{4,0},{5,1},{6,2},{7,3},{8,12},{9,13},{10,... | collective-permute-start | bytes 196616 | tf_op jit(solution)/shard_map/ppermute | solution.py:62
  11.9 5.2 %collective-permute-start.3 = (f16[256,128]{1,0:T(8,128)(2,1)S(1)}, f16[256,128]{1,0:T(8,128)(2,1)S(1)}, u32[]{:S(2)}, u32[]{:S(2)}) collective-permute-start(f16[256,128]{1,0:T(8,128)(2,1)S(1)} %get-tuple-element.14), channel_id=1, source_target_pairs={{0,6},{1,7},{2,4},{3,5},{4,2},{5,3},{6,0},{7,1},{8,14},{9,15},{10,... | collective-permute-start | bytes 196616 | tf_op jit(solution)/shard_map/ppermute | solution.py:62
  17.1 5.9 %collective-permute-start.4 = (f16[128,128]{1,0:T(8,128)(2,1)S(1)}, f16[128,128]{1,0:T(8,128)(2,1)S(1)}, u32[]{:S(2)}, u32[]{:S(2)}) collective-permute-start(f16[128,128]{1,0:T(8,128)(2,1)S(1)} %slice_convert_fusion), channel_id=1, source_target_pairs={{0,8},{1,9},{2,10},{3,11},{4,12},{5,13},{6,14},{7,15},{8,0},{9,1},... | collective-permute-start | bytes 98312 | tf_op jit(solution)/shard_map/ppermute | solution.py:62
  19.9 19.9 %slice-start = ((s8[8388608]{0:T(1024)(128)(4,1)}), s8[4194304]{0:T(1024)(128)(4,1)S(1)}, s32[]{:S(2)}) async-start(s8[8388608]{0:T(1024)(128)(4,1)} %bitcast.3), calls=%async_computation | async-start | bytes 8388608
  19.9 19.9 %slice-start.1 = ((s8[8388608]{0:T(1024)(128)(4,1)}), s8[4194304]{0:T(1024)(128)(4,1)S(1)}, s32[]{:S(2)}) async-start(s8[8388608]{0:T(1024)(128)(4,1)} %bitcast.3), calls=%async_computation.1 | async-start | bytes 8388608
  26.2 5.2 %collective-permute-start.5 = (bf16[1,144,128]{2,1,0:T(8,128)(2,1)S(1)}, bf16[1,144,128]{2,1,0:T(8,128)(2,1)S(1)}, u32[]{:S(2)}, u32[]{:S(2)}) collective-permute-start(bf16[1,144,128]{2,1,0:T(8,128)(2,1)S(1)} %bitcast.5), channel_id=1, source_target_pairs={{0,8},{1,9},{2,10},{3,11},{4,12},{5,13},{6,14},{7,15},{8,0},{9,1},... | collective-permute-start | bytes 110600 | tf_op jit(solution)/shard_map/ppermute | solution.py:62
  31.4 4.4 %collective-permute-start.6 = (bf16[2,144,128]{2,1,0:T(8,128)(2,1)S(1)}, bf16[2,144,128]{2,1,0:T(8,128)(2,1)S(1)}, u32[]{:S(2)}, u32[]{:S(2)}) collective-permute-start(bf16[2,144,128]{2,1,0:T(8,128)(2,1)S(1)} %pad_maximum_fusion), channel_id=1, source_target_pairs={{0,2},{1,3},{2,0},{3,1},{4,6},{5,7},{6,4},{7,5},{8,10},{9,11},{10,... | collective-permute-start | bytes 221192 | tf_op jit(solution)/shard_map/ppermute | solution.py:62
  31.7 4.4 %collective-permute-start.7 = (bf16[2,144,128]{2,1,0:T(8,128)(2,1)S(1)}, bf16[2,144,128]{2,1,0:T(8,128)(2,1)S(1)}, u32[]{:S(2)}, u32[]{:S(2)}) collective-permute-start(bf16[2,144,128]{2,1,0:T(8,128)(2,1)S(1)} %pad_maximum_fusion), channel_id=1, source_target_pairs={{0,4},{1,5},{2,6},{3,7},{4,0},{5,1},{6,2},{7,3},{8,12},{9,13},{10,... | collective-permute-start | bytes 221192 | tf_op jit(solution)/shard_map/ppermute | solution.py:62
  32.7 5.3 %collective-permute-start.8 = (bf16[2,144,128]{2,1,0:T(8,128)(2,1)S(1)}, bf16[2,144,128]{2,1,0:T(8,128)(2,1)S(1)}, u32[]{:S(2)}, u32[]{:S(2)}) collective-permute-start(bf16[2,144,128]{2,1,0:T(8,128)(2,1)S(1)} %pad_maximum_fusion), channel_id=1, source_target_pairs={{0,6},{1,7},{2,4},{3,5},{4,2},{5,3},{6,0},{7,1},{8,14},{9,15},{10,... | collective-permute-start | bytes 221192 | tf_op jit(solution)/shard_map/ppermute | solution.py:62
  38.1 1.6 %collective-permute-start.9 = (bf16[8,144,128]{2,1,0:T(8,128)(2,1)S(1)}, bf16[8,144,128]{2,1,0:T(8,128)(2,1)S(1)}, u32[]{:S(2)}, u32[]{:S(2)}) collective-permute-start(bf16[8,144,128]{2,1,0:T(8,128)(2,1)S(1)} %get-tuple-element.16), channel_id=1, source_target_pairs={{0,1},{1,0},{2,3},{3,2},{4,5},{5,4},{6,7},{7,6},{8,9},{9,8},{10,11... | collective-permute-start | bytes 884744 | tf_op jit(solution)/shard_map/ppermute | solution.py:62

commit v3 on v2

--- a/solution.py
+++ b/solution.py
@@ -39,7 +39,7 @@
 
 def offsets(group):
     result = [0]
-    for bit in group:
+    for bit in reversed(group):
         result = result + [other | (1 << bit) for other in result]
     return result
 
@@ -124,13 +124,15 @@
                 send_ref[pl.ds(at, half, stride=tile_rows), :] = block[half:]
 
 
-def fetch_kernel(cache_hbm, after_ref, cache_ref, sems):
-    del after_ref
+def fetch_kernel(part, cache_hbm, before_ref, cache_ref, after_ref, sems):
+    del before_ref, after_ref
     pieces = sems.shape[0]
-    span = cache_hbm.shape[2] // pieces
+    span = cache_ref.shape[2] // pieces
     copies = [
         pltpu.make_async_copy(
-            cache_hbm.at[:, :, pl.ds(i * span, span)], cache_ref.at[:, :, pl.ds(i * span, span)], sems.at[i]
+            cache_hbm.at[:, :, pl.ds((part * pieces + i) * span, span)],
+            cache_ref.at[:, :, pl.ds(i * span, span)],
+            sems.at[i],
         )
         for i in range(pieces)
     ]
@@ -140,20 +142,24 @@
         copy.wait()
 
 
-def fetch(cache, after):
+def fetch(cache, part, held):
     return pl.pallas_call(
-        fetch_kernel,
-        out_shape=struct(cache.shape, cache.dtype),
+        functools.partial(fetch_kernel, part),
+        out_shape=[
+            struct((*cache.shape[:2], cache.shape[2] // 2), cache.dtype),
+            struct(held.shape, held.dtype),
+        ],
         in_specs=[HBM, ANY],
-        out_specs=VMEM,
+        out_specs=[VMEM, ANY],
         scratch_shapes=[pltpu.SemaphoreType.DMA((4,))],
+        input_output_aliases={1: 1},
         compiler_params=params(1),
-        cost_estimate=pl.CostEstimate(flops=0, bytes_accessed=2 * cache.size, transcendentals=0),
-    )(in_hbm(cache), after)
+        cost_estimate=pl.CostEstimate(flops=0, bytes_accessed=cache.size, transcendentals=0),
+    )(in_hbm(cache), held)
 
 
 def attend_kernel(
-    kv_heads, group, steps, query_ref, gain_ref, cache_ref, first_ref, count_ref, mask_ref, out_ref
+    kv_heads, group, steps, query_ref, gain_ref, keys_ref, values_ref, first_ref, count_ref, mask_ref, out_ref
 ):
     head_size = gain_ref.shape[-1]
     kv_width = kv_heads * head_size
@@ -180,7 +186,7 @@
     blank = jnp.zeros((size, head_size), BF16)
     for base in range(0, kv_heads, join):
         at = base * head_size
-        keys = cache_ref[0, :, at : at + span]
+        keys = keys_ref[0, :, at : at + span]
         left = jnp.concatenate(
             [
                 jnp.concatenate(
@@ -200,7 +206,7 @@
         top = jnp.max(scores, axis=1, keepdims=True)
         weights = jnp.exp(scores - top).astype(BF16)
         total = jnp.sum(weights.astype(F32), axis=1, keepdims=True)
-        values = cache_ref[0, :, kv_width + at : kv_width + at + span]
+        values = values_ref[0, :, at : at + span]
         mixed = jnp.dot(weights, values, preferred_element_type=F32) / total
         for i in range(join):
             h = base + i
@@ -316,7 +322,7 @@
     stages = scatter_stages(devices.bit_length() - 1)
     order = positions(stages)
     half = devices // 2
-    chunks = 8
+    chunks = 4
     keep, send = pl.pallas_call(
         functools.partial(project_kernel, order, chunks, kv_heads, group, head_size),
         out_shape=[struct((half * tile_rows, head_size), F32)] * 2,
@@ -333,24 +339,25 @@
         compiler_params=params(12),
     )(*[in_hbm(x) for x in (normed_input, query_weight, image_first_slot, tile_count)])
     total = keep + exchange(send, 1, devices)
-    cache = None
+    cache = []
     for group_bits in stages[1:]:
         steps_out = offsets(group_bits)
         size = total.shape[0] // len(steps_out)
         pieces = [total[i * size : (i + 1) * size] for i in range(len(steps_out))]
         sent = [piece.astype(jnp.float16) for piece in pieces[1:]]
         got = [exchange(piece, step, devices) for piece, step in zip(sent, steps_out[1:])]
-        if cache is None:
-            cache = fetch(image_cache, pieces[0])
+        if len(cache) < 2:
+            half, pieces[0] = fetch(image_cache, len(cache), pieces[0])
+            cache.append(half)
         total = functools.reduce(jnp.add, [pieces[0]] + [piece.astype(F32) for piece in got])
     block = (kv_heads + 1) * steps * group
     tile = pl.pallas_call(
         functools.partial(attend_kernel, kv_heads, group, steps),
         out_shape=struct((block, head_size), BF16),
-        in_specs=[VMEM] * 3 + [SMEM] * 3,
+        in_specs=[VMEM] * 4 + [SMEM] * 3,
         out_specs=VMEM,
         compiler_params=params(6),
-    )(total, query_gain, cache, image_first_slot, tile_count, cross_tile_mask)
+    )(total, query_gain, *cache, image_first_slot, tile_count, cross_tile_mask)
     gathered = tile[None]
     for group_bits in reversed(stages):
         gathered = jnp.concatenate(

time: 44 us -> 41.3 us (0.939)
  waiting for transfers between devices: 14.2 us -> 10.7 us
  starting transfers between devices: 12.9 us -> 13.7 us
    ppermute x10, waiting for transfers between devices: 14.2 us -> 10.7 us  [exchange(): lax.ppermute(array, AXIS, [(i, i ^ difference) for i in range(count)])]
    pallas_call x1, Pallas kernels: 5.16 us -> 4.09 us  [body(): pl.pallas_call(functools.partial(project_kernel, order, chunks, kv_heads,...]
    pallas_call x1 -> x2, Pallas kernels: 3.14 us -> 4.09 us  [fetch(): pl.pallas_call(functools.partial(fetch_kernel, part), out_shape=[struct((...]
    ppermute x10, starting transfers between devices: 12.9 us -> 13.7 us  [exchange(): lax.ppermute(array, AXIS, [(i, i ^ difference) for i in range(count)])]
  transfers between devices with their start and end apart: 10 -> 10, of which waited for: 9 -> 9; matrix products, arithmetic and copies ran while one was open for 0% -> 0% of each run, Pallas kernels for 7% -> 10%
where the time goes in v3:
time: 41.3 us; the launch traced here: 41.1 us
  Pallas kernels  15.4 us (37%)
  starting transfers between devices  13.7 us (33%)
  waiting for transfers between devices  10.7 us (26%)
  between operations  0.83 us (2%)
    ppermute x10, starting transfers between devices, exchange(): lax.ppermute(array, AXIS, [(i, i ^ difference) for i in range(count)])  13.7 us
    ppermute x10, waiting for transfers between devices, exchange(): lax.ppermute(array, AXIS, [(i, i ^ difference) for i in range(count)])  10.7 us
    pallas_call x1, Pallas kernels, body(): pl.pallas_call(functools.partial(finish_kernel, order, kv_heads, group, s...  4.1 us
    pallas_call x2, Pallas kernels, fetch(): pl.pallas_call(functools.partial(fetch_kernel, part), out_shape=[struct((...  4.09 us
    pallas_call x1, Pallas kernels, body(): pl.pallas_call(functools.partial(project_kernel, order, chunks, kv_heads,...  4.09 us
    pallas_call x1, Pallas kernels, body(): pl.pallas_call(functools.partial(attend_kernel, kv_heads, group, steps),...  3.12 us
  transfers between devices with their start and end apart: 10, of which 9 were waited for; matrix products, arithmetic and copies ran while one was open for 0% of the time, Pallas kernels for 10%

profile of v3, /device:TPU:0, one launch (start us, length us, event | category | flops | bytes accessed | tf_op | source)
XLA Modules:
  0.0 41.1 jit_solution(11813711111034689453)
XLA Ops:
  0.0 4.1 %shard_map.91 = (f32[1024,128]{1,0:T(8,128)S(1)}, f32[1024,128]{1,0:T(8,128)S(1)}) custom-call(bf16[8,2,512]{2,1,0:T(2,128)(2,1)} %x_hbm.1, bf16[512,8192]{1,0:T(8,128)(2,1)} %weight_hbm.1, s32[8]{0:T(128)} %first_ref.3, s32[8]{0:T(128)} %count_ref.3), custom_call_target="tpu_custom_call" | custom-call | tf_op jit(solution)/shard_map/pallas_call | solution.py:326
  4.1 0.0 copy-start.3
  4.1 0.5 %collective-permute-start = (f32[1024,128]{1,0:T(8,128)S(1)}, f32[1024,128]{1,0:T(8,128)S(1)}, u32[]{:S(2)}, u32[]{:S(2)}) collective-permute-start(f32[1024,128]{1,0:T(8,128)S(1)} %get-tuple-element.12), channel_id=1, source_target_pairs={{0,1},{1,0},{2,3},{3,2},{4,5},{5,4},{6,7},{7,6},{8,9},{9,8},{10,11... | collective-permute-start | bytes 1572872 | tf_op jit(solution)/shard_map/ppermute | solution.py:62
  4.6 1.5 %collective-permute-done = f32[1024,128]{1,0:T(8,128)S(1)} collective-permute-done((f32[1024,128]{1,0:T(8,128)S(1)}, f32[1024,128]{1,0:T(8,128)S(1)}, u32[]{:S(2)}, u32[]{:S(2)}) %collective-permute-start) | collective-permute-done | bytes 524320 | tf_op jit(solution)/shard_map/ppermute | solution.py:62
  6.2 0.1 fusion
  6.3 3.0 %collective-permute-start.1 = (f16[256,128]{1,0:T(8,128)(2,1)S(1)}, f16[256,128]{1,0:T(8,128)(2,1)S(1)}, u32[]{:S(2)}, u32[]{:S(2)}) collective-permute-start(f16[256,128]{1,0:T(8,128)(2,1)S(1)} %get-tuple-element.19), channel_id=1, source_target_pairs={{0,4},{1,5},{2,6},{3,7},{4,0},{5,1},{6,2},{7,3},{8,12},{9,13},{10,... | collective-permute-start | bytes 196616 | tf_op jit(solution)/shard_map/ppermute | solution.py:62
  9.3 1.5 %collective-permute-start.2 = (f16[256,128]{1,0:T(8,128)(2,1)S(1)}, f16[256,128]{1,0:T(8,128)(2,1)S(1)}, u32[]{:S(2)}, u32[]{:S(2)}) collective-permute-start(f16[256,128]{1,0:T(8,128)(2,1)S(1)} %get-tuple-element.21), channel_id=1, source_target_pairs={{0,2},{1,3},{2,0},{3,1},{4,6},{5,7},{6,4},{7,5},{8,10},{9,11},{10,... | collective-permute-start | bytes 196616 | tf_op jit(solution)/shard_map/ppermute | solution.py:62
  10.8 0.0 collective-permute-start.3
  10.9 0.0 copy-start
  10.9 0.0 copy-start.1
  10.9 0.0 copy-start.2
  10.9 2.0 %shard_map.92 = (bf16[1,1601,1024]{2,1,0:T(8,128)(2,1)S(1)}, f32[256,128]{1,0:T(8,128)S(1)}) custom-call(bf16[1,1601,2048]{2,1,0:T(8,128)(2,1)} %cache_hbm.3, f32[256,128]{1,0:T(8,128)S(1)} %slice.28.before_ref), custom_call_target="tpu_custom_call", output_to_operand_aliasing={{1}: (1, {})} | custom-call | bytes 3278848 | tf_op jit(solution)/shard_map/pallas_call | solution.py:146
  12.9 0.0 collective-permute-done.1
  12.9 0.7 %collective-permute-done.2 = f16[256,128]{1,0:T(8,128)(2,1)S(1)} collective-permute-done((f16[256,128]{1,0:T(8,128)(2,1)S(1)}, f16[256,128]{1,0:T(8,128)(2,1)S(1)}, u32[]{:S(2)}, u32[]{:S(2)}) %collective-permute-start.2) | collective-permute-done | bytes 65568 | tf_op jit(solution)/shard_map/ppermute | solution.py:62
  13.6 2.4 %collective-permute-done.3 = f16[256,128]{1,0:T(8,128)(2,1)S(1)} collective-permute-done((f16[256,128]{1,0:T(8,128)(2,1)S(1)}, f16[256,128]{1,0:T(8,128)(2,1)S(1)}, u32[]{:S(2)}, u32[]{:S(2)}) %collective-permute-start.3) | collective-permute-done | bytes 65568 | tf_op jit(solution)/shard_map/ppermute | solution.py:62
  16.0 2.7 %collective-permute-start.4 = (f16[128,128]{1,0:T(8,128)(2,1)S(1)}, f16[128,128]{1,0:T(8,128)(2,1)S(1)}, u32[]{:S(2)}, u32[]{:S(2)}) collective-permute-start(f16[128,128]{1,0:T(8,128)(2,1)S(1)} %get-tuple-element.22), channel_id=1, source_target_pairs={{0,8},{1,9},{2,10},{3,11},{4,12},{5,13},{6,14},{7,15},{8,0},{9,1},... | collective-permute-start | bytes 98312 | tf_op jit(solution)/shard_map/ppermute | solution.py:62
  18.7 0.1 copy.12.mask_ref
  18.8 2.1 %shard_map.93 = (bf16[1,1601,1024]{2,1,0:T(8,128)(2,1)S(1)}, f32[128,128]{1,0:T(8,128)S(1)}) custom-call(bf16[1,1601,2048]{2,1,0:T(8,128)(2,1)} %cache_hbm.3, f32[128,128]{1,0:T(8,128)S(1)} %get-tuple-element.23.before_ref), custom_call_target="tpu_custom_call", output_to_operand_aliasing={{1}: (1, {})} | custom-call | bytes 3278848 | tf_op jit(solution)/shard_map/pallas_call | solution.py:146
  20.9 0.2 collective-permute-done.4
  21.2 0.0 slice-start.1
  21.2 3.1 %shard_map.94 = bf16[144,128]{1,0:T(8,128)(2,1)S(1)} custom-call(f32[128,128]{1,0:T(8,128)S(1)} %convert_add_fusion.1.query_ref, f32[128]{0:T(128)S(1)} %copy-done.2, bf16[1,1601,1024]{2,1,0:T(8,128)(2,1)S(1)} %get-tuple-element.15.keys_ref, bf16[1,1601,1024]{2,1,0:T(8,128)(2,1)S(1)} %get-tuple-element.16.values_ref, s32[8]{0:T(128)S(1)} %copy-done, ...), custom_call_target="tpu_custom_call" | custom-call | tf_op jit(solution)/shard_map/pallas_call | solution.py:354
  24.3 2.4 %collective-permute-start.5 = (bf16[1,144,128]{2,1,0:T(8,128)(2,1)S(1)}, bf16[1,144,128]{2,1,0:T(8,128)(2,1)S(1)}, u32[]{:S(2)}, u32[]{:S(2)}) collective-permute-start(bf16[1,144,128]{2,1,0:T(8,128)(2,1)S(1)} %bitcast.5), channel_id=1, source_target_pairs={{0,8},{1,9},{2,10},{3,11},{4,12},{5,13},{6,14},{7,15},{8,0},{9,1},... | collective-permute-start | bytes 110600 | tf_op jit(solution)/shard_map/ppermute | solution.py:62
  26.7 2.6 %collective-permute-done.5 = bf16[1,144,128]{2,1,0:T(8,128)(2,1)S(1)} collective-permute-done((bf16[1,144,128]{2,1,0:T(8,128)(2,1)S(1)}, bf16[1,144,128]{2,1,0:T(8,128)(2,1)S(1)}, u32[]{:S(2)}, u32[]{:S(2)}) %collective-permute-start.5) | collective-permute-done | bytes 36896 | tf_op jit(solution)/shard_map/ppermute | solution.py:62
  29.3 0.2 collective-permute-start.6
  29.5 0.5 %collective-permute-start.7 = (bf16[2,144,128]{2,1,0:T(8,128)(2,1)S(1)}, bf16[2,144,128]{2,1,0:T(8,128)(2,1)S(1)}, u32[]{:S(2)}, u32[]{:S(2)}) collective-permute-start(bf16[2,144,128]{2,1,0:T(8,128)(2,1)S(1)} %pad_maximum_fusion), channel_id=1, source_target_pairs={{0,2},{1,3},{2,0},{3,1},{4,6},{5,7},{6,4},{7,5},{8,10},{9,11},{10,... | collective-permute-start | bytes 221192 | tf_op jit(solution)/shard_map/ppermute | solution.py:62
  30.0 2.8 %collective-permute-start.8 = (bf16[2,144,128]{2,1,0:T(8,128)(2,1)S(1)}, bf16[2,144,128]{2,1,0:T(8,128)(2,1)S(1)}, u32[]{:S(2)}, u32[]{:S(2)}) collective-permute-start(bf16[2,144,128]{2,1,0:T(8,128)(2,1)S(1)} %pad_maximum_fusion), channel_id=1, source_target_pairs={{0,6},{1,7},{2,4},{3,5},{4,2},{5,3},{6,0},{7,1},{8,14},{9,15},{10,... | collective-permute-start | bytes 221192 | tf_op jit(solution)/shard_map/ppermute | solution.py:62
  32.9 0.8 %collective-permute-done.6 = bf16[2,144,128]{2,1,0:T(8,128)(2,1)S(1)} collective-permute-done((bf16[2,144,128]{2,1,0:T(8,128)(2,1)S(1)}, bf16[2,144,128]{2,1,0:T(8,128)(2,1)S(1)}, u32[]{:S(2)}, u32[]{:S(2)}) %collective-permute-start.6) | collective-permute-done | bytes 73760 | tf_op jit(solution)/shard_map/ppermute | solution.py:62
  33.7 0.1 collective-permute-done.7
  33.9 1.4 %collective-permute-done.8 = bf16[2,144,128]{2,1,0:T(8,128)(2,1)S(1)} collective-permute-done((bf16[2,144,128]{2,1,0:T(8,128)(2,1)S(1)}, bf16[2,144,128]{2,1,0:T(8,128)(2,1)S(1)}, u32[]{:S(2)}, u32[]{:S(2)}) %collective-permute-start.8) | collective-permute-done | bytes 73760 | tf_op jit(solution)/shard_map/ppermute | solution.py:62
  35.3 0.1 collective-permute-start.9
  36.0 0.9 %collective-permute-done.9 = bf16[8,144,128]{2,1,0:T(8,128)(2,1)S(1)} collective-permute-done((bf16[8,144,128]{2,1,0:T(8,128)(2,1)S(1)}, bf16[8,144,128]{2,1,0:T(8,128)(2,1)S(1)}, u32[]{:S(2)}, u32[]{:S(2)}) %collective-permute-start.9) | collective-permute-done | bytes 294944 | tf_op jit(solution)/shard_map/ppermute | solution.py:62
  37.0 4.1 %shard_map.95 = bf16[8,2,512]{2,1,0:T(2,128)(2,1)} custom-call(f32[1]{0:T(128)S(6)} %copy.24.gate_ref, s32[8]{0:T(128)S(1)} %copy-done, s32[8]{0:T(128)S(1)} %copy-done.1, bf16[16,144,128]{2,1,0:T(8,128)(2,1)S(1)} %constant_dynamic-update-slice_fusion.5.tiles_ref, bf16[8192,512]{1,0:T(8,128)(2,1)S(1)} %bitcast.4), custom_call_target="tpu_custom_call" | custom-call | tf_op jit(solution)/shard_map/pallas_call | solution.py:366
  (20 shorter events, 0.3 us)
Async XLA Ops:
  4.1 14.6 %copy-start.3 = (s32[8,2,4]{0,2,1:T(4,128)S(1)}, s32[8,2,4]{0,2,1:T(4,128)}, u32[]{:S(2)}) copy-start(s32[8,2,4]{0,2,1:T(4,128)} %param.15) | copy-start | bytes 772
  4.1 2.1 %collective-permute-start = (f32[1024,128]{1,0:T(8,128)S(1)}, f32[1024,128]{1,0:T(8,128)S(1)}, u32[]{:S(2)}, u32[]{:S(2)}) collective-permute-start(f32[1024,128]{1,0:T(8,128)S(1)} %get-tuple-element.12), channel_id=1, source_target_pairs={{0,1},{1,0},{2,3},{3,2},{4,5},{5,4},{6,7},{7,6},{8,9},{9,8},{10,11... | collective-permute-start | bytes 1572872 | tf_op jit(solution)/shard_map/ppermute | solution.py:62
  6.3 6.6 %collective-permute-start.1 = (f16[256,128]{1,0:T(8,128)(2,1)S(1)}, f16[256,128]{1,0:T(8,128)(2,1)S(1)}, u32[]{:S(2)}, u32[]{:S(2)}) collective-permute-start(f16[256,128]{1,0:T(8,128)(2,1)S(1)} %get-tuple-element.19), channel_id=1, source_target_pairs={{0,4},{1,5},{2,6},{3,7},{4,0},{5,1},{6,2},{7,3},{8,12},{9,13},{10,... | collective-permute-start | bytes 196616 | tf_op jit(solution)/shard_map/ppermute | solution.py:62
  9.3 4.3 %collective-permute-start.2 = (f16[256,128]{1,0:T(8,128)(2,1)S(1)}, f16[256,128]{1,0:T(8,128)(2,1)S(1)}, u32[]{:S(2)}, u32[]{:S(2)}) collective-permute-start(f16[256,128]{1,0:T(8,128)(2,1)S(1)} %get-tuple-element.21), channel_id=1, source_target_pairs={{0,2},{1,3},{2,0},{3,1},{4,6},{5,7},{6,4},{7,5},{8,10},{9,11},{10,... | collective-permute-start | bytes 196616 | tf_op jit(solution)/shard_map/ppermute | solution.py:62
  10.8 5.2 %collective-permute-start.3 = (f16[256,128]{1,0:T(8,128)(2,1)S(1)}, f16[256,128]{1,0:T(8,128)(2,1)S(1)}, u32[]{:S(2)}, u32[]{:S(2)}) collective-permute-start(f16[256,128]{1,0:T(8,128)(2,1)S(1)} %get-tuple-element.20), channel_id=1, source_target_pairs={{0,6},{1,7},{2,4},{3,5},{4,2},{5,3},{6,0},{7,1},{8,14},{9,15},{10,... | collective-permute-start | bytes 196616 | tf_op jit(solution)/shard_map/ppermute | solution.py:62
  10.9 10.3 %copy-start = (s32[8]{0:T(128)S(1)}, s32[8]{0:T(128)}, u32[]{:S(2)}) copy-start(s32[8]{0:T(128)} %first_ref.3) | copy-start | bytes 100
  10.9 10.3 %copy-start.1 = (s32[8]{0:T(128)S(1)}, s32[8]{0:T(128)}, u32[]{:S(2)}) copy-start(s32[8]{0:T(128)} %count_ref.3) | copy-start | bytes 100
  10.9 10.3 %copy-start.2 = (f32[128]{0:T(128)S(1)}, f32[128]{0:T(128)}, u32[]{:S(2)}) copy-start(f32[128]{0:T(128)} %gain_ref.1) | copy-start | bytes 1540
  16.0 5.1 %collective-permute-start.4 = (f16[128,128]{1,0:T(8,128)(2,1)S(1)}, f16[128,128]{1,0:T(8,128)(2,1)S(1)}, u32[]{:S(2)}, u32[]{:S(2)}) collective-permute-start(f16[128,128]{1,0:T(8,128)(2,1)S(1)} %get-tuple-element.22), channel_id=1, source_target_pairs={{0,8},{1,9},{2,10},{3,11},{4,12},{5,13},{6,14},{7,15},{8,0},{9,1},... | collective-permute-start | bytes 98312 | tf_op jit(solution)/shard_map/ppermute | solution.py:62
  18.8 18.2 %slice-start = ((s8[8388608]{0:T(1024)(128)(4,1)}), s8[4194304]{0:T(1024)(128)(4,1)S(1)}, s32[]{:S(2)}) async-start(s8[8388608]{0:T(1024)(128)(4,1)} %bitcast.3), calls=%async_computation | async-start | bytes 8388608
  21.2 15.8 %slice-start.1 = ((s8[8388608]{0:T(1024)(128)(4,1)}), s8[4194304]{0:T(1024)(128)(4,1)S(1)}, s32[]{:S(2)}) async-start(s8[8388608]{0:T(1024)(128)(4,1)} %bitcast.3), calls=%async_computation.1 | async-start | bytes 8388608
  24.3 5.0 %collective-permute-start.5 = (bf16[1,144,128]{2,1,0:T(8,128)(2,1)S(1)}, bf16[1,144,128]{2,1,0:T(8,128)(2,1)S(1)}, u32[]{:S(2)}, u32[]{:S(2)}) collective-permute-start(bf16[1,144,128]{2,1,0:T(8,128)(2,1)S(1)} %bitcast.5), channel_id=1, source_target_pairs={{0,8},{1,9},{2,10},{3,11},{4,12},{5,13},{6,14},{7,15},{8,0},{9,1},... | collective-permute-start | bytes 110600 | tf_op jit(solution)/shard_map/ppermute | solution.py:62
  29.3 4.4 %collective-permute-start.6 = (bf16[2,144,128]{2,1,0:T(8,128)(2,1)S(1)}, bf16[2,144,128]{2,1,0:T(8,128)(2,1)S(1)}, u32[]{:S(2)}, u32[]{:S(2)}) collective-permute-start(bf16[2,144,128]{2,1,0:T(8,128)(2,1)S(1)} %pad_maximum_fusion), channel_id=1, source_target_pairs={{0,4},{1,5},{2,6},{3,7},{4,0},{5,1},{6,2},{7,3},{8,12},{9,13},{10,... | collective-permute-start | bytes 221192 | tf_op jit(solution)/shard_map/ppermute | solution.py:62
  29.5 4.4 %collective-permute-start.7 = (bf16[2,144,128]{2,1,0:T(8,128)(2,1)S(1)}, bf16[2,144,128]{2,1,0:T(8,128)(2,1)S(1)}, u32[]{:S(2)}, u32[]{:S(2)}) collective-permute-start(bf16[2,144,128]{2,1,0:T(8,128)(2,1)S(1)} %pad_maximum_fusion), channel_id=1, source_target_pairs={{0,2},{1,3},{2,0},{3,1},{4,6},{5,7},{6,4},{7,5},{8,10},{9,11},{10,... | collective-permute-start | bytes 221192 | tf_op jit(solution)/shard_map/ppermute | solution.py:62
  30.0 5.3 %collective-permute-start.8 = (bf16[2,144,128]{2,1,0:T(8,128)(2,1)S(1)}, bf16[2,144,128]{2,1,0:T(8,128)(2,1)S(1)}, u32[]{:S(2)}, u32[]{:S(2)}) collective-permute-start(bf16[2,144,128]{2,1,0:T(8,128)(2,1)S(1)} %pad_maximum_fusion), channel_id=1, source_target_pairs={{0,6},{1,7},{2,4},{3,5},{4,2},{5,3},{6,0},{7,1},{8,14},{9,15},{10,... | collective-permute-start | bytes 221192 | tf_op jit(solution)/shard_map/ppermute | solution.py:62
  35.3 1.6 %collective-permute-start.9 = (bf16[8,144,128]{2,1,0:T(8,128)(2,1)S(1)}, bf16[8,144,128]{2,1,0:T(8,128)(2,1)S(1)}, u32[]{:S(2)}, u32[]{:S(2)}) collective-permute-start(bf16[8,144,128]{2,1,0:T(8,128)(2,1)S(1)} %get-tuple-element.24), channel_id=1, source_target_pairs={{0,1},{1,0},{2,3},{3,2},{4,5},{5,4},{6,7},{7,6},{8,9},{9,8},{10,11... | collective-permute-start | bytes 884744 | tf_op jit(solution)/shard_map/ppermute | solution.py:62

commit v4 on v3

--- a/solution.py
+++ b/solution.py
@@ -31,30 +31,30 @@
     return pltpu.CompilerParams(vmem_limit_bytes=mebibytes << 20)
 
 
-def scatter_stages(bits):
+def exchange_stages(bits):
     if bits < 3:
-        return [[bit] for bit in range(bits)]
-    return [[0], [1, 2]] + [[bit] for bit in range(3, bits)]
+        return [[1 << bit] for bit in range(bits)]
+    return [[1], [4, 3]] + [[(1 << bit) | 1] for bit in range(3, bits)]
 
 
 def offsets(group):
     result = [0]
-    for bit in reversed(group):
-        result = result + [other | (1 << bit) for other in result]
+    for difference in group:
+        result = result + [other ^ difference for other in result]
     return result
 
 
 def positions(stages):
     result = [0]
     for group in stages:
-        result = [base | step for base in result for step in offsets(group)]
+        result = [base ^ step for base in result for step in offsets(group)]
     return result
 
 
-def move_bits(value, moves):
+def combine_bits(value, masks):
     result = value & 0
-    for source, target in moves:
-        result = result | (((value >> source) & 1) << target)
+    for bit, mask in enumerate(masks):
+        result = result ^ (((value >> bit) & 1) * mask)
     return result
 
 
@@ -95,8 +95,7 @@
     place = out_row % slots
     step = out_row // slots
     in_row = lax.broadcasted_iota(jnp.int32, shape, 1)
-    bits = range(slots.bit_length() - 1)
-    slot = move_bits(place, [(i, order[1 << i].bit_length() - 1) for i in bits]) ^ me
+    slot = combine_bits(place, [order[1 << i] for i in range(slots.bit_length() - 1)]) ^ me
     start = jnp.zeros(shape, jnp.int32)
     length = jnp.zeros(shape, jnp.int32)
     for row in range(rows):
@@ -124,7 +123,7 @@
                 send_ref[pl.ds(at, half, stride=tile_rows), :] = block[half:]
 
 
-def fetch_kernel(part, cache_hbm, before_ref, cache_ref, after_ref, sems):
+def fetch_kernel(part, cache_hbm, before_ref, gate_ref, cache_ref, after_ref, tanh_ref, sems):
     del before_ref, after_ref
     pieces = sems.shape[0]
     span = cache_ref.shape[2] // pieces
@@ -138,24 +137,26 @@
     ]
     for copy in copies:
         copy.start()
+    tanh_ref[...] = jnp.tanh(jnp.full(tanh_ref.shape, gate_ref[0], F32))
     for copy in copies:
         copy.wait()
 
 
-def fetch(cache, part, held):
+def fetch(cache, part, held, gate):
     return pl.pallas_call(
         functools.partial(fetch_kernel, part),
         out_shape=[
             struct((*cache.shape[:2], cache.shape[2] // 2), cache.dtype),
             struct(held.shape, held.dtype),
+            struct((8, 128), F32),
         ],
-        in_specs=[HBM, ANY],
-        out_specs=[VMEM, ANY],
+        in_specs=[HBM, ANY, SMEM],
+        out_specs=[VMEM, ANY, VMEM],
         scratch_shapes=[pltpu.SemaphoreType.DMA((4,))],
         input_output_aliases={1: 1},
         compiler_params=params(1),
         cost_estimate=pl.CostEstimate(flops=0, bytes_accessed=cache.size, transcendentals=0),
-    )(in_hbm(cache), held)
+    )(in_hbm(cache), held, gate)
 
 
 def attend_kernel(
@@ -184,9 +185,10 @@
     stats = jnp.zeros((size, head_size), F32)
     scale = 1.0 / math.sqrt(head_size)
     blank = jnp.zeros((size, head_size), BF16)
-    for base in range(0, kv_heads, join):
-        at = base * head_size
-        keys = keys_ref[0, :, at : at + span]
+    bases = range(0, kv_heads, join)
+    scores = []
+    for base in bases:
+        keys = keys_ref[0, :, base * head_size : (base + join) * head_size]
         left = jnp.concatenate(
             [
                 jnp.concatenate(
@@ -200,14 +202,15 @@
             ],
             axis=0,
         )
-        scores = lax.dot_general(
-            left, keys, (((1,), (1,)), ((), ())), preferred_element_type=F32
-        ) * scale
-        top = jnp.max(scores, axis=1, keepdims=True)
-        weights = jnp.exp(scores - top).astype(BF16)
-        total = jnp.sum(weights.astype(F32), axis=1, keepdims=True)
-        values = values_ref[0, :, at : at + span]
-        mixed = jnp.dot(weights, values, preferred_element_type=F32) / total
+        scores.append(
+            lax.dot_general(left, keys, (((1,), (1,)), ((), ())), preferred_element_type=F32) * scale
+        )
+    tops = [jnp.max(score, axis=1, keepdims=True) for score in scores]
+    weights = [jnp.exp(score - top).astype(BF16) for score, top in zip(scores, tops)]
+    totals = [jnp.sum(weight.astype(F32), axis=1, keepdims=True) for weight in weights]
+    for base, top, weight, total in zip(bases, tops, weights, totals):
+        values = values_ref[0, :, base * head_size : (base + join) * head_size]
+        mixed = jnp.dot(weight, values, preferred_element_type=F32) / total
         for i in range(join):
             h = base + i
             rows_here = slice(i * size, (i + 1) * size)
@@ -233,7 +236,8 @@
 
 
 def finish_kernel(
-    order, kv_heads, group, steps, max_tiles, gate_ref, first_ref, count_ref, tiles_ref, weight_ref, out_ref, stats, turned
+    order, kv_heads, group, steps, max_tiles, gate_ref, first_ref, count_ref, tiles_ref, weight_ref,
+    out_ref, stats, turned
 ):
     rows = first_ref.shape[0]
     head_size = tiles_ref.shape[-1]
@@ -250,13 +254,13 @@
     stats[0] = whole
     stats[1] = pltpu.roll(whole, head_size - 3 * kv_heads, 1)
     pairs = rows * steps
-    moves = [(order[1 << i].bit_length() - 1, i) for i in range(slots.bit_length() - 1)]
+    masks = [order.index(1 << i) for i in range(slots.bit_length() - 1)]
 
     def one_row(row, carry):
         begin = first_ref[row]
         length = count_ref[row]
         places = [
-            move_bits(me ^ (begin + jnp.minimum(k, length - 1)), moves) for k in range(max_tiles)
+            combine_bits(me ^ (begin + jnp.minimum(k, length - 1)), masks) for k in range(max_tiles)
         ]
         tops = []
         for k in range(max_tiles):
@@ -281,7 +285,7 @@
                 ]
         return carry
 
-    lax.fori_loop(0, rows, one_row, 0)
+    lax.fori_loop(0, rows, one_row, 0, unroll=8)
     total = jnp.zeros((pairs, weight_ref.shape[1]), F32)
     for h in range(kv_heads):
         left = jnp.concatenate(
@@ -295,7 +299,7 @@
         total = total + jnp.dot(
             left, weight_ref[h * span : (h + 1) * span, :], preferred_element_type=F32
         )
-    gate = jnp.tanh(jnp.full((1, 1), gate_ref[0], F32))
+    gate = gate_ref[:1, :1]
     result = (total * gate).astype(BF16)
     out_ref[...] = result.reshape(rows, steps, result.shape[1])
 
@@ -319,7 +323,7 @@
     kv_heads = image_cache.shape[2] // (2 * head_size)
     group = heads // kv_heads
     tile_rows = steps * heads
-    stages = scatter_stages(devices.bit_length() - 1)
+    stages = exchange_stages(devices.bit_length() - 1)
     order = positions(stages)
     half = devices // 2
     chunks = 4
@@ -347,7 +351,7 @@
         sent = [piece.astype(jnp.float16) for piece in pieces[1:]]
         got = [exchange(piece, step, devices) for piece, step in zip(sent, steps_out[1:])]
         if len(cache) < 2:
-            half, pieces[0] = fetch(image_cache, len(cache), pieces[0])
+            half, pieces[0], gate = fetch(image_cache, len(cache), pieces[0], output_gate)
             cache.append(half)
         total = functools.reduce(jnp.add, [pieces[0]] + [piece.astype(F32) for piece in got])
     block = (kv_heads + 1) * steps * group
@@ -366,14 +370,14 @@
     return pl.pallas_call(
         functools.partial(finish_kernel, order, kv_heads, group, steps, cross_tile_mask.shape[2]),
         out_shape=struct((rows, steps, output_weight.shape[1]), BF16),
-        in_specs=[SMEM] * 3 + [VMEM, VMEM],
+        in_specs=[VMEM, SMEM, SMEM, VMEM, VMEM],
         out_specs=VMEM,
         scratch_shapes=[
             pltpu.VMEM((2, devices * steps * group, head_size), F32),
             pltpu.VMEM((heads * rows * steps, head_size), F32),
         ],
         compiler_params=params(8),
-    )(output_gate, image_first_slot, tile_count, gathered, output_weight)
+    )(gate, image_first_slot, tile_count, gathered, output_weight)
 
 
 def solution(mesh):

time: 41.3 us -> 38.7 us (0.937)
  Pallas kernels: 15.4 us -> 14 us
  waiting for transfers between devices: 10.7 us -> 9.87 us
    pallas_call x1, Pallas kernels: 4.1 us -> 2.9 us  [body(): pl.pallas_call(functools.partial(finish_kernel, order, kv_heads, group, s...]
    ppermute x10, waiting for transfers between devices: 10.7 us -> 9.87 us  [exchange(): lax.ppermute(array, AXIS, [(i, i ^ difference) for i in range(count)])]
    pallas_call x1, Pallas kernels: 3.12 us -> 2.34 us  [body(): pl.pallas_call(functools.partial(attend_kernel, kv_heads, group, steps),...]
    pallas_call x2, Pallas kernels: 4.09 us -> 4.68 us  [fetch(): pl.pallas_call(functools.partial(fetch_kernel, part), out_shape=[struct((...]
  transfers between devices with their start and end apart: 10 -> 10, of which waited for: 9 -> 8; matrix products, arithmetic and copies ran while one was open for 0% -> 0% of each run, Pallas kernels for 10% -> 12%
where the time goes in v4:
time: 38.7 us; the launch traced here: 38.5 us
  Pallas kernels  14 us (36%)
  starting transfers between devices  13.3 us (34%)
  waiting for transfers between devices  9.87 us (26%)
  between operations  0.86 us (2%)
    ppermute x10, starting transfers between devices, exchange(): lax.ppermute(array, AXIS, [(i, i ^ difference) for i in range(count)])  13.3 us
    ppermute x10, waiting for transfers between devices, exchange(): lax.ppermute(array, AXIS, [(i, i ^ difference) for i in range(count)])  9.87 us
    pallas_call x2, Pallas kernels, fetch(): pl.pallas_call(functools.partial(fetch_kernel, part), out_shape=[struct((...  4.68 us
    pallas_call x1, Pallas kernels, body(): pl.pallas_call(functools.partial(project_kernel, order, chunks, kv_heads,...  4.09 us
    pallas_call x1, Pallas kernels, body(): pl.pallas_call(functools.partial(finish_kernel, order, kv_heads, group, s...  2.9 us
    pallas_call x1, Pallas kernels, body(): pl.pallas_call(functools.partial(attend_kernel, kv_heads, group, steps),...  2.34 us
  transfers between devices with their start and end apart: 10, of which 8 were waited for; matrix products, arithmetic and copies ran while one was open for 0% of the time, Pallas kernels for 12%

profile of v4, /device:TPU:0, one launch (start us, length us, event | category | flops | bytes accessed | tf_op | source)
XLA Modules:
  0.0 38.5 jit_solution(11625015835067747482)
XLA Ops:
  0.0 4.1 %shard_map.91 = (f32[1024,128]{1,0:T(8,128)S(1)}, f32[1024,128]{1,0:T(8,128)S(1)}) custom-call(bf16[8,2,512]{2,1,0:T(2,128)(2,1)} %x_hbm.1, bf16[512,8192]{1,0:T(8,128)(2,1)} %weight_hbm.1, s32[8]{0:T(128)} %first_ref.3, s32[8]{0:T(128)} %count_ref.3), custom_call_target="tpu_custom_call" | custom-call | tf_op jit(solution)/shard_map/pallas_call | solution.py:330
  4.1 0.0 copy-start.3
  4.1 0.5 %collective-permute-start = (f32[1024,128]{1,0:T(8,128)S(1)}, f32[1024,128]{1,0:T(8,128)S(1)}, u32[]{:S(2)}, u32[]{:S(2)}) collective-permute-start(f32[1024,128]{1,0:T(8,128)S(1)} %get-tuple-element.13), channel_id=1, source_target_pairs={{0,1},{1,0},{2,3},{3,2},{4,5},{5,4},{6,7},{7,6},{8,9},{9,8},{10,11... | collective-permute-start | bytes 1572872 | tf_op jit(solution)/shard_map/ppermute | solution.py:62
  4.6 1.5 %collective-permute-done = f32[1024,128]{1,0:T(8,128)S(1)} collective-permute-done((f32[1024,128]{1,0:T(8,128)S(1)}, f32[1024,128]{1,0:T(8,128)S(1)}, u32[]{:S(2)}, u32[]{:S(2)}) %collective-permute-start) | collective-permute-done | bytes 524320 | tf_op jit(solution)/shard_map/ppermute | solution.py:62
  6.2 0.1 fusion
  6.3 3.0 %collective-permute-start.1 = (f16[256,128]{1,0:T(8,128)(2,1)S(1)}, f16[256,128]{1,0:T(8,128)(2,1)S(1)}, u32[]{:S(2)}, u32[]{:S(2)}) collective-permute-start(f16[256,128]{1,0:T(8,128)(2,1)S(1)} %get-tuple-element.21), channel_id=1, source_target_pairs={{0,4},{1,5},{2,6},{3,7},{4,0},{5,1},{6,2},{7,3},{8,12},{9,13},{10,... | collective-permute-start | bytes 196616 | tf_op jit(solution)/shard_map/ppermute | solution.py:62
  9.3 1.0 %collective-permute-start.2 = (f16[256,128]{1,0:T(8,128)(2,1)S(1)}, f16[256,128]{1,0:T(8,128)(2,1)S(1)}, u32[]{:S(2)}, u32[]{:S(2)}) collective-permute-start(f16[256,128]{1,0:T(8,128)(2,1)S(1)} %get-tuple-element.23), channel_id=1, source_target_pairs={{0,3},{1,2},{2,1},{3,0},{4,7},{5,6},{6,5},{7,4},{8,11},{9,10},{10,... | collective-permute-start | bytes 196616 | tf_op jit(solution)/shard_map/ppermute | solution.py:62
  10.3 0.3 collective-permute-start.3
  11.2 0.0 copy-start
  11.2 0.0 copy-start.1
  11.3 0.0 copy-start.2
  11.3 2.6 %shard_map.92 = (bf16[1,1601,1024]{2,1,0:T(8,128)(2,1)S(1)}, f32[256,128]{1,0:T(8,128)S(1)}, f32[8,128]{1,0:T(8,128)}) custom-call(bf16[1,1601,2048]{2,1,0:T(8,128)(2,1)} %cache_hbm.3, f32[256,128]{1,0:T(8,128)S(1)} %slice.28.before_ref, f32[1]{0:T(128)S(6)} %copy.24.gate_ref), custom_call_target="tpu_custom_call", output_to_operand_aliasing={{1}: (1, {})} | custom-call | bytes 3278848 | tf_op jit(solution)/shard_map/pallas_call | solution.py:146
  13.8 0.0 collective-permute-done.1
  13.9 0.3 collective-permute-done.2
  14.1 0.7 %collective-permute-done.3 = f16[256,128]{1,0:T(8,128)(2,1)S(1)} collective-permute-done((f16[256,128]{1,0:T(8,128)(2,1)S(1)}, f16[256,128]{1,0:T(8,128)(2,1)S(1)}, u32[]{:S(2)}, u32[]{:S(2)}) %collective-permute-start.3) | collective-permute-done | bytes 65568 | tf_op jit(solution)/shard_map/ppermute | solution.py:62
  14.9 2.9 %collective-permute-start.4 = (f16[128,128]{1,0:T(8,128)(2,1)S(1)}, f16[128,128]{1,0:T(8,128)(2,1)S(1)}, u32[]{:S(2)}, u32[]{:S(2)}) collective-permute-start(f16[128,128]{1,0:T(8,128)(2,1)S(1)} %get-tuple-element.24), channel_id=1, source_target_pairs={{0,9},{1,8},{2,11},{3,10},{4,13},{5,12},{6,15},{7,14},{8,1},{9,0},... | collective-permute-start | bytes 98312 | tf_op jit(solution)/shard_map/ppermute | solution.py:62
  17.8 0.1 copy.12.mask_ref
  17.9 2.1 %shard_map.93 = (bf16[1,1601,1024]{2,1,0:T(8,128)(2,1)S(1)}, f32[128,128]{1,0:T(8,128)S(1)}, f32[8,128]{1,0:T(8,128)S(1)}) custom-call(bf16[1,1601,2048]{2,1,0:T(8,128)(2,1)} %cache_hbm.3, f32[128,128]{1,0:T(8,128)S(1)} %get-tuple-element.25.before_ref, f32[1]{0:T(128)S(6)} %copy.24.gate_ref), custom_call_target="tpu_custom_call", output_to_operand_aliasing={{1}: (1, {})} | custom-call | bytes 3278848 | tf_op jit(solution)/shard_map/pallas_call | solution.py:146
  20.0 0.1 collective-permute-done.4
  20.2 0.0 slice-start.1
  20.2 2.3 %shard_map.94 = bf16[144,128]{1,0:T(8,128)(2,1)S(1)} custom-call(f32[128,128]{1,0:T(8,128)S(1)} %convert_add_fusion.1.query_ref, f32[128]{0:T(128)S(1)} %copy-done.2, bf16[1,1601,1024]{2,1,0:T(8,128)(2,1)S(1)} %get-tuple-element.17.keys_ref, bf16[1,1601,1024]{2,1,0:T(8,128)(2,1)S(1)} %get-tuple-element.18.values_ref, s32[8]{0:T(128)S(1)} %copy-done, ...), custom_call_target="tpu_custom_call" | custom-call | tf_op jit(solution)/shard_map/pallas_call | solution.py:358
  22.6 2.0 %collective-permute-start.5 = (bf16[1,144,128]{2,1,0:T(8,128)(2,1)S(1)}, bf16[1,144,128]{2,1,0:T(8,128)(2,1)S(1)}, u32[]{:S(2)}, u32[]{:S(2)}) collective-permute-start(bf16[1,144,128]{2,1,0:T(8,128)(2,1)S(1)} %bitcast.5), channel_id=1, source_target_pairs={{0,9},{1,8},{2,11},{3,10},{4,13},{5,12},{6,15},{7,14},{8,1},{9,0},... | collective-permute-start | bytes 110600 | tf_op jit(solution)/shard_map/ppermute | solution.py:62
  24.5 3.3 %collective-permute-done.5 = bf16[1,144,128]{2,1,0:T(8,128)(2,1)S(1)} collective-permute-done((bf16[1,144,128]{2,1,0:T(8,128)(2,1)S(1)}, bf16[1,144,128]{2,1,0:T(8,128)(2,1)S(1)}, u32[]{:S(2)}, u32[]{:S(2)}) %collective-permute-start.5) | collective-permute-done | bytes 36896 | tf_op jit(solution)/shard_map/ppermute | solution.py:62
  27.8 0.1 collective-permute-start.6
  27.9 1.0 %collective-permute-start.7 = (bf16[2,144,128]{2,1,0:T(8,128)(2,1)S(1)}, bf16[2,144,128]{2,1,0:T(8,128)(2,1)S(1)}, u32[]{:S(2)}, u32[]{:S(2)}) collective-permute-start(bf16[2,144,128]{2,1,0:T(8,128)(2,1)S(1)} %pad_maximum_fusion), channel_id=1, source_target_pairs={{0,3},{1,2},{2,1},{3,0},{4,7},{5,6},{6,5},{7,4},{8,11},{9,10},{10,... | collective-permute-start | bytes 221192 | tf_op jit(solution)/shard_map/ppermute | solution.py:62
  28.9 2.2 %collective-permute-start.8 = (bf16[2,144,128]{2,1,0:T(8,128)(2,1)S(1)}, bf16[2,144,128]{2,1,0:T(8,128)(2,1)S(1)}, u32[]{:S(2)}, u32[]{:S(2)}) collective-permute-start(bf16[2,144,128]{2,1,0:T(8,128)(2,1)S(1)} %pad_maximum_fusion), channel_id=1, source_target_pairs={{0,7},{1,6},{2,5},{3,4},{4,3},{5,2},{6,1},{7,0},{8,15},{9,14},{10,... | collective-permute-start | bytes 221192 | tf_op jit(solution)/shard_map/ppermute | solution.py:62
  31.1 1.3 %collective-permute-done.6 = bf16[2,144,128]{2,1,0:T(8,128)(2,1)S(1)} collective-permute-done((bf16[2,144,128]{2,1,0:T(8,128)(2,1)S(1)}, bf16[2,144,128]{2,1,0:T(8,128)(2,1)S(1)}, u32[]{:S(2)}, u32[]{:S(2)}) %collective-permute-start.6) | collective-permute-done | bytes 73760 | tf_op jit(solution)/shard_map/ppermute | solution.py:62
  32.4 0.0 collective-permute-done.7
  32.4 1.5 %collective-permute-done.8 = bf16[2,144,128]{2,1,0:T(8,128)(2,1)S(1)} collective-permute-done((bf16[2,144,128]{2,1,0:T(8,128)(2,1)S(1)}, bf16[2,144,128]{2,1,0:T(8,128)(2,1)S(1)}, u32[]{:S(2)}, u32[]{:S(2)}) %collective-permute-start.8) | collective-permute-done | bytes 73760 | tf_op jit(solution)/shard_map/ppermute | solution.py:62
  33.9 0.4 %collective-permute-start.9 = (bf16[8,144,128]{2,1,0:T(8,128)(2,1)S(1)}, bf16[8,144,128]{2,1,0:T(8,128)(2,1)S(1)}, u32[]{:S(2)}, u32[]{:S(2)}) collective-permute-start(bf16[8,144,128]{2,1,0:T(8,128)(2,1)S(1)} %get-tuple-element.26), channel_id=1, source_target_pairs={{0,1},{1,0},{2,3},{3,2},{4,5},{5,4},{6,7},{7,6},{8,9},{9,8},{10,11... | collective-permute-start | bytes 884744 | tf_op jit(solution)/shard_map/ppermute | solution.py:62
  34.4 1.2 %collective-permute-done.9 = bf16[8,144,128]{2,1,0:T(8,128)(2,1)S(1)} collective-permute-done((bf16[8,144,128]{2,1,0:T(8,128)(2,1)S(1)}, bf16[8,144,128]{2,1,0:T(8,128)(2,1)S(1)}, u32[]{:S(2)}, u32[]{:S(2)}) %collective-permute-start.9) | collective-permute-done | bytes 294944 | tf_op jit(solution)/shard_map/ppermute | solution.py:62
  35.7 2.9 %shard_map.95 = bf16[8,2,512]{2,1,0:T(2,128)(2,1)} custom-call(f32[8,128]{1,0:T(8,128)S(1)} %get-tuple-element.15.gate_ref, s32[8]{0:T(128)S(1)} %copy-done, s32[8]{0:T(128)S(1)} %copy-done.1, bf16[16,144,128]{2,1,0:T(8,128)(2,1)S(1)} %constant_dynamic-update-slice_fusion.5.tiles_ref, bf16[8192,512]{1,0:T(8,128)(2,1)S(1)} %bitcast.4), custom_call_target="tpu_custom_call" | custom-call | tf_op jit(solution)/shard_map/pallas_call | solution.py:370
  (20 shorter events, 0.3 us)
Async XLA Ops:
  4.1 13.7 %copy-start.3 = (s32[8,2,4]{0,2,1:T(4,128)S(1)}, s32[8,2,4]{0,2,1:T(4,128)}, u32[]{:S(2)}) copy-start(s32[8,2,4]{0,2,1:T(4,128)} %param.15) | copy-start | bytes 772
  4.1 2.1 %collective-permute-start = (f32[1024,128]{1,0:T(8,128)S(1)}, f32[1024,128]{1,0:T(8,128)S(1)}, u32[]{:S(2)}, u32[]{:S(2)}) collective-permute-start(f32[1024,128]{1,0:T(8,128)S(1)} %get-tuple-element.13), channel_id=1, source_target_pairs={{0,1},{1,0},{2,3},{3,2},{4,5},{5,4},{6,7},{7,6},{8,9},{9,8},{10,11... | collective-permute-start | bytes 1572872 | tf_op jit(solution)/shard_map/ppermute | solution.py:62
  6.3 7.6 %collective-permute-start.1 = (f16[256,128]{1,0:T(8,128)(2,1)S(1)}, f16[256,128]{1,0:T(8,128)(2,1)S(1)}, u32[]{:S(2)}, u32[]{:S(2)}) collective-permute-start(f16[256,128]{1,0:T(8,128)(2,1)S(1)} %get-tuple-element.21), channel_id=1, source_target_pairs={{0,4},{1,5},{2,6},{3,7},{4,0},{5,1},{6,2},{7,3},{8,12},{9,13},{10,... | collective-permute-start | bytes 196616 | tf_op jit(solution)/shard_map/ppermute | solution.py:62
  9.3 4.8 %collective-permute-start.2 = (f16[256,128]{1,0:T(8,128)(2,1)S(1)}, f16[256,128]{1,0:T(8,128)(2,1)S(1)}, u32[]{:S(2)}, u32[]{:S(2)}) collective-permute-start(f16[256,128]{1,0:T(8,128)(2,1)S(1)} %get-tuple-element.23), channel_id=1, source_target_pairs={{0,3},{1,2},{2,1},{3,0},{4,7},{5,6},{6,5},{7,4},{8,11},{9,10},{10,... | collective-permute-start | bytes 196616 | tf_op jit(solution)/shard_map/ppermute | solution.py:62
  10.3 4.6 %collective-permute-start.3 = (f16[256,128]{1,0:T(8,128)(2,1)S(1)}, f16[256,128]{1,0:T(8,128)(2,1)S(1)}, u32[]{:S(2)}, u32[]{:S(2)}) collective-permute-start(f16[256,128]{1,0:T(8,128)(2,1)S(1)} %get-tuple-element.22), channel_id=1, source_target_pairs={{0,7},{1,6},{2,5},{3,4},{4,3},{5,2},{6,1},{7,0},{8,15},{9,14},{10,... | collective-permute-start | bytes 196616 | tf_op jit(solution)/shard_map/ppermute | solution.py:62
  11.2 8.9 %copy-start = (s32[8]{0:T(128)S(1)}, s32[8]{0:T(128)}, u32[]{:S(2)}) copy-start(s32[8]{0:T(128)} %first_ref.3) | copy-start | bytes 100
  11.2 8.9 %copy-start.1 = (s32[8]{0:T(128)S(1)}, s32[8]{0:T(128)}, u32[]{:S(2)}) copy-start(s32[8]{0:T(128)} %count_ref.3) | copy-start | bytes 100
  11.3 8.9 %copy-start.2 = (f32[128]{0:T(128)S(1)}, f32[128]{0:T(128)}, u32[]{:S(2)}) copy-start(f32[128]{0:T(128)} %gain_ref.1) | copy-start | bytes 1540
  14.9 5.3 %collective-permute-start.4 = (f16[128,128]{1,0:T(8,128)(2,1)S(1)}, f16[128,128]{1,0:T(8,128)(2,1)S(1)}, u32[]{:S(2)}, u32[]{:S(2)}) collective-permute-start(f16[128,128]{1,0:T(8,128)(2,1)S(1)} %get-tuple-element.24), channel_id=1, source_target_pairs={{0,9},{1,8},{2,11},{3,10},{4,13},{5,12},{6,15},{7,14},{8,1},{9,0},... | collective-permute-start | bytes 98312 | tf_op jit(solution)/shard_map/ppermute | solution.py:62
  17.9 17.7 %slice-start = ((s8[8388608]{0:T(1024)(128)(4,1)}), s8[4194304]{0:T(1024)(128)(4,1)S(1)}, s32[]{:S(2)}) async-start(s8[8388608]{0:T(1024)(128)(4,1)} %bitcast.3), calls=%async_computation | async-start | bytes 8388608
  20.2 15.4 %slice-start.1 = ((s8[8388608]{0:T(1024)(128)(4,1)}), s8[4194304]{0:T(1024)(128)(4,1)S(1)}, s32[]{:S(2)}) async-start(s8[8388608]{0:T(1024)(128)(4,1)} %bitcast.3), calls=%async_computation.1 | async-start | bytes 8388608
  22.6 5.2 %collective-permute-start.5 = (bf16[1,144,128]{2,1,0:T(8,128)(2,1)S(1)}, bf16[1,144,128]{2,1,0:T(8,128)(2,1)S(1)}, u32[]{:S(2)}, u32[]{:S(2)}) collective-permute-start(bf16[1,144,128]{2,1,0:T(8,128)(2,1)S(1)} %bitcast.5), channel_id=1, source_target_pairs={{0,9},{1,8},{2,11},{3,10},{4,13},{5,12},{6,15},{7,14},{8,1},{9,0},... | collective-permute-start | bytes 110600 | tf_op jit(solution)/shard_map/ppermute | solution.py:62
  27.8 4.6 %collective-permute-start.6 = (bf16[2,144,128]{2,1,0:T(8,128)(2,1)S(1)}, bf16[2,144,128]{2,1,0:T(8,128)(2,1)S(1)}, u32[]{:S(2)}, u32[]{:S(2)}) collective-permute-start(bf16[2,144,128]{2,1,0:T(8,128)(2,1)S(1)} %pad_maximum_fusion), channel_id=1, source_target_pairs={{0,4},{1,5},{2,6},{3,7},{4,0},{5,1},{6,2},{7,3},{8,12},{9,13},{10,... | collective-permute-start | bytes 221192 | tf_op jit(solution)/shard_map/ppermute | solution.py:62
  27.9 4.5 %collective-permute-start.7 = (bf16[2,144,128]{2,1,0:T(8,128)(2,1)S(1)}, bf16[2,144,128]{2,1,0:T(8,128)(2,1)S(1)}, u32[]{:S(2)}, u32[]{:S(2)}) collective-permute-start(bf16[2,144,128]{2,1,0:T(8,128)(2,1)S(1)} %pad_maximum_fusion), channel_id=1, source_target_pairs={{0,3},{1,2},{2,1},{3,0},{4,7},{5,6},{6,5},{7,4},{8,11},{9,10},{10,... | collective-permute-start | bytes 221192 | tf_op jit(solution)/shard_map/ppermute | solution.py:62
  28.9 5.0 %collective-permute-start.8 = (bf16[2,144,128]{2,1,0:T(8,128)(2,1)S(1)}, bf16[2,144,128]{2,1,0:T(8,128)(2,1)S(1)}, u32[]{:S(2)}, u32[]{:S(2)}) collective-permute-start(bf16[2,144,128]{2,1,0:T(8,128)(2,1)S(1)} %pad_maximum_fusion), channel_id=1, source_target_pairs={{0,7},{1,6},{2,5},{3,4},{4,3},{5,2},{6,1},{7,0},{8,15},{9,14},{10,... | collective-permute-start | bytes 221192 | tf_op jit(solution)/shard_map/ppermute | solution.py:62
  33.9 1.6 %collective-permute-start.9 = (bf16[8,144,128]{2,1,0:T(8,128)(2,1)S(1)}, bf16[8,144,128]{2,1,0:T(8,128)(2,1)S(1)}, u32[]{:S(2)}, u32[]{:S(2)}) collective-permute-start(bf16[8,144,128]{2,1,0:T(8,128)(2,1)S(1)} %get-tuple-element.26), channel_id=1, source_target_pairs={{0,1},{1,0},{2,3},{3,2},{4,5},{5,4},{6,7},{7,6},{8,9},{9,8},{10,11... | collective-permute-start | bytes 884744 | tf_op jit(solution)/shard_map/ppermute | solution.py:62

commit v5 on v4

--- a/solution.py
+++ b/solution.py
@@ -160,8 +160,16 @@
 
 
 def attend_kernel(
-    kv_heads, group, steps, query_ref, gain_ref, keys_ref, values_ref, first_ref, count_ref, mask_ref, out_ref
+    kv_heads, group, steps, query_ref, gain_ref, keys_ref, values_ref, first_in, count_in, mask_in,
+    out_ref, first_ref, count_ref, mask_ref, sems
 ):
+    copies = [
+        pltpu.make_async_copy(first_in, first_ref, sems.at[0]),
+        pltpu.make_async_copy(count_in, count_ref, sems.at[1]),
+        pltpu.make_async_copy(mask_in, mask_ref, sems.at[2]),
+    ]
+    for copy in copies:
+        copy.start()
     head_size = gain_ref.shape[-1]
     kv_width = kv_heads * head_size
     join = 2 if kv_heads % 2 == 0 else 1
@@ -170,15 +178,6 @@
     mean = jnp.mean(query * query, axis=1, keepdims=True)
     normed = (query * lax.rsqrt(mean + EPSILON) * gain_ref[...]).astype(BF16)
     me = lax.axis_index(AXIS)
-    rows = first_ref.shape[0]
-
-    def find(row, carry):
-        owner, tile = carry
-        offset = me - first_ref[row]
-        inside = (offset >= 0) & (offset < count_ref[row])
-        return jnp.where(inside, row, owner), jnp.where(inside, offset, tile)
-
-    owner, tile = lax.fori_loop(0, rows, find, (jnp.int32(0), jnp.int32(0)), unroll=rows <= 16)
     size = steps * group
     row_in_tile = lax.broadcasted_iota(jnp.int32, (size, head_size), 0)
     lane = lax.broadcasted_iota(jnp.int32, (size, head_size), 1)
@@ -221,6 +220,17 @@
             stats = jnp.where(
                 here, jnp.where(lane < 3 * kv_heads, top[rows_here], total[rows_here]), stats
             )
+    for copy in copies:
+        copy.wait()
+    rows = first_ref.shape[0]
+
+    def find(row, carry):
+        owner, tile = carry
+        offset = me - first_ref[row]
+        inside = (offset >= 0) & (offset < count_ref[row])
+        return jnp.where(inside, row, owner), jnp.where(inside, offset, tile)
+
+    owner, tile = lax.fori_loop(0, rows, find, (jnp.int32(0), jnp.int32(0)), unroll=rows <= 16)
     live = jnp.zeros((size, head_size), jnp.bool_)
     for s in range(steps):
         alive = (tile == 0) | (mask_ref[owner, s, tile] == 1)
@@ -253,12 +263,15 @@
     )
     stats[0] = whole
     stats[1] = pltpu.roll(whole, head_size - 3 * kv_heads, 1)
+    first = first_ref[...].reshape(1, rows)
+    count = count_ref[...].reshape(1, rows)
     pairs = rows * steps
     masks = [order.index(1 << i) for i in range(slots.bit_length() - 1)]
 
     def one_row(row, carry):
-        begin = first_ref[row]
-        length = count_ref[row]
+        here = (lax.broadcasted_iota(jnp.int32, (1, rows), 1) == row).astype(jnp.int32)
+        begin = jnp.sum(first * here)
+        length = jnp.sum(count * here)
         places = [
             combine_bits(me ^ (begin + jnp.minimum(k, length - 1)), masks) for k in range(max_tiles)
         ]
@@ -358,8 +371,14 @@
     tile = pl.pallas_call(
         functools.partial(attend_kernel, kv_heads, group, steps),
         out_shape=struct((block, head_size), BF16),
-        in_specs=[VMEM] * 4 + [SMEM] * 3,
+        in_specs=[VMEM] * 7,
         out_specs=VMEM,
+        scratch_shapes=[
+            pltpu.SMEM(image_first_slot.shape, jnp.int32),
+            pltpu.SMEM(tile_count.shape, jnp.int32),
+            pltpu.SMEM(cross_tile_mask.shape, jnp.int32),
+            pltpu.SemaphoreType.DMA((3,)),
+        ],
         compiler_params=params(6),
     )(total, query_gain, *cache, image_first_slot, tile_count, cross_tile_mask)
     gathered = tile[None]
@@ -367,16 +386,17 @@
         gathered = jnp.concatenate(
             [gathered] + [exchange(gathered, step, devices) for step in offsets(group_bits)[1:]], axis=0
         )
+    scratch = 4 * head_size * (2 * devices * steps * group + heads * rows * steps)
     return pl.pallas_call(
         functools.partial(finish_kernel, order, kv_heads, group, steps, cross_tile_mask.shape[2]),
         out_shape=struct((rows, steps, output_weight.shape[1]), BF16),
-        in_specs=[VMEM, SMEM, SMEM, VMEM, VMEM],
+        in_specs=[VMEM] * 5,
         out_specs=VMEM,
         scratch_shapes=[
             pltpu.VMEM((2, devices * steps * group, head_size), F32),
             pltpu.VMEM((heads * rows * steps, head_size), F32),
         ],
-        compiler_params=params(8),
+        compiler_params=params(6 + (2 * scratch >> 20)),
     )(gate, image_first_slot, tile_count, gathered, output_weight)
 
 

time: 38.7 us -> 37.7 us (0.974)
  Pallas kernels: 14 us -> 13 us
    pallas_call x1, Pallas kernels: 2.34 us -> 1.78 us  [body(): pl.pallas_call(functools.partial(attend_kernel, kv_heads, group, steps),...]
    pallas_call x1, Pallas kernels: 2.9 us -> 2.5 us  [body(): pl.pallas_call(functools.partial(finish_kernel, order, kv_heads, group, s...]
where the time goes in v5:
time: 37.7 us; the launch traced here: 37.6 us
  starting transfers between devices  13.3 us (35%)
  Pallas kernels  13 us (34%)
  waiting for transfers between devices  9.87 us (26%)
  between operations  0.86 us (2%)
    ppermute x10, starting transfers between devices, exchange(): lax.ppermute(array, AXIS, [(i, i ^ difference) for i in range(count)])  13.3 us
    ppermute x10, waiting for transfers between devices, exchange(): lax.ppermute(array, AXIS, [(i, i ^ difference) for i in range(count)])  9.87 us
    pallas_call x2, Pallas kernels, fetch(): pl.pallas_call(functools.partial(fetch_kernel, part), out_shape=[struct((...  4.68 us
    pallas_call x1, Pallas kernels, body(): pl.pallas_call(functools.partial(project_kernel, order, chunks, kv_heads,...  4.09 us
    pallas_call x1, Pallas kernels, body(): pl.pallas_call(functools.partial(finish_kernel, order, kv_heads, group, s...  2.5 us
    pallas_call x1, Pallas kernels, body(): pl.pallas_call(functools.partial(attend_kernel, kv_heads, group, steps),...  1.78 us
  transfers between devices with their start and end apart: 10, of which 8 were waited for; matrix products, arithmetic and copies ran while one was open for 0% of the time, Pallas kernels for 12%

profile of v5, /device:TPU:0, one launch (start us, length us, event | category | flops | bytes accessed | tf_op | source)
XLA Modules:
  0.0 37.6 jit_solution(5259910537557813753)
XLA Ops:
  0.0 4.1 %shard_map.91 = (f32[1024,128]{1,0:T(8,128)S(1)}, f32[1024,128]{1,0:T(8,128)S(1)}) custom-call(bf16[8,2,512]{2,1,0:T(2,128)(2,1)} %x_hbm.1, bf16[512,8192]{1,0:T(8,128)(2,1)} %weight_hbm.1, s32[8]{0:T(128)} %first_ref.1, s32[8]{0:T(128)} %count_ref.1), custom_call_target="tpu_custom_call" | custom-call | tf_op jit(solution)/shard_map/pallas_call | solution.py:343
  4.1 0.0 copy-start.3
  4.1 0.5 %collective-permute-start = (f32[1024,128]{1,0:T(8,128)S(1)}, f32[1024,128]{1,0:T(8,128)S(1)}, u32[]{:S(2)}, u32[]{:S(2)}) collective-permute-start(f32[1024,128]{1,0:T(8,128)S(1)} %get-tuple-element.13), channel_id=1, source_target_pairs={{0,1},{1,0},{2,3},{3,2},{4,5},{5,4},{6,7},{7,6},{8,9},{9,8},{10,11... | collective-permute-start | bytes 1572872 | tf_op jit(solution)/shard_map/ppermute | solution.py:62
  4.6 1.5 %collective-permute-done = f32[1024,128]{1,0:T(8,128)S(1)} collective-permute-done((f32[1024,128]{1,0:T(8,128)S(1)}, f32[1024,128]{1,0:T(8,128)S(1)}, u32[]{:S(2)}, u32[]{:S(2)}) %collective-permute-start) | collective-permute-done | bytes 524320 | tf_op jit(solution)/shard_map/ppermute | solution.py:62
  6.2 0.1 fusion
  6.3 3.0 %collective-permute-start.1 = (f16[256,128]{1,0:T(8,128)(2,1)S(1)}, f16[256,128]{1,0:T(8,128)(2,1)S(1)}, u32[]{:S(2)}, u32[]{:S(2)}) collective-permute-start(f16[256,128]{1,0:T(8,128)(2,1)S(1)} %get-tuple-element.21), channel_id=1, source_target_pairs={{0,4},{1,5},{2,6},{3,7},{4,0},{5,1},{6,2},{7,3},{8,12},{9,13},{10,... | collective-permute-start | bytes 196616 | tf_op jit(solution)/shard_map/ppermute | solution.py:62
  9.3 1.0 %collective-permute-start.2 = (f16[256,128]{1,0:T(8,128)(2,1)S(1)}, f16[256,128]{1,0:T(8,128)(2,1)S(1)}, u32[]{:S(2)}, u32[]{:S(2)}) collective-permute-start(f16[256,128]{1,0:T(8,128)(2,1)S(1)} %get-tuple-element.23), channel_id=1, source_target_pairs={{0,3},{1,2},{2,1},{3,0},{4,7},{5,6},{6,5},{7,4},{8,11},{9,10},{10,... | collective-permute-start | bytes 196616 | tf_op jit(solution)/shard_map/ppermute | solution.py:62
  10.3 0.3 collective-permute-start.3
  11.2 0.0 copy-start
  11.2 0.0 copy-start.1
  11.3 0.0 copy-start.2
  11.3 2.6 %shard_map.92 = (bf16[1,1601,1024]{2,1,0:T(8,128)(2,1)S(1)}, f32[256,128]{1,0:T(8,128)S(1)}, f32[8,128]{1,0:T(8,128)}) custom-call(bf16[1,1601,2048]{2,1,0:T(8,128)(2,1)} %cache_hbm.3, f32[256,128]{1,0:T(8,128)S(1)} %slice.28.before_ref, f32[1]{0:T(128)S(6)} %copy.24.gate_ref), custom_call_target="tpu_custom_call", output_to_operand_aliasing={{1}: (1, {})} | custom-call | bytes 3278848 | tf_op jit(solution)/shard_map/pallas_call | solution.py:146
  13.8 0.0 collective-permute-done.1
  13.9 0.3 collective-permute-done.2
  14.1 0.7 %collective-permute-done.3 = f16[256,128]{1,0:T(8,128)(2,1)S(1)} collective-permute-done((f16[256,128]{1,0:T(8,128)(2,1)S(1)}, f16[256,128]{1,0:T(8,128)(2,1)S(1)}, u32[]{:S(2)}, u32[]{:S(2)}) %collective-permute-start.3) | collective-permute-done | bytes 65568 | tf_op jit(solution)/shard_map/ppermute | solution.py:62
  14.9 2.9 %collective-permute-start.4 = (f16[128,128]{1,0:T(8,128)(2,1)S(1)}, f16[128,128]{1,0:T(8,128)(2,1)S(1)}, u32[]{:S(2)}, u32[]{:S(2)}) collective-permute-start(f16[128,128]{1,0:T(8,128)(2,1)S(1)} %get-tuple-element.24), channel_id=1, source_target_pairs={{0,9},{1,8},{2,11},{3,10},{4,13},{5,12},{6,15},{7,14},{8,1},{9,0},... | collective-permute-start | bytes 98312 | tf_op jit(solution)/shard_map/ppermute | solution.py:62
  17.8 0.1 copy.12.mask_in
  17.9 2.1 %shard_map.93 = (bf16[1,1601,1024]{2,1,0:T(8,128)(2,1)S(1)}, f32[128,128]{1,0:T(8,128)S(1)}, f32[8,128]{1,0:T(8,128)S(1)}) custom-call(bf16[1,1601,2048]{2,1,0:T(8,128)(2,1)} %cache_hbm.3, f32[128,128]{1,0:T(8,128)S(1)} %get-tuple-element.25.before_ref, f32[1]{0:T(128)S(6)} %copy.24.gate_ref), custom_call_target="tpu_custom_call", output_to_operand_aliasing={{1}: (1, {})} | custom-call | bytes 3278848 | tf_op jit(solution)/shard_map/pallas_call | solution.py:146
  20.0 0.1 collective-permute-done.4
  20.2 0.0 slice-start.1
  20.2 1.8 %shard_map.94 = bf16[144,128]{1,0:T(8,128)(2,1)S(1)} custom-call(f32[128,128]{1,0:T(8,128)S(1)} %convert_add_fusion.1.query_ref, f32[128]{0:T(128)S(1)} %copy-done.2, bf16[1,1601,1024]{2,1,0:T(8,128)(2,1)S(1)} %get-tuple-element.17.keys_ref, bf16[1,1601,1024]{2,1,0:T(8,128)(2,1)S(1)} %get-tuple-element.18.values_ref, s32[8]{0:T(128)S(1)} %copy-done, ...), custom_call_target="tpu_custom_call" | custom-call | tf_op jit(solution)/shard_map/pallas_call | solution.py:371
  22.0 2.0 %collective-permute-start.5 = (bf16[1,144,128]{2,1,0:T(8,128)(2,1)S(1)}, bf16[1,144,128]{2,1,0:T(8,128)(2,1)S(1)}, u32[]{:S(2)}, u32[]{:S(2)}) collective-permute-start(bf16[1,144,128]{2,1,0:T(8,128)(2,1)S(1)} %bitcast.5), channel_id=1, source_target_pairs={{0,9},{1,8},{2,11},{3,10},{4,13},{5,12},{6,15},{7,14},{8,1},{9,0},... | collective-permute-start | bytes 110600 | tf_op jit(solution)/shard_map/ppermute | solution.py:62
  24.0 3.3 %collective-permute-done.5 = bf16[1,144,128]{2,1,0:T(8,128)(2,1)S(1)} collective-permute-done((bf16[1,144,128]{2,1,0:T(8,128)(2,1)S(1)}, bf16[1,144,128]{2,1,0:T(8,128)(2,1)S(1)}, u32[]{:S(2)}, u32[]{:S(2)}) %collective-permute-start.5) | collective-permute-done | bytes 36896 | tf_op jit(solution)/shard_map/ppermute | solution.py:62
  27.2 0.1 collective-permute-start.6
  27.3 1.0 %collective-permute-start.7 = (bf16[2,144,128]{2,1,0:T(8,128)(2,1)S(1)}, bf16[2,144,128]{2,1,0:T(8,128)(2,1)S(1)}, u32[]{:S(2)}, u32[]{:S(2)}) collective-permute-start(bf16[2,144,128]{2,1,0:T(8,128)(2,1)S(1)} %pad_maximum_fusion), channel_id=1, source_target_pairs={{0,3},{1,2},{2,1},{3,0},{4,7},{5,6},{6,5},{7,4},{8,11},{9,10},{10,... | collective-permute-start | bytes 221192 | tf_op jit(solution)/shard_map/ppermute | solution.py:62
  28.3 2.2 %collective-permute-start.8 = (bf16[2,144,128]{2,1,0:T(8,128)(2,1)S(1)}, bf16[2,144,128]{2,1,0:T(8,128)(2,1)S(1)}, u32[]{:S(2)}, u32[]{:S(2)}) collective-permute-start(bf16[2,144,128]{2,1,0:T(8,128)(2,1)S(1)} %pad_maximum_fusion), channel_id=1, source_target_pairs={{0,7},{1,6},{2,5},{3,4},{4,3},{5,2},{6,1},{7,0},{8,15},{9,14},{10,... | collective-permute-start | bytes 221192 | tf_op jit(solution)/shard_map/ppermute | solution.py:62
  30.5 1.3 %collective-permute-done.6 = bf16[2,144,128]{2,1,0:T(8,128)(2,1)S(1)} collective-permute-done((bf16[2,144,128]{2,1,0:T(8,128)(2,1)S(1)}, bf16[2,144,128]{2,1,0:T(8,128)(2,1)S(1)}, u32[]{:S(2)}, u32[]{:S(2)}) %collective-permute-start.6) | collective-permute-done | bytes 73760 | tf_op jit(solution)/shard_map/ppermute | solution.py:62
  31.8 0.0 collective-permute-done.7
  31.9 1.5 %collective-permute-done.8 = bf16[2,144,128]{2,1,0:T(8,128)(2,1)S(1)} collective-permute-done((bf16[2,144,128]{2,1,0:T(8,128)(2,1)S(1)}, bf16[2,144,128]{2,1,0:T(8,128)(2,1)S(1)}, u32[]{:S(2)}, u32[]{:S(2)}) %collective-permute-start.8) | collective-permute-done | bytes 73760 | tf_op jit(solution)/shard_map/ppermute | solution.py:62
  33.4 0.4 %collective-permute-start.9 = (bf16[8,144,128]{2,1,0:T(8,128)(2,1)S(1)}, bf16[8,144,128]{2,1,0:T(8,128)(2,1)S(1)}, u32[]{:S(2)}, u32[]{:S(2)}) collective-permute-start(bf16[8,144,128]{2,1,0:T(8,128)(2,1)S(1)} %get-tuple-element.26), channel_id=1, source_target_pairs={{0,1},{1,0},{2,3},{3,2},{4,5},{5,4},{6,7},{7,6},{8,9},{9,8},{10,11... | collective-permute-start | bytes 884744 | tf_op jit(solution)/shard_map/ppermute | solution.py:62
  33.8 1.2 %collective-permute-done.9 = bf16[8,144,128]{2,1,0:T(8,128)(2,1)S(1)} collective-permute-done((bf16[8,144,128]{2,1,0:T(8,128)(2,1)S(1)}, bf16[8,144,128]{2,1,0:T(8,128)(2,1)S(1)}, u32[]{:S(2)}, u32[]{:S(2)}) %collective-permute-start.9) | collective-permute-done | bytes 294944 | tf_op jit(solution)/shard_map/ppermute | solution.py:62
  35.1 2.5 %shard_map.95 = bf16[8,2,512]{2,1,0:T(2,128)(2,1)} custom-call(f32[8,128]{1,0:T(8,128)S(1)} %get-tuple-element.15.gate_ref, s32[8]{0:T(128)S(1)} %copy-done, s32[8]{0:T(128)S(1)} %copy-done.1, bf16[16,144,128]{2,1,0:T(8,128)(2,1)S(1)} %constant_dynamic-update-slice_fusion.5.tiles_ref, bf16[8192,512]{1,0:T(8,128)(2,1)S(1)} %bitcast.4), custom_call_target="tpu_custom_call" | custom-call | tf_op jit(solution)/shard_map/pallas_call | solution.py:390
  (20 shorter events, 0.3 us)
Async XLA Ops:
  4.1 13.7 %copy-start.3 = (s32[8,2,4]{0,2,1:T(4,128)S(1)}, s32[8,2,4]{0,2,1:T(4,128)}, u32[]{:S(2)}) copy-start(s32[8,2,4]{0,2,1:T(4,128)} %param.15) | copy-start | bytes 772
  4.1 2.1 %collective-permute-start = (f32[1024,128]{1,0:T(8,128)S(1)}, f32[1024,128]{1,0:T(8,128)S(1)}, u32[]{:S(2)}, u32[]{:S(2)}) collective-permute-start(f32[1024,128]{1,0:T(8,128)S(1)} %get-tuple-element.13), channel_id=1, source_target_pairs={{0,1},{1,0},{2,3},{3,2},{4,5},{5,4},{6,7},{7,6},{8,9},{9,8},{10,11... | collective-permute-start | bytes 1572872 | tf_op jit(solution)/shard_map/ppermute | solution.py:62
  6.3 7.6 %collective-permute-start.1 = (f16[256,128]{1,0:T(8,128)(2,1)S(1)}, f16[256,128]{1,0:T(8,128)(2,1)S(1)}, u32[]{:S(2)}, u32[]{:S(2)}) collective-permute-start(f16[256,128]{1,0:T(8,128)(2,1)S(1)} %get-tuple-element.21), channel_id=1, source_target_pairs={{0,4},{1,5},{2,6},{3,7},{4,0},{5,1},{6,2},{7,3},{8,12},{9,13},{10,... | collective-permute-start | bytes 196616 | tf_op jit(solution)/shard_map/ppermute | solution.py:62
  9.3 4.8 %collective-permute-start.2 = (f16[256,128]{1,0:T(8,128)(2,1)S(1)}, f16[256,128]{1,0:T(8,128)(2,1)S(1)}, u32[]{:S(2)}, u32[]{:S(2)}) collective-permute-start(f16[256,128]{1,0:T(8,128)(2,1)S(1)} %get-tuple-element.23), channel_id=1, source_target_pairs={{0,3},{1,2},{2,1},{3,0},{4,7},{5,6},{6,5},{7,4},{8,11},{9,10},{10,... | collective-permute-start | bytes 196616 | tf_op jit(solution)/shard_map/ppermute | solution.py:62
  10.3 4.6 %collective-permute-start.3 = (f16[256,128]{1,0:T(8,128)(2,1)S(1)}, f16[256,128]{1,0:T(8,128)(2,1)S(1)}, u32[]{:S(2)}, u32[]{:S(2)}) collective-permute-start(f16[256,128]{1,0:T(8,128)(2,1)S(1)} %get-tuple-element.22), channel_id=1, source_target_pairs={{0,7},{1,6},{2,5},{3,4},{4,3},{5,2},{6,1},{7,0},{8,15},{9,14},{10,... | collective-permute-start | bytes 196616 | tf_op jit(solution)/shard_map/ppermute | solution.py:62
  11.2 8.9 %copy-start = (s32[8]{0:T(128)S(1)}, s32[8]{0:T(128)}, u32[]{:S(2)}) copy-start(s32[8]{0:T(128)} %first_ref.1) | copy-start | bytes 100
  11.2 8.9 %copy-start.1 = (s32[8]{0:T(128)S(1)}, s32[8]{0:T(128)}, u32[]{:S(2)}) copy-start(s32[8]{0:T(128)} %count_ref.1) | copy-start | bytes 100
  11.3 8.9 %copy-start.2 = (f32[128]{0:T(128)S(1)}, f32[128]{0:T(128)}, u32[]{:S(2)}) copy-start(f32[128]{0:T(128)} %gain_ref.1) | copy-start | bytes 1540
  14.9 5.3 %collective-permute-start.4 = (f16[128,128]{1,0:T(8,128)(2,1)S(1)}, f16[128,128]{1,0:T(8,128)(2,1)S(1)}, u32[]{:S(2)}, u32[]{:S(2)}) collective-permute-start(f16[128,128]{1,0:T(8,128)(2,1)S(1)} %get-tuple-element.24), channel_id=1, source_target_pairs={{0,9},{1,8},{2,11},{3,10},{4,13},{5,12},{6,15},{7,14},{8,1},{9,0},... | collective-permute-start | bytes 98312 | tf_op jit(solution)/shard_map/ppermute | solution.py:62
  17.9 17.2 %slice-start = ((s8[8388608]{0:T(1024)(128)(4,1)}), s8[4194304]{0:T(1024)(128)(4,1)S(1)}, s32[]{:S(2)}) async-start(s8[8388608]{0:T(1024)(128)(4,1)} %bitcast.3), calls=%async_computation | async-start | bytes 8388608
  20.2 14.9 %slice-start.1 = ((s8[8388608]{0:T(1024)(128)(4,1)}), s8[4194304]{0:T(1024)(128)(4,1)S(1)}, s32[]{:S(2)}) async-start(s8[8388608]{0:T(1024)(128)(4,1)} %bitcast.3), calls=%async_computation.1 | async-start | bytes 8388608
  22.0 5.2 %collective-permute-start.5 = (bf16[1,144,128]{2,1,0:T(8,128)(2,1)S(1)}, bf16[1,144,128]{2,1,0:T(8,128)(2,1)S(1)}, u32[]{:S(2)}, u32[]{:S(2)}) collective-permute-start(bf16[1,144,128]{2,1,0:T(8,128)(2,1)S(1)} %bitcast.5), channel_id=1, source_target_pairs={{0,9},{1,8},{2,11},{3,10},{4,13},{5,12},{6,15},{7,14},{8,1},{9,0},... | collective-permute-start | bytes 110600 | tf_op jit(solution)/shard_map/ppermute | solution.py:62
  27.2 4.6 %collective-permute-start.6 = (bf16[2,144,128]{2,1,0:T(8,128)(2,1)S(1)}, bf16[2,144,128]{2,1,0:T(8,128)(2,1)S(1)}, u32[]{:S(2)}, u32[]{:S(2)}) collective-permute-start(bf16[2,144,128]{2,1,0:T(8,128)(2,1)S(1)} %pad_maximum_fusion), channel_id=1, source_target_pairs={{0,4},{1,5},{2,6},{3,7},{4,0},{5,1},{6,2},{7,3},{8,12},{9,13},{10,... | collective-permute-start | bytes 221192 | tf_op jit(solution)/shard_map/ppermute | solution.py:62
  27.3 4.5 %collective-permute-start.7 = (bf16[2,144,128]{2,1,0:T(8,128)(2,1)S(1)}, bf16[2,144,128]{2,1,0:T(8,128)(2,1)S(1)}, u32[]{:S(2)}, u32[]{:S(2)}) collective-permute-start(bf16[2,144,128]{2,1,0:T(8,128)(2,1)S(1)} %pad_maximum_fusion), channel_id=1, source_target_pairs={{0,3},{1,2},{2,1},{3,0},{4,7},{5,6},{6,5},{7,4},{8,11},{9,10},{10,... | collective-permute-start | bytes 221192 | tf_op jit(solution)/shard_map/ppermute | solution.py:62
  28.3 5.0 %collective-permute-start.8 = (bf16[2,144,128]{2,1,0:T(8,128)(2,1)S(1)}, bf16[2,144,128]{2,1,0:T(8,128)(2,1)S(1)}, u32[]{:S(2)}, u32[]{:S(2)}) collective-permute-start(bf16[2,144,128]{2,1,0:T(8,128)(2,1)S(1)} %pad_maximum_fusion), channel_id=1, source_target_pairs={{0,7},{1,6},{2,5},{3,4},{4,3},{5,2},{6,1},{7,0},{8,15},{9,14},{10,... | collective-permute-start | bytes 221192 | tf_op jit(solution)/shard_map/ppermute | solution.py:62
  33.4 1.6 %collective-permute-start.9 = (bf16[8,144,128]{2,1,0:T(8,128)(2,1)S(1)}, bf16[8,144,128]{2,1,0:T(8,128)(2,1)S(1)}, u32[]{:S(2)}, u32[]{:S(2)}) collective-permute-start(bf16[8,144,128]{2,1,0:T(8,128)(2,1)S(1)} %get-tuple-element.26), channel_id=1, source_target_pairs={{0,1},{1,0},{2,3},{3,2},{4,5},{5,4},{6,7},{7,6},{8,9},{9,8},{10,11... | collective-permute-start | bytes 884744 | tf_op jit(solution)/shard_map/ppermute | solution.py:62

commit v6 on v5

--- a/solution.py
+++ b/solution.py
@@ -361,12 +361,12 @@
         steps_out = offsets(group_bits)
         size = total.shape[0] // len(steps_out)
         pieces = [total[i * size : (i + 1) * size] for i in range(len(steps_out))]
-        sent = [piece.astype(jnp.float16) for piece in pieces[1:]]
+        sent = pieces[1:]
         got = [exchange(piece, step, devices) for piece, step in zip(sent, steps_out[1:])]
         if len(cache) < 2:
             half, pieces[0], gate = fetch(image_cache, len(cache), pieces[0], output_gate)
             cache.append(half)
-        total = functools.reduce(jnp.add, [pieces[0]] + [piece.astype(F32) for piece in got])
+        total = functools.reduce(jnp.add, [pieces[0]] + got)
     block = (kv_heads + 1) * steps * group
     tile = pl.pallas_call(
         functools.partial(attend_kernel, kv_heads, group, steps),

time: 37.7 us -> 41.7 us (1.11)
  waiting for transfers between devices: 9.87 us -> 15.4 us
  starting transfers between devices: 13.3 us -> 11.9 us
    ppermute x10, waiting for transfers between devices: 9.87 us -> 15.4 us  [exchange(): lax.ppermute(array, AXIS, [(i, i ^ difference) for i in range(count)])]
    ppermute x10, starting transfers between devices: 13.3 us -> 11.9 us  [exchange(): lax.ppermute(array, AXIS, [(i, i ^ difference) for i in range(count)])]
  transfers between devices with their start and end apart: 10 -> 10, of which waited for: 8 -> 7; matrix products, arithmetic and copies ran while one was open for 0% -> 0% of each run, Pallas kernels for 12% -> 11%
where the time goes in v6:
time: 41.7 us; the launch traced here: 41.6 us
  waiting for transfers between devices  15.4 us (37%)
  Pallas kernels  13 us (31%)
  starting transfers between devices  11.9 us (29%)
  between operations  0.85 us (2%)
    ppermute x10, waiting for transfers between devices, exchange(): lax.ppermute(array, AXIS, [(i, i ^ difference) for i in range(count)])  15.4 us
    ppermute x10, starting transfers between devices, exchange(): lax.ppermute(array, AXIS, [(i, i ^ difference) for i in range(count)])  11.9 us
    pallas_call x2, Pallas kernels, fetch(): pl.pallas_call(functools.partial(fetch_kernel, part), out_shape=[struct((...  4.68 us
    pallas_call x1, Pallas kernels, body(): pl.pallas_call(functools.partial(project_kernel, order, chunks, kv_heads,...  4.09 us
    pallas_call x1, Pallas kernels, body(): pl.pallas_call(functools.partial(finish_kernel, order, kv_heads, group, s...  2.5 us
    pallas_call x1, Pallas kernels, body(): pl.pallas_call(functools.partial(attend_kernel, kv_heads, group, steps),...  1.78 us
  transfers between devices with their start and end apart: 10, of which 7 were waited for; matrix products, arithmetic and copies ran while one was open for 0% of the time, Pallas kernels for 11%

profile of v6, /device:TPU:0, one launch (start us, length us, event | category | flops | bytes accessed | tf_op | source)
XLA Modules:
  0.0 41.6 jit_solution(4802932368028050500)
XLA Ops:
  0.0 4.1 %shard_map.91 = (f32[1024,128]{1,0:T(8,128)S(1)}, f32[1024,128]{1,0:T(8,128)S(1)}) custom-call(bf16[8,2,512]{2,1,0:T(2,128)(2,1)} %x_hbm.1, bf16[512,8192]{1,0:T(8,128)(2,1)} %weight_hbm.1, s32[8]{0:T(128)} %first_ref.1, s32[8]{0:T(128)} %count_ref.1), custom_call_target="tpu_custom_call" | custom-call | tf_op jit(solution)/shard_map/pallas_call | solution.py:343
  4.1 0.0 copy-start.3
  4.1 0.5 %collective-permute-start = (f32[1024,128]{1,0:T(8,128)S(1)}, f32[1024,128]{1,0:T(8,128)S(1)}, u32[]{:S(2)}, u32[]{:S(2)}) collective-permute-start(f32[1024,128]{1,0:T(8,128)S(1)} %get-tuple-element.13), channel_id=1, source_target_pairs={{0,1},{1,0},{2,3},{3,2},{4,5},{5,4},{6,7},{7,6},{8,9},{9,8},{10,11... | collective-permute-start | bytes 1572872 | tf_op jit(solution)/shard_map/ppermute | solution.py:62
  4.6 1.5 %collective-permute-done = f32[1024,128]{1,0:T(8,128)S(1)} collective-permute-done((f32[1024,128]{1,0:T(8,128)S(1)}, f32[1024,128]{1,0:T(8,128)S(1)}, u32[]{:S(2)}, u32[]{:S(2)}) %collective-permute-start) | collective-permute-done | bytes 524320 | tf_op jit(solution)/shard_map/ppermute | solution.py:62
  6.2 0.1 add.15
  6.3 3.0 %collective-permute-start.1 = (f32[256,128]{1,0:T(8,128)S(1)}, f32[256,128]{1,0:T(8,128)S(1)}, u32[]{:S(2)}, u32[]{:S(2)}) collective-permute-start(f32[256,128]{1,0:T(8,128)S(1)} %get-tuple-element.19), channel_id=1, source_target_pairs={{0,4},{1,5},{2,6},{3,7},{4,0},{5,1},{6,2},{7,3},{8,12},{9,13},{10,... | collective-permute-start | bytes 393224 | tf_op jit(solution)/shard_map/ppermute | solution.py:62
  9.3 1.0 %collective-permute-start.2 = (f32[256,128]{1,0:T(8,128)S(1)}, f32[256,128]{1,0:T(8,128)S(1)}, u32[]{:S(2)}, u32[]{:S(2)}) collective-permute-start(f32[256,128]{1,0:T(8,128)S(1)} %get-tuple-element.21), channel_id=1, source_target_pairs={{0,3},{1,2},{2,1},{3,0},{4,7},{5,6},{6,5},{7,4},{8,11},{9,10},{10,... | collective-permute-start | bytes 393224 | tf_op jit(solution)/shard_map/ppermute | solution.py:62
  10.2 0.3 collective-permute-start.3
  11.2 0.0 copy-start
  11.2 0.0 copy-start.1
  11.2 0.0 copy-start.2
  11.2 2.6 %shard_map.92 = (bf16[1,1601,1024]{2,1,0:T(8,128)(2,1)S(1)}, f32[256,128]{1,0:T(8,128)S(1)}, f32[8,128]{1,0:T(8,128)}) custom-call(bf16[1,1601,2048]{2,1,0:T(8,128)(2,1)} %cache_hbm.3, f32[256,128]{1,0:T(8,128)S(1)} %get-tuple-element.22.before_ref, f32[1]{0:T(128)S(6)} %copy.24.gate_ref), custom_call_target="tpu_custom_call", output_to_operand_aliasing={{1}: (1, {})} | custom-call | bytes 3278848 | tf_op jit(solution)/shard_map/pallas_call | solution.py:146
  13.8 0.0 collective-permute-done.1
  13.8 4.0 %collective-permute-done.2 = f32[256,128]{1,0:T(8,128)S(1)} collective-permute-done((f32[256,128]{1,0:T(8,128)S(1)}, f32[256,128]{1,0:T(8,128)S(1)}, u32[]{:S(2)}, u32[]{:S(2)}) %collective-permute-start.2) | collective-permute-done | bytes 131104 | tf_op jit(solution)/shard_map/ppermute | solution.py:62
  17.8 0.0 collective-permute-done.3
  17.9 2.4 %collective-permute-start.4 = (f32[128,128]{1,0:T(8,128)S(1)}, f32[128,128]{1,0:T(8,128)S(1)}, u32[]{:S(2)}, u32[]{:S(2)}) collective-permute-start(f32[128,128]{1,0:T(8,128)S(1)} %get-tuple-element.23), channel_id=1, source_target_pairs={{0,9},{1,8},{2,11},{3,10},{4,13},{5,12},{6,15},{7,14},{8,1},{9,0},... | collective-permute-start | bytes 196616 | tf_op jit(solution)/shard_map/ppermute | solution.py:62
  20.3 0.1 copy.12.mask_in
  20.4 2.1 %shard_map.93 = (bf16[1,1601,1024]{2,1,0:T(8,128)(2,1)S(1)}, f32[128,128]{1,0:T(8,128)S(1)}, f32[8,128]{1,0:T(8,128)S(1)}) custom-call(bf16[1,1601,2048]{2,1,0:T(8,128)(2,1)} %cache_hbm.3, f32[128,128]{1,0:T(8,128)S(1)} %get-tuple-element.24.before_ref, f32[1]{0:T(128)S(6)} %copy.24.gate_ref), custom_call_target="tpu_custom_call", output_to_operand_aliasing={{1}: (1, {})} | custom-call | bytes 3278848 | tf_op jit(solution)/shard_map/pallas_call | solution.py:146
  22.5 1.7 %collective-permute-done.4 = f32[128,128]{1,0:T(8,128)S(1)} collective-permute-done((f32[128,128]{1,0:T(8,128)S(1)}, f32[128,128]{1,0:T(8,128)S(1)}, u32[]{:S(2)}, u32[]{:S(2)}) %collective-permute-start.4) | collective-permute-done | bytes 65568 | tf_op jit(solution)/shard_map/ppermute | solution.py:62
  24.2 0.0 slice-start.1
  24.2 1.8 %shard_map.94 = bf16[144,128]{1,0:T(8,128)(2,1)S(1)} custom-call(f32[128,128]{1,0:T(8,128)S(1)} %add.19.query_ref, f32[128]{0:T(128)S(1)} %copy-done.2, bf16[1,1601,1024]{2,1,0:T(8,128)(2,1)S(1)} %get-tuple-element.17.keys_ref, bf16[1,1601,1024]{2,1,0:T(8,128)(2,1)S(1)} %get-tuple-element.18.values_ref, s32[8]{0:T(128)S(1)} %copy-done, s32[8]{0:T(128)S(1)} %copy-done.1, ...), custom_call_target="tpu_custom_call" | custom-call | tf_op jit(solution)/shard_map/pallas_call | solution.py:371
  26.0 1.2 %collective-permute-start.5 = (bf16[1,144,128]{2,1,0:T(8,128)(2,1)S(1)}, bf16[1,144,128]{2,1,0:T(8,128)(2,1)S(1)}, u32[]{:S(2)}, u32[]{:S(2)}) collective-permute-start(bf16[1,144,128]{2,1,0:T(8,128)(2,1)S(1)} %bitcast.5), channel_id=1, source_target_pairs={{0,9},{1,8},{2,11},{3,10},{4,13},{5,12},{6,15},{7,14},{8,1},{9,0},... | collective-permute-start | bytes 110600 | tf_op jit(solution)/shard_map/ppermute | solution.py:62
  27.2 3.2 %collective-permute-done.5 = bf16[1,144,128]{2,1,0:T(8,128)(2,1)S(1)} collective-permute-done((bf16[1,144,128]{2,1,0:T(8,128)(2,1)S(1)}, bf16[1,144,128]{2,1,0:T(8,128)(2,1)S(1)}, u32[]{:S(2)}, u32[]{:S(2)}) %collective-permute-start.5) | collective-permute-done | bytes 36896 | tf_op jit(solution)/shard_map/ppermute | solution.py:62
  30.4 0.1 collective-permute-start.6
  30.5 1.7 %collective-permute-start.7 = (bf16[2,144,128]{2,1,0:T(8,128)(2,1)S(1)}, bf16[2,144,128]{2,1,0:T(8,128)(2,1)S(1)}, u32[]{:S(2)}, u32[]{:S(2)}) collective-permute-start(bf16[2,144,128]{2,1,0:T(8,128)(2,1)S(1)} %pad_maximum_fusion), channel_id=1, source_target_pairs={{0,3},{1,2},{2,1},{3,0},{4,7},{5,6},{6,5},{7,4},{8,11},{9,10},{10,... | collective-permute-start | bytes 221192 | tf_op jit(solution)/shard_map/ppermute | solution.py:62
  32.2 1.5 %collective-permute-start.8 = (bf16[2,144,128]{2,1,0:T(8,128)(2,1)S(1)}, bf16[2,144,128]{2,1,0:T(8,128)(2,1)S(1)}, u32[]{:S(2)}, u32[]{:S(2)}) collective-permute-start(bf16[2,144,128]{2,1,0:T(8,128)(2,1)S(1)} %pad_maximum_fusion), channel_id=1, source_target_pairs={{0,7},{1,6},{2,5},{3,4},{4,3},{5,2},{6,1},{7,0},{8,15},{9,14},{10,... | collective-permute-start | bytes 221192 | tf_op jit(solution)/shard_map/ppermute | solution.py:62
  33.7 1.1 %collective-permute-done.6 = bf16[2,144,128]{2,1,0:T(8,128)(2,1)S(1)} collective-permute-done((bf16[2,144,128]{2,1,0:T(8,128)(2,1)S(1)}, bf16[2,144,128]{2,1,0:T(8,128)(2,1)S(1)}, u32[]{:S(2)}, u32[]{:S(2)}) %collective-permute-start.6) | collective-permute-done | bytes 73760 | tf_op jit(solution)/shard_map/ppermute | solution.py:62
  34.9 0.0 collective-permute-done.7
  34.9 2.4 %collective-permute-done.8 = bf16[2,144,128]{2,1,0:T(8,128)(2,1)S(1)} collective-permute-done((bf16[2,144,128]{2,1,0:T(8,128)(2,1)S(1)}, bf16[2,144,128]{2,1,0:T(8,128)(2,1)S(1)}, u32[]{:S(2)}, u32[]{:S(2)}) %collective-permute-start.8) | collective-permute-done | bytes 73760 | tf_op jit(solution)/shard_map/ppermute | solution.py:62
  37.4 0.3 collective-permute-start.9
  37.7 1.4 %collective-permute-done.9 = bf16[8,144,128]{2,1,0:T(8,128)(2,1)S(1)} collective-permute-done((bf16[8,144,128]{2,1,0:T(8,128)(2,1)S(1)}, bf16[8,144,128]{2,1,0:T(8,128)(2,1)S(1)}, u32[]{:S(2)}, u32[]{:S(2)}) %collective-permute-start.9) | collective-permute-done | bytes 294944 | tf_op jit(solution)/shard_map/ppermute | solution.py:62
  39.1 2.5 %shard_map.95 = bf16[8,2,512]{2,1,0:T(2,128)(2,1)} custom-call(f32[8,128]{1,0:T(8,128)S(1)} %get-tuple-element.15.gate_ref, s32[8]{0:T(128)S(1)} %copy-done, s32[8]{0:T(128)S(1)} %copy-done.1, bf16[16,144,128]{2,1,0:T(8,128)(2,1)S(1)} %constant_dynamic-update-slice_fusion.5.tiles_ref, bf16[8192,512]{1,0:T(8,128)(2,1)S(1)} %bitcast.4), custom_call_target="tpu_custom_call" | custom-call | tf_op jit(solution)/shard_map/pallas_call | solution.py:390
  (19 shorter events, 0.3 us)
Async XLA Ops:
  4.1 16.2 %copy-start.3 = (s32[8,2,4]{0,2,1:T(4,128)S(1)}, s32[8,2,4]{0,2,1:T(4,128)}, u32[]{:S(2)}) copy-start(s32[8,2,4]{0,2,1:T(4,128)} %param.15) | copy-start | bytes 772
  4.1 2.1 %collective-permute-start = (f32[1024,128]{1,0:T(8,128)S(1)}, f32[1024,128]{1,0:T(8,128)S(1)}, u32[]{:S(2)}, u32[]{:S(2)}) collective-permute-start(f32[1024,128]{1,0:T(8,128)S(1)} %get-tuple-element.13), channel_id=1, source_target_pairs={{0,1},{1,0},{2,3},{3,2},{4,5},{5,4},{6,7},{7,6},{8,9},{9,8},{10,11... | collective-permute-start | bytes 1572872 | tf_op jit(solution)/shard_map/ppermute | solution.py:62
  6.3 7.5 %collective-permute-start.1 = (f32[256,128]{1,0:T(8,128)S(1)}, f32[256,128]{1,0:T(8,128)S(1)}, u32[]{:S(2)}, u32[]{:S(2)}) collective-permute-start(f32[256,128]{1,0:T(8,128)S(1)} %get-tuple-element.19), channel_id=1, source_target_pairs={{0,4},{1,5},{2,6},{3,7},{4,0},{5,1},{6,2},{7,3},{8,12},{9,13},{10,... | collective-permute-start | bytes 393224 | tf_op jit(solution)/shard_map/ppermute | solution.py:62
  9.3 8.6 %collective-permute-start.2 = (f32[256,128]{1,0:T(8,128)S(1)}, f32[256,128]{1,0:T(8,128)S(1)}, u32[]{:S(2)}, u32[]{:S(2)}) collective-permute-start(f32[256,128]{1,0:T(8,128)S(1)} %get-tuple-element.21), channel_id=1, source_target_pairs={{0,3},{1,2},{2,1},{3,0},{4,7},{5,6},{6,5},{7,4},{8,11},{9,10},{10,... | collective-permute-start | bytes 393224 | tf_op jit(solution)/shard_map/ppermute | solution.py:62
  10.2 7.6 %collective-permute-start.3 = (f32[256,128]{1,0:T(8,128)S(1)}, f32[256,128]{1,0:T(8,128)S(1)}, u32[]{:S(2)}, u32[]{:S(2)}) collective-permute-start(f32[256,128]{1,0:T(8,128)S(1)} %get-tuple-element.20), channel_id=1, source_target_pairs={{0,7},{1,6},{2,5},{3,4},{4,3},{5,2},{6,1},{7,0},{8,15},{9,14},{10,... | collective-permute-start | bytes 393224 | tf_op jit(solution)/shard_map/ppermute | solution.py:62
  11.2 13.0 %copy-start = (s32[8]{0:T(128)S(1)}, s32[8]{0:T(128)}, u32[]{:S(2)}) copy-start(s32[8]{0:T(128)} %first_ref.1) | copy-start | bytes 100
  11.2 13.0 %copy-start.1 = (s32[8]{0:T(128)S(1)}, s32[8]{0:T(128)}, u32[]{:S(2)}) copy-start(s32[8]{0:T(128)} %count_ref.1) | copy-start | bytes 100
  11.2 13.0 %copy-start.2 = (f32[128]{0:T(128)S(1)}, f32[128]{0:T(128)}, u32[]{:S(2)}) copy-start(f32[128]{0:T(128)} %gain_ref.1) | copy-start | bytes 1540
  17.9 6.3 %collective-permute-start.4 = (f32[128,128]{1,0:T(8,128)S(1)}, f32[128,128]{1,0:T(8,128)S(1)}, u32[]{:S(2)}, u32[]{:S(2)}) collective-permute-start(f32[128,128]{1,0:T(8,128)S(1)} %get-tuple-element.23), channel_id=1, source_target_pairs={{0,9},{1,8},{2,11},{3,10},{4,13},{5,12},{6,15},{7,14},{8,1},{9,0},... | collective-permute-start | bytes 196616 | tf_op jit(solution)/shard_map/ppermute | solution.py:62
  20.4 18.7 %slice-start = ((s8[8388608]{0:T(1024)(128)(4,1)}), s8[4194304]{0:T(1024)(128)(4,1)S(1)}, s32[]{:S(2)}) async-start(s8[8388608]{0:T(1024)(128)(4,1)} %bitcast.3), calls=%async_computation | async-start | bytes 8388608
  24.2 14.9 %slice-start.1 = ((s8[8388608]{0:T(1024)(128)(4,1)}), s8[4194304]{0:T(1024)(128)(4,1)S(1)}, s32[]{:S(2)}) async-start(s8[8388608]{0:T(1024)(128)(4,1)} %bitcast.3), calls=%async_computation.1 | async-start | bytes 8388608
  26.0 4.4 %collective-permute-start.5 = (bf16[1,144,128]{2,1,0:T(8,128)(2,1)S(1)}, bf16[1,144,128]{2,1,0:T(8,128)(2,1)S(1)}, u32[]{:S(2)}, u32[]{:S(2)}) collective-permute-start(bf16[1,144,128]{2,1,0:T(8,128)(2,1)S(1)} %bitcast.5), channel_id=1, source_target_pairs={{0,9},{1,8},{2,11},{3,10},{4,13},{5,12},{6,15},{7,14},{8,1},{9,0},... | collective-permute-start | bytes 110600 | tf_op jit(solution)/shard_map/ppermute | solution.py:62
  30.4 4.4 %collective-permute-start.6 = (bf16[2,144,128]{2,1,0:T(8,128)(2,1)S(1)}, bf16[2,144,128]{2,1,0:T(8,128)(2,1)S(1)}, u32[]{:S(2)}, u32[]{:S(2)}) collective-permute-start(bf16[2,144,128]{2,1,0:T(8,128)(2,1)S(1)} %pad_maximum_fusion), channel_id=1, source_target_pairs={{0,4},{1,5},{2,6},{3,7},{4,0},{5,1},{6,2},{7,3},{8,12},{9,13},{10,... | collective-permute-start | bytes 221192 | tf_op jit(solution)/shard_map/ppermute | solution.py:62
  30.5 4.4 %collective-permute-start.7 = (bf16[2,144,128]{2,1,0:T(8,128)(2,1)S(1)}, bf16[2,144,128]{2,1,0:T(8,128)(2,1)S(1)}, u32[]{:S(2)}, u32[]{:S(2)}) collective-permute-start(bf16[2,144,128]{2,1,0:T(8,128)(2,1)S(1)} %pad_maximum_fusion), channel_id=1, source_target_pairs={{0,3},{1,2},{2,1},{3,0},{4,7},{5,6},{6,5},{7,4},{8,11},{9,10},{10,... | collective-permute-start | bytes 221192 | tf_op jit(solution)/shard_map/ppermute | solution.py:62
  32.2 5.2 %collective-permute-start.8 = (bf16[2,144,128]{2,1,0:T(8,128)(2,1)S(1)}, bf16[2,144,128]{2,1,0:T(8,128)(2,1)S(1)}, u32[]{:S(2)}, u32[]{:S(2)}) collective-permute-start(bf16[2,144,128]{2,1,0:T(8,128)(2,1)S(1)} %pad_maximum_fusion), channel_id=1, source_target_pairs={{0,7},{1,6},{2,5},{3,4},{4,3},{5,2},{6,1},{7,0},{8,15},{9,14},{10,... | collective-permute-start | bytes 221192 | tf_op jit(solution)/shard_map/ppermute | solution.py:62
  37.4 1.6 %collective-permute-start.9 = (bf16[8,144,128]{2,1,0:T(8,128)(2,1)S(1)}, bf16[8,144,128]{2,1,0:T(8,128)(2,1)S(1)}, u32[]{:S(2)}, u32[]{:S(2)}) collective-permute-start(bf16[8,144,128]{2,1,0:T(8,128)(2,1)S(1)} %get-tuple-element.25), channel_id=1, source_target_pairs={{0,1},{1,0},{2,3},{3,2},{4,5},{5,4},{6,7},{7,6},{8,9},{9,8},{10,11... | collective-permute-start | bytes 884744 | tf_op jit(solution)/shard_map/ppermute | solution.py:62

commit v7 on v6

--- a/solution.py
+++ b/solution.py
@@ -31,10 +31,10 @@
     return pltpu.CompilerParams(vmem_limit_bytes=mebibytes << 20)
 
 
-def exchange_stages(bits):
+def exchange_stages(bits, square):
     if bits < 3:
         return [[1 << bit] for bit in range(bits)]
-    return [[1], [4, 3]] + [[(1 << bit) | 1] for bit in range(3, bits)]
+    return [[1], square] + [[(1 << bit) | 1] for bit in range(3, bits)]
 
 
 def offsets(group):
@@ -336,7 +336,7 @@
     kv_heads = image_cache.shape[2] // (2 * head_size)
     group = heads // kv_heads
     tile_rows = steps * heads
-    stages = exchange_stages(devices.bit_length() - 1)
+    stages = exchange_stages(devices.bit_length() - 1, [4, 2])
     order = positions(stages)
     half = devices // 2
     chunks = 4
@@ -381,6 +381,8 @@
         ],
         compiler_params=params(6),
     )(total, query_gain, *cache, image_first_slot, tile_count, cross_tile_mask)
+    stages = exchange_stages(devices.bit_length() - 1, [4, 3])
+    order = positions(stages)
     gathered = tile[None]
     for group_bits in reversed(stages):
         gathered = jnp.concatenate(

time: 41.7 us -> 41.2 us (0.988)
  starting transfers between devices: 11.9 us -> 9.62 us
  waiting for transfers between devices: 15.4 us -> 17.1 us
    ppermute x10, starting transfers between devices: 11.9 us -> 9.62 us  [exchange(): lax.ppermute(array, AXIS, [(i, i ^ difference) for i in range(count)])]
    ppermute x10, waiting for transfers between devices: 15.4 us -> 17.1 us  [exchange(): lax.ppermute(array, AXIS, [(i, i ^ difference) for i in range(count)])]
where the time goes in v7:
time: 41.2 us; the launch traced here: 41.1 us
  waiting for transfers between devices  17.1 us (42%)
  Pallas kernels  13.1 us (32%)
  starting transfers between devices  9.62 us (23%)
  between operations  0.87 us (2%)
    ppermute x10, waiting for transfers between devices, exchange(): lax.ppermute(array, AXIS, [(i, i ^ difference) for i in range(count)])  17.1 us
    ppermute x10, starting transfers between devices, exchange(): lax.ppermute(array, AXIS, [(i, i ^ difference) for i in range(count)])  9.62 us
    pallas_call x2, Pallas kernels, fetch(): pl.pallas_call(functools.partial(fetch_kernel, part), out_shape=[struct((...  4.68 us
    pallas_call x1, Pallas kernels, body(): pl.pallas_call(functools.partial(project_kernel, order, chunks, kv_heads,...  4.09 us
    pallas_call x1, Pallas kernels, body(): pl.pallas_call(functools.partial(finish_kernel, order, kv_heads, group, s...  2.5 us
    pallas_call x1, Pallas kernels, body(): pl.pallas_call(functools.partial(attend_kernel, kv_heads, group, steps),...  1.78 us
  transfers between devices with their start and end apart: 10, of which 7 were waited for; matrix products, arithmetic and copies ran while one was open for 0% of the time, Pallas kernels for 11%

profile of v7, /device:TPU:0, one launch (start us, length us, event | category | flops | bytes accessed | tf_op | source)
XLA Modules:
  0.0 41.1 jit_solution(12778740825330958129)
XLA Ops:
  0.0 4.1 %shard_map.91 = (f32[1024,128]{1,0:T(8,128)S(1)}, f32[1024,128]{1,0:T(8,128)S(1)}) custom-call(bf16[8,2,512]{2,1,0:T(2,128)(2,1)} %x_hbm.1, bf16[512,8192]{1,0:T(8,128)(2,1)} %weight_hbm.1, s32[8]{0:T(128)} %first_ref.1, s32[8]{0:T(128)} %count_ref.1), custom_call_target="tpu_custom_call" | custom-call | tf_op jit(solution)/shard_map/pallas_call | solution.py:343
  4.1 0.0 copy-start.3
  4.1 0.5 %collective-permute-start = (f32[1024,128]{1,0:T(8,128)S(1)}, f32[1024,128]{1,0:T(8,128)S(1)}, u32[]{:S(2)}, u32[]{:S(2)}) collective-permute-start(f32[1024,128]{1,0:T(8,128)S(1)} %get-tuple-element.13), channel_id=1, source_target_pairs={{0,1},{1,0},{2,3},{3,2},{4,5},{5,4},{6,7},{7,6},{8,9},{9,8},{10,11... | collective-permute-start | bytes 1572872 | tf_op jit(solution)/shard_map/ppermute | solution.py:62
  4.6 1.5 %collective-permute-done = f32[1024,128]{1,0:T(8,128)S(1)} collective-permute-done((f32[1024,128]{1,0:T(8,128)S(1)}, f32[1024,128]{1,0:T(8,128)S(1)}, u32[]{:S(2)}, u32[]{:S(2)}) %collective-permute-start) | collective-permute-done | bytes 524320 | tf_op jit(solution)/shard_map/ppermute | solution.py:62
  6.2 0.1 add.15
  6.3 3.0 %collective-permute-start.1 = (f32[256,128]{1,0:T(8,128)S(1)}, f32[256,128]{1,0:T(8,128)S(1)}, u32[]{:S(2)}, u32[]{:S(2)}) collective-permute-start(f32[256,128]{1,0:T(8,128)S(1)} %get-tuple-element.19), channel_id=1, source_target_pairs={{0,4},{1,5},{2,6},{3,7},{4,0},{5,1},{6,2},{7,3},{8,12},{9,13},{10,... | collective-permute-start | bytes 393224 | tf_op jit(solution)/shard_map/ppermute | solution.py:62
  9.3 1.5 %collective-permute-start.2 = (f32[256,128]{1,0:T(8,128)S(1)}, f32[256,128]{1,0:T(8,128)S(1)}, u32[]{:S(2)}, u32[]{:S(2)}) collective-permute-start(f32[256,128]{1,0:T(8,128)S(1)} %get-tuple-element.21), channel_id=1, source_target_pairs={{0,2},{1,3},{2,0},{3,1},{4,6},{5,7},{6,4},{7,5},{8,10},{9,11},{10,... | collective-permute-start | bytes 393224 | tf_op jit(solution)/shard_map/ppermute | solution.py:62
  10.8 0.0 collective-permute-start.3
  11.5 0.0 copy-start
  11.5 0.0 copy-start.1
  11.5 0.0 copy-start.2
  11.5 2.6 %shard_map.92 = (bf16[1,1601,1024]{2,1,0:T(8,128)(2,1)S(1)}, f32[256,128]{1,0:T(8,128)S(1)}, f32[8,128]{1,0:T(8,128)}) custom-call(bf16[1,1601,2048]{2,1,0:T(8,128)(2,1)} %cache_hbm.3, f32[256,128]{1,0:T(8,128)S(1)} %get-tuple-element.22.before_ref, f32[1]{0:T(128)S(6)} %copy.24.gate_ref), custom_call_target="tpu_custom_call", output_to_operand_aliasing={{1}: (1, {})} | custom-call | bytes 3278848 | tf_op jit(solution)/shard_map/pallas_call | solution.py:146
  14.1 0.0 collective-permute-done.1
  14.1 3.3 %collective-permute-done.2 = f32[256,128]{1,0:T(8,128)S(1)} collective-permute-done((f32[256,128]{1,0:T(8,128)S(1)}, f32[256,128]{1,0:T(8,128)S(1)}, u32[]{:S(2)}, u32[]{:S(2)}) %collective-permute-start.2) | collective-permute-done | bytes 131104 | tf_op jit(solution)/shard_map/ppermute | solution.py:62
  17.3 0.0 collective-permute-done.3
  17.4 0.9 %collective-permute-start.4 = (f32[128,128]{1,0:T(8,128)S(1)}, f32[128,128]{1,0:T(8,128)S(1)}, u32[]{:S(2)}, u32[]{:S(2)}) collective-permute-start(f32[128,128]{1,0:T(8,128)S(1)} %get-tuple-element.23), channel_id=1, source_target_pairs={{0,9},{1,8},{2,11},{3,10},{4,13},{5,12},{6,15},{7,14},{8,1},{9,0},... | collective-permute-start | bytes 196616 | tf_op jit(solution)/shard_map/ppermute | solution.py:62
  18.3 0.1 copy.12.mask_in
  18.4 2.1 %shard_map.93 = (bf16[1,1601,1024]{2,1,0:T(8,128)(2,1)S(1)}, f32[128,128]{1,0:T(8,128)S(1)}, f32[8,128]{1,0:T(8,128)S(1)}) custom-call(bf16[1,1601,2048]{2,1,0:T(8,128)(2,1)} %cache_hbm.3, f32[128,128]{1,0:T(8,128)S(1)} %get-tuple-element.24.before_ref, f32[1]{0:T(128)S(6)} %copy.24.gate_ref), custom_call_target="tpu_custom_call", output_to_operand_aliasing={{1}: (1, {})} | custom-call | bytes 3278848 | tf_op jit(solution)/shard_map/pallas_call | solution.py:146
  20.5 3.4 %collective-permute-done.4 = f32[128,128]{1,0:T(8,128)S(1)} collective-permute-done((f32[128,128]{1,0:T(8,128)S(1)}, f32[128,128]{1,0:T(8,128)S(1)}, u32[]{:S(2)}, u32[]{:S(2)}) %collective-permute-start.4) | collective-permute-done | bytes 65568 | tf_op jit(solution)/shard_map/ppermute | solution.py:62
  24.0 0.0 slice-start.1
  24.0 1.8 %shard_map.94 = bf16[144,128]{1,0:T(8,128)(2,1)S(1)} custom-call(f32[128,128]{1,0:T(8,128)S(1)} %add.19.query_ref, f32[128]{0:T(128)S(1)} %copy-done.2, bf16[1,1601,1024]{2,1,0:T(8,128)(2,1)S(1)} %get-tuple-element.17.keys_ref, bf16[1,1601,1024]{2,1,0:T(8,128)(2,1)S(1)} %get-tuple-element.18.values_ref, s32[8]{0:T(128)S(1)} %copy-done, s32[8]{0:T(128)S(1)} %copy-done.1, ...), custom_call_target="tpu_custom_call" | custom-call | tf_op jit(solution)/shard_map/pallas_call | solution.py:371
  25.8 0.1 collective-permute-start.5
  25.9 4.8 %collective-permute-done.5 = bf16[1,144,128]{2,1,0:T(8,128)(2,1)S(1)} collective-permute-done((bf16[1,144,128]{2,1,0:T(8,128)(2,1)S(1)}, bf16[1,144,128]{2,1,0:T(8,128)(2,1)S(1)}, u32[]{:S(2)}, u32[]{:S(2)}) %collective-permute-start.5) | collective-permute-done | bytes 36896 | tf_op jit(solution)/shard_map/ppermute | solution.py:62
  30.6 0.1 collective-permute-start.6
  30.7 1.0 %collective-permute-start.7 = (bf16[2,144,128]{2,1,0:T(8,128)(2,1)S(1)}, bf16[2,144,128]{2,1,0:T(8,128)(2,1)S(1)}, u32[]{:S(2)}, u32[]{:S(2)}) collective-permute-start(bf16[2,144,128]{2,1,0:T(8,128)(2,1)S(1)} %pad_maximum_fusion), channel_id=1, source_target_pairs={{0,3},{1,2},{2,1},{3,0},{4,7},{5,6},{6,5},{7,4},{8,11},{9,10},{10,... | collective-permute-start | bytes 221192 | tf_op jit(solution)/shard_map/ppermute | solution.py:62
  31.7 2.2 %collective-permute-start.8 = (bf16[2,144,128]{2,1,0:T(8,128)(2,1)S(1)}, bf16[2,144,128]{2,1,0:T(8,128)(2,1)S(1)}, u32[]{:S(2)}, u32[]{:S(2)}) collective-permute-start(bf16[2,144,128]{2,1,0:T(8,128)(2,1)S(1)} %pad_maximum_fusion), channel_id=1, source_target_pairs={{0,7},{1,6},{2,5},{3,4},{4,3},{5,2},{6,1},{7,0},{8,15},{9,14},{10,... | collective-permute-start | bytes 221192 | tf_op jit(solution)/shard_map/ppermute | solution.py:62
  33.9 1.3 %collective-permute-done.6 = bf16[2,144,128]{2,1,0:T(8,128)(2,1)S(1)} collective-permute-done((bf16[2,144,128]{2,1,0:T(8,128)(2,1)S(1)}, bf16[2,144,128]{2,1,0:T(8,128)(2,1)S(1)}, u32[]{:S(2)}, u32[]{:S(2)}) %collective-permute-start.6) | collective-permute-done | bytes 73760 | tf_op jit(solution)/shard_map/ppermute | solution.py:62
  35.2 0.0 collective-permute-done.7
  35.3 1.6 %collective-permute-done.8 = bf16[2,144,128]{2,1,0:T(8,128)(2,1)S(1)} collective-permute-done((bf16[2,144,128]{2,1,0:T(8,128)(2,1)S(1)}, bf16[2,144,128]{2,1,0:T(8,128)(2,1)S(1)}, u32[]{:S(2)}, u32[]{:S(2)}) %collective-permute-start.8) | collective-permute-done | bytes 73760 | tf_op jit(solution)/shard_map/ppermute | solution.py:62
  36.9 0.3 collective-permute-start.9
  37.2 1.4 %collective-permute-done.9 = bf16[8,144,128]{2,1,0:T(8,128)(2,1)S(1)} collective-permute-done((bf16[8,144,128]{2,1,0:T(8,128)(2,1)S(1)}, bf16[8,144,128]{2,1,0:T(8,128)(2,1)S(1)}, u32[]{:S(2)}, u32[]{:S(2)}) %collective-permute-start.9) | collective-permute-done | bytes 294944 | tf_op jit(solution)/shard_map/ppermute | solution.py:62
  38.6 2.5 %shard_map.95 = bf16[8,2,512]{2,1,0:T(2,128)(2,1)} custom-call(f32[8,128]{1,0:T(8,128)S(1)} %get-tuple-element.15.gate_ref, s32[8]{0:T(128)S(1)} %copy-done, s32[8]{0:T(128)S(1)} %copy-done.1, bf16[16,144,128]{2,1,0:T(8,128)(2,1)S(1)} %constant_dynamic-update-slice_fusion.5.tiles_ref, bf16[8192,512]{1,0:T(8,128)(2,1)S(1)} %bitcast.4), custom_call_target="tpu_custom_call" | custom-call | tf_op jit(solution)/shard_map/pallas_call | solution.py:392
  (19 shorter events, 0.3 us)
Async XLA Ops:
  4.1 14.2 %copy-start.3 = (s32[8,2,4]{0,2,1:T(4,128)S(1)}, s32[8,2,4]{0,2,1:T(4,128)}, u32[]{:S(2)}) copy-start(s32[8,2,4]{0,2,1:T(4,128)} %param.15) | copy-start | bytes 772
  4.1 2.1 %collective-permute-start = (f32[1024,128]{1,0:T(8,128)S(1)}, f32[1024,128]{1,0:T(8,128)S(1)}, u32[]{:S(2)}, u32[]{:S(2)}) collective-permute-start(f32[1024,128]{1,0:T(8,128)S(1)} %get-tuple-element.13), channel_id=1, source_target_pairs={{0,1},{1,0},{2,3},{3,2},{4,5},{5,4},{6,7},{7,6},{8,9},{9,8},{10,11... | collective-permute-start | bytes 1572872 | tf_op jit(solution)/shard_map/ppermute | solution.py:62
  6.3 7.8 %collective-permute-start.1 = (f32[256,128]{1,0:T(8,128)S(1)}, f32[256,128]{1,0:T(8,128)S(1)}, u32[]{:S(2)}, u32[]{:S(2)}) collective-permute-start(f32[256,128]{1,0:T(8,128)S(1)} %get-tuple-element.19), channel_id=1, source_target_pairs={{0,4},{1,5},{2,6},{3,7},{4,0},{5,1},{6,2},{7,3},{8,12},{9,13},{10,... | collective-permute-start | bytes 393224 | tf_op jit(solution)/shard_map/ppermute | solution.py:62
  9.3 8.1 %collective-permute-start.2 = (f32[256,128]{1,0:T(8,128)S(1)}, f32[256,128]{1,0:T(8,128)S(1)}, u32[]{:S(2)}, u32[]{:S(2)}) collective-permute-start(f32[256,128]{1,0:T(8,128)S(1)} %get-tuple-element.21), channel_id=1, source_target_pairs={{0,2},{1,3},{2,0},{3,1},{4,6},{5,7},{6,4},{7,5},{8,10},{9,11},{10,... | collective-permute-start | bytes 393224 | tf_op jit(solution)/shard_map/ppermute | solution.py:62
  10.8 6.6 %collective-permute-start.3 = (f32[256,128]{1,0:T(8,128)S(1)}, f32[256,128]{1,0:T(8,128)S(1)}, u32[]{:S(2)}, u32[]{:S(2)}) collective-permute-start(f32[256,128]{1,0:T(8,128)S(1)} %get-tuple-element.20), channel_id=1, source_target_pairs={{0,6},{1,7},{2,4},{3,5},{4,2},{5,3},{6,0},{7,1},{8,14},{9,15},{10,... | collective-permute-start | bytes 393224 | tf_op jit(solution)/shard_map/ppermute | solution.py:62
  11.5 12.5 %copy-start = (s32[8]{0:T(128)S(1)}, s32[8]{0:T(128)}, u32[]{:S(2)}) copy-start(s32[8]{0:T(128)} %first_ref.1) | copy-start | bytes 100
  11.5 12.5 %copy-start.1 = (s32[8]{0:T(128)S(1)}, s32[8]{0:T(128)}, u32[]{:S(2)}) copy-start(s32[8]{0:T(128)} %count_ref.1) | copy-start | bytes 100
  11.5 12.5 %copy-start.2 = (f32[128]{0:T(128)S(1)}, f32[128]{0:T(128)}, u32[]{:S(2)}) copy-start(f32[128]{0:T(128)} %gain_ref.1) | copy-start | bytes 1540
  17.4 6.5 %collective-permute-start.4 = (f32[128,128]{1,0:T(8,128)S(1)}, f32[128,128]{1,0:T(8,128)S(1)}, u32[]{:S(2)}, u32[]{:S(2)}) collective-permute-start(f32[128,128]{1,0:T(8,128)S(1)} %get-tuple-element.23), channel_id=1, source_target_pairs={{0,9},{1,8},{2,11},{3,10},{4,13},{5,12},{6,15},{7,14},{8,1},{9,0},... | collective-permute-start | bytes 196616 | tf_op jit(solution)/shard_map/ppermute | solution.py:62
  18.4 20.2 %slice-start = ((s8[8388608]{0:T(1024)(128)(4,1)}), s8[4194304]{0:T(1024)(128)(4,1)S(1)}, s32[]{:S(2)}) async-start(s8[8388608]{0:T(1024)(128)(4,1)} %bitcast.3), calls=%async_computation | async-start | bytes 8388608
  24.0 14.6 %slice-start.1 = ((s8[8388608]{0:T(1024)(128)(4,1)}), s8[4194304]{0:T(1024)(128)(4,1)S(1)}, s32[]{:S(2)}) async-start(s8[8388608]{0:T(1024)(128)(4,1)} %bitcast.3), calls=%async_computation.1 | async-start | bytes 8388608
  25.8 4.9 %collective-permute-start.5 = (bf16[1,144,128]{2,1,0:T(8,128)(2,1)S(1)}, bf16[1,144,128]{2,1,0:T(8,128)(2,1)S(1)}, u32[]{:S(2)}, u32[]{:S(2)}) collective-permute-start(bf16[1,144,128]{2,1,0:T(8,128)(2,1)S(1)} %bitcast.5), channel_id=1, source_target_pairs={{0,9},{1,8},{2,11},{3,10},{4,13},{5,12},{6,15},{7,14},{8,1},{9,0},... | collective-permute-start | bytes 110600 | tf_op jit(solution)/shard_map/ppermute | solution.py:62
  30.6 4.6 %collective-permute-start.6 = (bf16[2,144,128]{2,1,0:T(8,128)(2,1)S(1)}, bf16[2,144,128]{2,1,0:T(8,128)(2,1)S(1)}, u32[]{:S(2)}, u32[]{:S(2)}) collective-permute-start(bf16[2,144,128]{2,1,0:T(8,128)(2,1)S(1)} %pad_maximum_fusion), channel_id=1, source_target_pairs={{0,4},{1,5},{2,6},{3,7},{4,0},{5,1},{6,2},{7,3},{8,12},{9,13},{10,... | collective-permute-start | bytes 221192 | tf_op jit(solution)/shard_map/ppermute | solution.py:62
  30.7 4.5 %collective-permute-start.7 = (bf16[2,144,128]{2,1,0:T(8,128)(2,1)S(1)}, bf16[2,144,128]{2,1,0:T(8,128)(2,1)S(1)}, u32[]{:S(2)}, u32[]{:S(2)}) collective-permute-start(bf16[2,144,128]{2,1,0:T(8,128)(2,1)S(1)} %pad_maximum_fusion), channel_id=1, source_target_pairs={{0,3},{1,2},{2,1},{3,0},{4,7},{5,6},{6,5},{7,4},{8,11},{9,10},{10,... | collective-permute-start | bytes 221192 | tf_op jit(solution)/shard_map/ppermute | solution.py:62
  31.7 5.2 %collective-permute-start.8 = (bf16[2,144,128]{2,1,0:T(8,128)(2,1)S(1)}, bf16[2,144,128]{2,1,0:T(8,128)(2,1)S(1)}, u32[]{:S(2)}, u32[]{:S(2)}) collective-permute-start(bf16[2,144,128]{2,1,0:T(8,128)(2,1)S(1)} %pad_maximum_fusion), channel_id=1, source_target_pairs={{0,7},{1,6},{2,5},{3,4},{4,3},{5,2},{6,1},{7,0},{8,15},{9,14},{10,... | collective-permute-start | bytes 221192 | tf_op jit(solution)/shard_map/ppermute | solution.py:62
  36.9 1.6 %collective-permute-start.9 = (bf16[8,144,128]{2,1,0:T(8,128)(2,1)S(1)}, bf16[8,144,128]{2,1,0:T(8,128)(2,1)S(1)}, u32[]{:S(2)}, u32[]{:S(2)}) collective-permute-start(bf16[8,144,128]{2,1,0:T(8,128)(2,1)S(1)} %get-tuple-element.25), channel_id=1, source_target_pairs={{0,1},{1,0},{2,3},{3,2},{4,5},{5,4},{6,7},{7,6},{8,9},{9,8},{10,11... | collective-permute-start | bytes 884744 | tf_op jit(solution)/shard_map/ppermute | solution.py:62

commit v8 on v7

--- a/solution.py
+++ b/solution.py
@@ -202,10 +202,14 @@
             axis=0,
         )
         scores.append(
-            lax.dot_general(left, keys, (((1,), (1,)), ((), ())), preferred_element_type=F32) * scale
+            lax.dot_general(left, keys, (((1,), (1,)), ((), ())), preferred_element_type=F32)
         )
     tops = [jnp.max(score, axis=1, keepdims=True) for score in scores]
-    weights = [jnp.exp(score - top).astype(BF16) for score, top in zip(scores, tops)]
+    weights = [
+        jnp.exp2((score - top) * (scale * math.log2(math.e))).astype(BF16)
+        for score, top in zip(scores, tops)
+    ]
+    tops = [top * scale for top in tops]
     totals = [jnp.sum(weight.astype(F32), axis=1, keepdims=True) for weight in weights]
     for base, top, weight, total in zip(bases, tops, weights, totals):
         values = values_ref[0, :, base * head_size : (base + join) * head_size]

time: 41.2 us -> 41.2 us (level)
  no operation moved by 1% of the time
where the time goes in v8:
time: 41.2 us; the launch traced here: 41.1 us
  waiting for transfers between devices  17.1 us (42%)
  Pallas kernels  13 us (32%)
  starting transfers between devices  9.62 us (23%)
  between operations  0.87 us (2%)
    ppermute x10, waiting for transfers between devices, exchange(): lax.ppermute(array, AXIS, [(i, i ^ difference) for i in range(count)])  17.1 us
    ppermute x10, starting transfers between devices, exchange(): lax.ppermute(array, AXIS, [(i, i ^ difference) for i in range(count)])  9.62 us
    pallas_call x2, Pallas kernels, fetch(): pl.pallas_call(functools.partial(fetch_kernel, part), out_shape=[struct((...  4.68 us
    pallas_call x1, Pallas kernels, body(): pl.pallas_call(functools.partial(project_kernel, order, chunks, kv_heads,...  4.09 us
    pallas_call x1, Pallas kernels, body(): pl.pallas_call(functools.partial(finish_kernel, order, kv_heads, group, s...  2.51 us
    pallas_call x1, Pallas kernels, body(): pl.pallas_call(functools.partial(attend_kernel, kv_heads, group, steps),...  1.75 us
  transfers between devices with their start and end apart: 10, of which 7 were waited for; matrix products, arithmetic and copies ran while one was open for 0% of the time, Pallas kernels for 11%

profile of v8, /device:TPU:0, one launch (start us, length us, event | category | flops | bytes accessed | tf_op | source)
XLA Modules:
  0.0 41.1 jit_solution(9236054157021915023)
XLA Ops:
  0.0 4.1 %shard_map.91 = (f32[1024,128]{1,0:T(8,128)S(1)}, f32[1024,128]{1,0:T(8,128)S(1)}) custom-call(bf16[8,2,512]{2,1,0:T(2,128)(2,1)} %x_hbm.1, bf16[512,8192]{1,0:T(8,128)(2,1)} %weight_hbm.1, s32[8]{0:T(128)} %first_ref.1, s32[8]{0:T(128)} %count_ref.1), custom_call_target="tpu_custom_call" | custom-call | tf_op jit(solution)/shard_map/pallas_call | solution.py:347
  4.1 0.0 copy-start.3
  4.1 0.5 %collective-permute-start = (f32[1024,128]{1,0:T(8,128)S(1)}, f32[1024,128]{1,0:T(8,128)S(1)}, u32[]{:S(2)}, u32[]{:S(2)}) collective-permute-start(f32[1024,128]{1,0:T(8,128)S(1)} %get-tuple-element.13), channel_id=1, source_target_pairs={{0,1},{1,0},{2,3},{3,2},{4,5},{5,4},{6,7},{7,6},{8,9},{9,8},{10,11... | collective-permute-start | bytes 1572872 | tf_op jit(solution)/shard_map/ppermute | solution.py:62
  4.6 1.5 %collective-permute-done = f32[1024,128]{1,0:T(8,128)S(1)} collective-permute-done((f32[1024,128]{1,0:T(8,128)S(1)}, f32[1024,128]{1,0:T(8,128)S(1)}, u32[]{:S(2)}, u32[]{:S(2)}) %collective-permute-start) | collective-permute-done | bytes 524320 | tf_op jit(solution)/shard_map/ppermute | solution.py:62
  6.2 0.1 add.15
  6.3 3.0 %collective-permute-start.1 = (f32[256,128]{1,0:T(8,128)S(1)}, f32[256,128]{1,0:T(8,128)S(1)}, u32[]{:S(2)}, u32[]{:S(2)}) collective-permute-start(f32[256,128]{1,0:T(8,128)S(1)} %get-tuple-element.19), channel_id=1, source_target_pairs={{0,4},{1,5},{2,6},{3,7},{4,0},{5,1},{6,2},{7,3},{8,12},{9,13},{10,... | collective-permute-start | bytes 393224 | tf_op jit(solution)/shard_map/ppermute | solution.py:62
  9.3 1.5 %collective-permute-start.2 = (f32[256,128]{1,0:T(8,128)S(1)}, f32[256,128]{1,0:T(8,128)S(1)}, u32[]{:S(2)}, u32[]{:S(2)}) collective-permute-start(f32[256,128]{1,0:T(8,128)S(1)} %get-tuple-element.21), channel_id=1, source_target_pairs={{0,2},{1,3},{2,0},{3,1},{4,6},{5,7},{6,4},{7,5},{8,10},{9,11},{10,... | collective-permute-start | bytes 393224 | tf_op jit(solution)/shard_map/ppermute | solution.py:62
  10.8 0.0 collective-permute-start.3
  11.5 0.0 copy-start
  11.5 0.0 copy-start.1
  11.5 0.0 copy-start.2
  11.5 2.6 %shard_map.92 = (bf16[1,1601,1024]{2,1,0:T(8,128)(2,1)S(1)}, f32[256,128]{1,0:T(8,128)S(1)}, f32[8,128]{1,0:T(8,128)}) custom-call(bf16[1,1601,2048]{2,1,0:T(8,128)(2,1)} %cache_hbm.3, f32[256,128]{1,0:T(8,128)S(1)} %get-tuple-element.22.before_ref, f32[1]{0:T(128)S(6)} %copy.24.gate_ref), custom_call_target="tpu_custom_call", output_to_operand_aliasing={{1}: (1, {})} | custom-call | bytes 3278848 | tf_op jit(solution)/shard_map/pallas_call | solution.py:146
  14.1 0.0 collective-permute-done.1
  14.1 3.3 %collective-permute-done.2 = f32[256,128]{1,0:T(8,128)S(1)} collective-permute-done((f32[256,128]{1,0:T(8,128)S(1)}, f32[256,128]{1,0:T(8,128)S(1)}, u32[]{:S(2)}, u32[]{:S(2)}) %collective-permute-start.2) | collective-permute-done | bytes 131104 | tf_op jit(solution)/shard_map/ppermute | solution.py:62
  17.3 0.0 collective-permute-done.3
  17.4 0.9 %collective-permute-start.4 = (f32[128,128]{1,0:T(8,128)S(1)}, f32[128,128]{1,0:T(8,128)S(1)}, u32[]{:S(2)}, u32[]{:S(2)}) collective-permute-start(f32[128,128]{1,0:T(8,128)S(1)} %get-tuple-element.23), channel_id=1, source_target_pairs={{0,9},{1,8},{2,11},{3,10},{4,13},{5,12},{6,15},{7,14},{8,1},{9,0},... | collective-permute-start | bytes 196616 | tf_op jit(solution)/shard_map/ppermute | solution.py:62
  18.3 0.1 copy.12.mask_in
  18.4 2.1 %shard_map.93 = (bf16[1,1601,1024]{2,1,0:T(8,128)(2,1)S(1)}, f32[128,128]{1,0:T(8,128)S(1)}, f32[8,128]{1,0:T(8,128)S(1)}) custom-call(bf16[1,1601,2048]{2,1,0:T(8,128)(2,1)} %cache_hbm.3, f32[128,128]{1,0:T(8,128)S(1)} %get-tuple-element.24.before_ref, f32[1]{0:T(128)S(6)} %copy.24.gate_ref), custom_call_target="tpu_custom_call", output_to_operand_aliasing={{1}: (1, {})} | custom-call | bytes 3278848 | tf_op jit(solution)/shard_map/pallas_call | solution.py:146
  20.5 3.4 %collective-permute-done.4 = f32[128,128]{1,0:T(8,128)S(1)} collective-permute-done((f32[128,128]{1,0:T(8,128)S(1)}, f32[128,128]{1,0:T(8,128)S(1)}, u32[]{:S(2)}, u32[]{:S(2)}) %collective-permute-start.4) | collective-permute-done | bytes 65568 | tf_op jit(solution)/shard_map/ppermute | solution.py:62
  24.0 0.0 slice-start.1
  24.0 1.7 %shard_map.94 = bf16[144,128]{1,0:T(8,128)(2,1)S(1)} custom-call(f32[128,128]{1,0:T(8,128)S(1)} %add.19.query_ref, f32[128]{0:T(128)S(1)} %copy-done.2, bf16[1,1601,1024]{2,1,0:T(8,128)(2,1)S(1)} %get-tuple-element.17.keys_ref, bf16[1,1601,1024]{2,1,0:T(8,128)(2,1)S(1)} %get-tuple-element.18.values_ref, s32[8]{0:T(128)S(1)} %copy-done, s32[8]{0:T(128)S(1)} %copy-done.1, ...), custom_call_target="tpu_custom_call" | custom-call | tf_op jit(solution)/shard_map/pallas_call | solution.py:375
  25.7 0.1 collective-permute-start.5
  25.8 4.8 %collective-permute-done.5 = bf16[1,144,128]{2,1,0:T(8,128)(2,1)S(1)} collective-permute-done((bf16[1,144,128]{2,1,0:T(8,128)(2,1)S(1)}, bf16[1,144,128]{2,1,0:T(8,128)(2,1)S(1)}, u32[]{:S(2)}, u32[]{:S(2)}) %collective-permute-start.5) | collective-permute-done | bytes 36896 | tf_op jit(solution)/shard_map/ppermute | solution.py:62
  30.6 0.1 collective-permute-start.6
  30.7 1.0 %collective-permute-start.7 = (bf16[2,144,128]{2,1,0:T(8,128)(2,1)S(1)}, bf16[2,144,128]{2,1,0:T(8,128)(2,1)S(1)}, u32[]{:S(2)}, u32[]{:S(2)}) collective-permute-start(bf16[2,144,128]{2,1,0:T(8,128)(2,1)S(1)} %pad_maximum_fusion), channel_id=1, source_target_pairs={{0,3},{1,2},{2,1},{3,0},{4,7},{5,6},{6,5},{7,4},{8,11},{9,10},{10,... | collective-permute-start | bytes 221192 | tf_op jit(solution)/shard_map/ppermute | solution.py:62
  31.6 2.2 %collective-permute-start.8 = (bf16[2,144,128]{2,1,0:T(8,128)(2,1)S(1)}, bf16[2,144,128]{2,1,0:T(8,128)(2,1)S(1)}, u32[]{:S(2)}, u32[]{:S(2)}) collective-permute-start(bf16[2,144,128]{2,1,0:T(8,128)(2,1)S(1)} %pad_maximum_fusion), channel_id=1, source_target_pairs={{0,7},{1,6},{2,5},{3,4},{4,3},{5,2},{6,1},{7,0},{8,15},{9,14},{10,... | collective-permute-start | bytes 221192 | tf_op jit(solution)/shard_map/ppermute | solution.py:62
  33.9 1.3 %collective-permute-done.6 = bf16[2,144,128]{2,1,0:T(8,128)(2,1)S(1)} collective-permute-done((bf16[2,144,128]{2,1,0:T(8,128)(2,1)S(1)}, bf16[2,144,128]{2,1,0:T(8,128)(2,1)S(1)}, u32[]{:S(2)}, u32[]{:S(2)}) %collective-permute-start.6) | collective-permute-done | bytes 73760 | tf_op jit(solution)/shard_map/ppermute | solution.py:62
  35.2 0.0 collective-permute-done.7
  35.2 1.6 %collective-permute-done.8 = bf16[2,144,128]{2,1,0:T(8,128)(2,1)S(1)} collective-permute-done((bf16[2,144,128]{2,1,0:T(8,128)(2,1)S(1)}, bf16[2,144,128]{2,1,0:T(8,128)(2,1)S(1)}, u32[]{:S(2)}, u32[]{:S(2)}) %collective-permute-start.8) | collective-permute-done | bytes 73760 | tf_op jit(solution)/shard_map/ppermute | solution.py:62
  36.8 0.3 collective-permute-start.9
  37.1 1.4 %collective-permute-done.9 = bf16[8,144,128]{2,1,0:T(8,128)(2,1)S(1)} collective-permute-done((bf16[8,144,128]{2,1,0:T(8,128)(2,1)S(1)}, bf16[8,144,128]{2,1,0:T(8,128)(2,1)S(1)}, u32[]{:S(2)}, u32[]{:S(2)}) %collective-permute-start.9) | collective-permute-done | bytes 294944 | tf_op jit(solution)/shard_map/ppermute | solution.py:62
  38.5 2.5 %shard_map.95 = bf16[8,2,512]{2,1,0:T(2,128)(2,1)} custom-call(f32[8,128]{1,0:T(8,128)S(1)} %get-tuple-element.15.gate_ref, s32[8]{0:T(128)S(1)} %copy-done, s32[8]{0:T(128)S(1)} %copy-done.1, bf16[16,144,128]{2,1,0:T(8,128)(2,1)S(1)} %constant_dynamic-update-slice_fusion.5.tiles_ref, bf16[8192,512]{1,0:T(8,128)(2,1)S(1)} %bitcast.4), custom_call_target="tpu_custom_call" | custom-call | tf_op jit(solution)/shard_map/pallas_call | solution.py:396
  (19 shorter events, 0.3 us)
Async XLA Ops:
  4.1 14.2 %copy-start.3 = (s32[8,2,4]{0,2,1:T(4,128)S(1)}, s32[8,2,4]{0,2,1:T(4,128)}, u32[]{:S(2)}) copy-start(s32[8,2,4]{0,2,1:T(4,128)} %param.15) | copy-start | bytes 772
  4.1 2.1 %collective-permute-start = (f32[1024,128]{1,0:T(8,128)S(1)}, f32[1024,128]{1,0:T(8,128)S(1)}, u32[]{:S(2)}, u32[]{:S(2)}) collective-permute-start(f32[1024,128]{1,0:T(8,128)S(1)} %get-tuple-element.13), channel_id=1, source_target_pairs={{0,1},{1,0},{2,3},{3,2},{4,5},{5,4},{6,7},{7,6},{8,9},{9,8},{10,11... | collective-permute-start | bytes 1572872 | tf_op jit(solution)/shard_map/ppermute | solution.py:62
  6.3 7.8 %collective-permute-start.1 = (f32[256,128]{1,0:T(8,128)S(1)}, f32[256,128]{1,0:T(8,128)S(1)}, u32[]{:S(2)}, u32[]{:S(2)}) collective-permute-start(f32[256,128]{1,0:T(8,128)S(1)} %get-tuple-element.19), channel_id=1, source_target_pairs={{0,4},{1,5},{2,6},{3,7},{4,0},{5,1},{6,2},{7,3},{8,12},{9,13},{10,... | collective-permute-start | bytes 393224 | tf_op jit(solution)/shard_map/ppermute | solution.py:62
  9.3 8.1 %collective-permute-start.2 = (f32[256,128]{1,0:T(8,128)S(1)}, f32[256,128]{1,0:T(8,128)S(1)}, u32[]{:S(2)}, u32[]{:S(2)}) collective-permute-start(f32[256,128]{1,0:T(8,128)S(1)} %get-tuple-element.21), channel_id=1, source_target_pairs={{0,2},{1,3},{2,0},{3,1},{4,6},{5,7},{6,4},{7,5},{8,10},{9,11},{10,... | collective-permute-start | bytes 393224 | tf_op jit(solution)/shard_map/ppermute | solution.py:62
  10.8 6.6 %collective-permute-start.3 = (f32[256,128]{1,0:T(8,128)S(1)}, f32[256,128]{1,0:T(8,128)S(1)}, u32[]{:S(2)}, u32[]{:S(2)}) collective-permute-start(f32[256,128]{1,0:T(8,128)S(1)} %get-tuple-element.20), channel_id=1, source_target_pairs={{0,6},{1,7},{2,4},{3,5},{4,2},{5,3},{6,0},{7,1},{8,14},{9,15},{10,... | collective-permute-start | bytes 393224 | tf_op jit(solution)/shard_map/ppermute | solution.py:62
  11.5 12.5 %copy-start = (s32[8]{0:T(128)S(1)}, s32[8]{0:T(128)}, u32[]{:S(2)}) copy-start(s32[8]{0:T(128)} %first_ref.1) | copy-start | bytes 100
  11.5 12.5 %copy-start.1 = (s32[8]{0:T(128)S(1)}, s32[8]{0:T(128)}, u32[]{:S(2)}) copy-start(s32[8]{0:T(128)} %count_ref.1) | copy-start | bytes 100
  11.5 12.5 %copy-start.2 = (f32[128]{0:T(128)S(1)}, f32[128]{0:T(128)}, u32[]{:S(2)}) copy-start(f32[128]{0:T(128)} %gain_ref.1) | copy-start | bytes 1540
  17.4 6.5 %collective-permute-start.4 = (f32[128,128]{1,0:T(8,128)S(1)}, f32[128,128]{1,0:T(8,128)S(1)}, u32[]{:S(2)}, u32[]{:S(2)}) collective-permute-start(f32[128,128]{1,0:T(8,128)S(1)} %get-tuple-element.23), channel_id=1, source_target_pairs={{0,9},{1,8},{2,11},{3,10},{4,13},{5,12},{6,15},{7,14},{8,1},{9,0},... | collective-permute-start | bytes 196616 | tf_op jit(solution)/shard_map/ppermute | solution.py:62
  18.4 20.1 %slice-start = ((s8[8388608]{0:T(1024)(128)(4,1)}), s8[4194304]{0:T(1024)(128)(4,1)S(1)}, s32[]{:S(2)}) async-start(s8[8388608]{0:T(1024)(128)(4,1)} %bitcast.3), calls=%async_computation | async-start | bytes 8388608
  24.0 14.6 %slice-start.1 = ((s8[8388608]{0:T(1024)(128)(4,1)}), s8[4194304]{0:T(1024)(128)(4,1)S(1)}, s32[]{:S(2)}) async-start(s8[8388608]{0:T(1024)(128)(4,1)} %bitcast.3), calls=%async_computation.1 | async-start | bytes 8388608
  25.7 4.9 %collective-permute-start.5 = (bf16[1,144,128]{2,1,0:T(8,128)(2,1)S(1)}, bf16[1,144,128]{2,1,0:T(8,128)(2,1)S(1)}, u32[]{:S(2)}, u32[]{:S(2)}) collective-permute-start(bf16[1,144,128]{2,1,0:T(8,128)(2,1)S(1)} %bitcast.5), channel_id=1, source_target_pairs={{0,9},{1,8},{2,11},{3,10},{4,13},{5,12},{6,15},{7,14},{8,1},{9,0},... | collective-permute-start | bytes 110600 | tf_op jit(solution)/shard_map/ppermute | solution.py:62
  30.6 4.6 %collective-permute-start.6 = (bf16[2,144,128]{2,1,0:T(8,128)(2,1)S(1)}, bf16[2,144,128]{2,1,0:T(8,128)(2,1)S(1)}, u32[]{:S(2)}, u32[]{:S(2)}) collective-permute-start(bf16[2,144,128]{2,1,0:T(8,128)(2,1)S(1)} %pad_maximum_fusion), channel_id=1, source_target_pairs={{0,4},{1,5},{2,6},{3,7},{4,0},{5,1},{6,2},{7,3},{8,12},{9,13},{10,... | collective-permute-start | bytes 221192 | tf_op jit(solution)/shard_map/ppermute | solution.py:62
  30.7 4.5 %collective-permute-start.7 = (bf16[2,144,128]{2,1,0:T(8,128)(2,1)S(1)}, bf16[2,144,128]{2,1,0:T(8,128)(2,1)S(1)}, u32[]{:S(2)}, u32[]{:S(2)}) collective-permute-start(bf16[2,144,128]{2,1,0:T(8,128)(2,1)S(1)} %pad_maximum_fusion), channel_id=1, source_target_pairs={{0,3},{1,2},{2,1},{3,0},{4,7},{5,6},{6,5},{7,4},{8,11},{9,10},{10,... | collective-permute-start | bytes 221192 | tf_op jit(solution)/shard_map/ppermute | solution.py:62
  31.6 5.1 %collective-permute-start.8 = (bf16[2,144,128]{2,1,0:T(8,128)(2,1)S(1)}, bf16[2,144,128]{2,1,0:T(8,128)(2,1)S(1)}, u32[]{:S(2)}, u32[]{:S(2)}) collective-permute-start(bf16[2,144,128]{2,1,0:T(8,128)(2,1)S(1)} %pad_maximum_fusion), channel_id=1, source_target_pairs={{0,7},{1,6},{2,5},{3,4},{4,3},{5,2},{6,1},{7,0},{8,15},{9,14},{10,... | collective-permute-start | bytes 221192 | tf_op jit(solution)/shard_map/ppermute | solution.py:62
  36.8 1.6 %collective-permute-start.9 = (bf16[8,144,128]{2,1,0:T(8,128)(2,1)S(1)}, bf16[8,144,128]{2,1,0:T(8,128)(2,1)S(1)}, u32[]{:S(2)}, u32[]{:S(2)}) collective-permute-start(bf16[8,144,128]{2,1,0:T(8,128)(2,1)S(1)} %get-tuple-element.25), channel_id=1, source_target_pairs={{0,1},{1,0},{2,3},{3,2},{4,5},{5,4},{6,7},{7,6},{8,9},{9,8},{10,11... | collective-permute-start | bytes 884744 | tf_op jit(solution)/shard_map/ppermute | solution.py:62
